TPU v7x, 32 devices: a whole 2x2x4 slice. The times are simulated.
32 devices in a mesh: groups: 2 (over x), pb: 16 (over z, y, core).
Axes of the slice: x: 2, y: 2, z: 4, core: 2. Of those that a mesh axis runs over, the one named last changes fastest.
Arguments:
- tokens: bfloat16 [6144, 512], P(('groups', 'pb')), parts along dimension 0, may hold values from -6 to 6
- stamps: int32 [6144], P(('groups', 'pb')), parts along dimension 0, may hold values from 0 to 1086324736, as said below
- norm_gain: float32 [512], replicated, may hold values from 0.5 to 1.5
- w_proj: bfloat16 [512, 2048], replicated, may hold values from -0.25 to 0.25
- rel_bias: float32 [8, 16], replicated, may hold values from -1.5 to 1.5
- attn_gain: float32 [512], replicated, may hold values from 0.5 to 1.5
- w_out: bfloat16 [512, 512], replicated, may hold values from -0.25 to 0.25
Outputs:
- mixed: bfloat16 [6144, 512], P(('groups', 'pb')), parts along dimension 0
There are 2 independent parts, one for each index of `groups`. A program takes and returns all parts, laid end to end along the dimension named above; an argument that names none is the same for every part. Nothing has to cross between parts.
Inputs may be any that keep to these rules, and one draw needn't show every extreme that they name: `stamps`: stamps never fall from one row to the next.
All inputs are finite; a program needn't handle non-finite values.
Results may differ from a plain program's by a relative error of at most 0.008.
Values may be sent and summed in bfloat16 or wider, within the bound.
No kernel may reach another device: no remote copies, remote signals or barrier semaphores. Data moves between devices by JAX's collectives and lax.ppermute only.
A program may use at most 128 MiB of HBM per device.

v0:
```python
import jax
import jax.numpy as jnp
from jax import lax
from jax.sharding import PartitionSpec as P

HEADS = 8
BUCKETS = 16


epsilon = 1e-05


def layer_norm(values, gain):
    centered = values - jnp.mean(values, axis=-1, keepdims=True)
    spread = jnp.mean(centered * centered, axis=-1, keepdims=True)
    return centered * lax.rsqrt(spread + epsilon) * gain


def bucket_of(elapsed):
    bucket_ids = jnp.zeros(elapsed.shape, jnp.int32)
    for exponent in range(BUCKETS - 1):
        bucket_ids = bucket_ids + (elapsed >= 4**exponent).astype(jnp.int32)
    return bucket_ids


def relative_bias(bias_table, bucket):
    bias = jnp.zeros((bias_table.shape[0],) + bucket.shape, jnp.float32)
    for bucket_id in range(BUCKETS):
        bias = jnp.where((bucket == bucket_id)[None], bias_table[:, bucket_id][:, None, None], bias)
    return bias


def attend(queries, key_rows, value_rows, query_pos, key_pos, query_stamp, key_stamp, bias_table):
    query_count = queries.shape[0]
    key_count = key_rows.shape[0]
    head_size = queries.shape[1] // HEADS
    q_heads = queries.reshape(query_count, HEADS, head_size)
    k_heads = key_rows.reshape(key_count, HEADS, head_size)
    v_heads = value_rows.reshape(key_count, HEADS, head_size)
    scores = jnp.einsum(
        "qhd,khd->hqk", q_heads, k_heads, preferred_element_type=jnp.float32
    ) * head_size ** (-0.5)
    bucket = bucket_of(query_stamp[:, None] - key_stamp[None, :])
    scores = scores + relative_bias(bias_table, bucket)
    visible = key_pos[None, :] <= query_pos[:, None]
    weight = jnp.where(visible[None], jax.nn.silu(scores), 0.0).astype(jnp.bfloat16)
    mixture = jnp.einsum("hqk,khd->qhd", weight, v_heads, preferred_element_type=jnp.float32)
    return mixture.reshape(query_count, HEADS * head_size)


def body(tokens, stamps, norm_gain, w_proj, rel_bias, attn_gain, w_out):
    my_index = lax.axis_index("pb")
    row_count, tok_width = tokens.shape
    every_stamp = lax.all_gather(stamps, "pb", axis=0, tiled=True)
    row_index = jnp.arange(row_count, dtype=jnp.int32)
    own_pos = my_index * row_count + row_index
    own_stamp = jnp.take(every_stamp, own_pos)
    normed = layer_norm(tokens.astype(jnp.float32), norm_gain).astype(jnp.bfloat16)
    front_proj = jnp.dot(normed, w_proj[:, : 2 * tok_width], preferred_element_type=jnp.float32)
    gate_vals = jax.nn.silu(front_proj[:, :tok_width]).astype(jnp.bfloat16)
    queries = front_proj[:, tok_width:].astype(jnp.bfloat16)
    back_weight = w_proj[:, 2 * tok_width :]

    def visit_block(running, key_block, value_block, first_row):
        key_count = key_block.shape[0]
        key_pos = first_row + jnp.arange(key_count, dtype=jnp.int32)
        key_stamp = lax.dynamic_slice_in_dim(every_stamp, first_row, key_count, 0)
        return lax.cond(
            first_row <= my_index * row_count + row_count - 1,
            lambda: running
            + attend(
                queries, key_block, value_block, own_pos, key_pos, own_stamp, key_stamp, rel_bias
            ),
            lambda: running,
        )

    def from_inputs(partial_sum, blocks, first_row):
        both_proj = jnp.dot(blocks[0], back_weight, preferred_element_type=jnp.float32)
        key_block = both_proj[:, :tok_width].astype(jnp.bfloat16)
        value_block = both_proj[:, tok_width:].astype(jnp.bfloat16)
        return visit_block(partial_sum, key_block, value_block, first_row)

    empty_sum = jnp.zeros((row_count, tok_width), jnp.float32)
    piece = (lax.all_gather(normed, "pb", axis=0, tiled=True),)
    shard_count = piece[0].shape[0] // row_count
    group_size = 1
    for candidate in range(1, shard_count + 1):
        if shard_count % candidate == 0 and candidate * row_count <= 2048:
            group_size = candidate
    block_length = group_size * row_count

    def one_group(group_step, partial_sum):
        blocks = tuple(
            (
                lax.dynamic_slice_in_dim(member, group_step * block_length, block_length, 0)
                for member in piece
            )
        )
        return from_inputs(partial_sum, blocks, group_step * block_length)

    attended = lax.fori_loop(0, shard_count // group_size, one_group, empty_sum)
    gated = (layer_norm(attended, attn_gain) * gate_vals.astype(jnp.float32)).astype(jnp.bfloat16)
    result = (
        tokens.astype(jnp.float32) + jnp.dot(gated, w_out, preferred_element_type=jnp.float32)
    ).astype(jnp.bfloat16)
    return result


def solution(mesh):
    return jax.shard_map(
        body,
        mesh=mesh,
        in_specs=(P(("groups", "pb"), None), P(("groups", "pb")), P(), P(), P(), P(), P()),
        out_specs=P(("groups", "pb"), None),
        check_vma=False,
    )
```

profile of v0, /device:TPU:31, one launch (start us, length us, event | category | flops | bytes accessed | tf_op | source)
XLA Modules:
  0.0 168.2 jit_solution(9190498993229262674)
XLA Ops:
  6.5 0.0 copy-start
  6.5 0.0 copy-start.1
  6.5 0.0 all-gather.2.cloned.1.call-start
  6.5 1.2 convert_reduce_fusion
  7.7 1.1 fusion.13
  8.9 1.8 %fusion.15 = bf16[192,512]{1,0:T(8,128)(2,1)} fusion(bf16[192,512]{1,0:T(8,128)(2,1)} %param.11, f32[512]{0:T(512)} %param.13, f32[192]{0:T(256)S(1)} %add_rsqrt_fusion.1, f32[192]{0:T(256)S(1)} %broadcast_multiply_fusion.1), kind=kLoop, calls=%fused_computation.72 | loop fusion | flops 491520 | bytes 396800 | tf_op jit(solution)/shard_map/convert_element_type | solution.py:58
  10.6 0.0 copy-start.2
  10.7 0.0 all-gather.2.cloned.1.call-update
  10.7 0.8 copy.16
  11.5 0.0 copy-start.6
  11.5 0.0 copy-start.4
  11.5 2.3 %slice.81 = bf16[512,1024]{1,0:T(8,128)(2,1)} slice(bf16[512,2048]{1,0:T(8,128)(2,1)} %param.14), slice={[0:512], [1024:2048]} | slice | bytes 2097152 | tf_op jit(solution)/shard_map/slice | solution.py:62
  13.8 0.0 copy-done.1
  13.8 0.0 copy-done.2
  13.8 0.4 fusion.9
  14.2 0.0 copy-start.3
  14.2 0.9 copy-done.3
  15.1 0.8 copy.15
  15.9 0.0 copy-done.6
  15.9 0.6 dynamic-slice
  17.1 0.0 copy-done.4
  17.1 0.3 dynamic-update-slice
  17.4 57.3 %all-reduce = s32[3072]{0:T(1024)S(1)} all-reduce(s32[3072]{0:T(1024)S(1)} %dynamic-update-slice), channel_id=1, replica_groups=mesh['groups'=2,'pb'=16] {'pb'}, use_global_device_ids=true, to_apply=%add | all-reduce | flops 3072 | bytes 24576
  74.7 1.4 gather_fusion
  76.1 0.0 all-gather.2.cloned.1.call-done
  76.2 0.0 copy-start.5
  76.2 82.6 %while.19 = (s32[]{:T(128)}, f32[192,512]{0,1:T(8,128)S(1)}, s32[]{:T(128)}, bf16[3072,512]{1,0:T(8,128)(2,1)}, bf16[512,1024]{1,0:T(8,128)(2,1)}, /*index=5*/bf...) while((s32[]{:T(128)}, f32[192,512]{0,1:T(8,128)S(1)}, ...), condition=%wide.region_5.6_spmd.clone, body=%wide.region_2.0_spmd.clone.sunk | while | flops 2291173120 | bytes 41205836 | solution.py:101
  76.3 5.2 %convolution_convert_fusion.2 = bf16[1536,1024]{1,0:T(8,128)(2,1)} fusion(bf16[512,1024]{1,0:T(8,128)(2,1)} %get-tuple-element.503, bf16[3072,512]{1,0:T(8,128)(2,1)} %get-tuple-element.502, s32[]{:T(128)} %select_n.144), kind=kOutput, calls=%fused_computation.59.clone.1 | convolution fusion | flops 1612185600 | bytes 5767680 | tf_op jit(solution)/shard_map/while/body/eval_jaxpr/dot_general | solution.py:78
  81.4 36.1 %conditional.3 = (f32[192,512]{0,1:T(8,128)S(1)}) conditional(s32[]{:T(128)} %convert_element_type.1355, f32[192,512]{0,1:T(8,128)S(1)} %get-tuple-element.486, (s32[]{:T(128)}, s32[1536]{0:T(1024)S(1)}, s32[]{:T(128)}, bf16[192,512]{0,1:T(8,128)(2,1)}, bf16[1536,1024]{1,0:T(8,128)(2,1)}, /*index=5*/s32[192]{0:T(256)S(1)}, s32[3072]{0:T(1024)S(1)}, ...), branch_computations={%region_3.3_spmd, %region_4.4_spmd} | conditional | flops 678987456 | bytes 35430956 | solution.py:68
  81.4 0.1 dynamic_slice.16
  81.5 0.2 broadcast_compare_fusion.16
  81.8 4.7 %copy.14 = bf16[1536,1024]{0,1:T(8,128)(2,1)} copy(bf16[1536,1024]{1,0:T(8,128)(2,1)} %get-tuple-element.343) | data formatting | bytes 6291456 | tf_op jit(solution)/shard_map
  86.5 4.7 %copy.13 = bf16[1536,1024]{0,1:T(8,128)(2,1)} copy(bf16[1536,1024]{1,0:T(8,128)(2,1)} %get-tuple-element.343) | data formatting | bytes 6291456 | tf_op jit(solution)/shard_map
  91.1 2.7 %slice.89 = bf16[1536,512]{0,1:T(8,128)(2,1)} slice(bf16[1536,1024]{0,1:T(8,128)(2,1)} %copy.13), slice={[0:1536], [0:512]} | slice | bytes 3145728 | tf_op jit(solution)/shard_map/while/body/eval_jaxpr/slice | solution.py:79
  93.9 0.0 slice-start
  93.9 5.7 %broadcast_compare_fusion.13 = (pred[192,1536]{1,0:T(8,128)(4,1)}, pred[192,1536]{1,0:T(8,128)(4,1)}, pred[192,1536]{1,0:T(8,128)(4,1)}, pred[192,1536]{1,0:T(8,...) fusion(s32[1536]{0:T(1024)S(1)} %dynamic_slice.16, ...), kind=kLoop, calls=%fused_computation.33 | loop fusion | flops 17989632 | bytes 4725504 | tf_op jit(solution)/shard_map/while/body/eval_jaxpr/cond/branch_1_fun/eq | solution.py:29
  99.6 0.0 slice-done
  99.6 17.8 %fusion.2 = f32[8,192,64]{1,2,0:T(8,128)S(1)} fusion(bf16[1536,8,64]{0,2,1:T(8,128)(2,1)S(1)} %bitcast.49, bf16[192,8,64]{0,2,1:T(8,128)(2,1)} %bitcast, bf16[1536,8,64]{0,2,1:T(8,128)(2,1)} %bitcast.50, f32[8]{0:T(128)S(1)} %get-tuple-element.409, f32[8]{0:T(128)S(1)} %get-tuple-element.395, f32[8]{0:T(128)S(1)} %get-tuple-element.396, ...), kind=kOutput, calls=%fused_computation.18 | convolution fusion | flops 660602880 | bytes 8749568 | tf_op jit(solution)/shard_map/while/body/eval_jaxpr/cond/branch_1_fun/hqk,khd->qhd/dot_general | solution.py:47
  117.4 0.1 bitcast_add_fusion
  117.5 5.2 %convolution_convert_fusion.2 = bf16[1536,1024]{1,0:T(8,128)(2,1)} fusion(bf16[512,1024]{1,0:T(8,128)(2,1)} %get-tuple-element.503, bf16[3072,512]{1,0:T(8,128)(2,1)} %get-tuple-element.502, s32[]{:T(128)} %select_n.144), kind=kOutput, calls=%fused_computation.59.clone.1 | convolution fusion | flops 1612185600 | bytes 5767680 | tf_op jit(solution)/shard_map/while/body/eval_jaxpr/dot_general | solution.py:78
  122.7 36.1 %conditional.3 = (f32[192,512]{0,1:T(8,128)S(1)}) conditional(s32[]{:T(128)} %convert_element_type.1355, f32[192,512]{0,1:T(8,128)S(1)} %get-tuple-element.486, (s32[]{:T(128)}, s32[1536]{0:T(1024)S(1)}, s32[]{:T(128)}, bf16[192,512]{0,1:T(8,128)(2,1)}, bf16[1536,1024]{1,0:T(8,128)(2,1)}, /*index=5*/s32[192]{0:T(256)S(1)}, s32[3072]{0:T(1024)S(1)}, ...), branch_computations={%region_3.3_spmd, %region_4.4_spmd} | conditional | flops 678987456 | bytes 35430956 | solution.py:68
  122.7 0.1 dynamic_slice.16
  122.8 0.2 broadcast_compare_fusion.16
  123.0 4.7 %copy.14 = bf16[1536,1024]{0,1:T(8,128)(2,1)} copy(bf16[1536,1024]{1,0:T(8,128)(2,1)} %get-tuple-element.343) | data formatting | bytes 6291456 | tf_op jit(solution)/shard_map
  127.8 4.7 %copy.13 = bf16[1536,1024]{0,1:T(8,128)(2,1)} copy(bf16[1536,1024]{1,0:T(8,128)(2,1)} %get-tuple-element.343) | data formatting | bytes 6291456 | tf_op jit(solution)/shard_map
  132.4 2.7 %slice.89 = bf16[1536,512]{0,1:T(8,128)(2,1)} slice(bf16[1536,1024]{0,1:T(8,128)(2,1)} %copy.13), slice={[0:1536], [0:512]} | slice | bytes 3145728 | tf_op jit(solution)/shard_map/while/body/eval_jaxpr/slice | solution.py:79
  135.1 0.0 slice-start
  135.1 5.7 %broadcast_compare_fusion.13 = (pred[192,1536]{1,0:T(8,128)(4,1)}, pred[192,1536]{1,0:T(8,128)(4,1)}, pred[192,1536]{1,0:T(8,128)(4,1)}, pred[192,1536]{1,0:T(8,...) fusion(s32[1536]{0:T(1024)S(1)} %dynamic_slice.16, ...), kind=kLoop, calls=%fused_computation.33 | loop fusion | flops 17989632 | bytes 4725504 | tf_op jit(solution)/shard_map/while/body/eval_jaxpr/cond/branch_1_fun/eq | solution.py:29
  140.9 0.0 slice-done
  140.9 17.8 %fusion.2 = f32[8,192,64]{1,2,0:T(8,128)S(1)} fusion(bf16[1536,8,64]{0,2,1:T(8,128)(2,1)S(1)} %bitcast.49, bf16[192,8,64]{0,2,1:T(8,128)(2,1)} %bitcast, bf16[1536,8,64]{0,2,1:T(8,128)(2,1)} %bitcast.50, f32[8]{0:T(128)S(1)} %get-tuple-element.409, f32[8]{0:T(128)S(1)} %get-tuple-element.395, f32[8]{0:T(128)S(1)} %get-tuple-element.396, ...), kind=kOutput, calls=%fused_computation.18 | convolution fusion | flops 660602880 | bytes 8749568 | tf_op jit(solution)/shard_map/while/body/eval_jaxpr/cond/branch_1_fun/hqk,khd->qhd/dot_general | solution.py:47
  158.7 0.1 bitcast_add_fusion
  158.8 0.1 reduce_sum.38
  158.9 0.2 copy.17
  159.1 0.2 multiply_reduce_fusion
  159.3 0.0 copy-done
  159.3 0.0 copy-done.5
  159.3 2.1 %fusion.8 = bf16[192,512]{1,0:T(8,128)(2,1)} fusion(bf16[512,512]{1,0:T(8,128)(2,1)S(1)} %copy-done, bf16[192,512]{1,0:T(8,128)(2,1)} %param.11, f32[192,512]{1,0:T(8,128)S(1)} %copy.17, f32[192,1024]{1,0:T(8,128)} %copy-done.3, f32[512]{0:T(512)S(1)} %copy-done.5, f32[192]{0:T(256)S(1)} %add_rsqrt_fusion, f32[192]{0:T(256)S(1)} %broadcast_multiply_fusion), kind=kOutput, calls=%fused_computation.63 | convolution fusion | flops 102039552 | bytes 1707520 | tf_op jit(solution)/shard_map/dot_general | solution.py:104
  (20 shorter events, 0.1 us)
Async XLA Ops:
  6.5 152.8 %copy-start = (bf16[512,512]{1,0:T(8,128)(2,1)S(1)}, bf16[512,512]{1,0:T(8,128)(2,1)}, u32[]{:S(2)}) copy-start(bf16[512,512]{1,0:T(8,128)(2,1)} %param.17) | copy-start | bytes 1572868
  6.5 7.3 %copy-start.1 = (bf16[512,2048]{1,0:T(8,128)(2,1)S(1)}, bf16[512,2048]{1,0:T(8,128)(2,1)}, u32[]{:S(2)}) copy-start(bf16[512,2048]{1,0:T(8,128)(2,1)} %param.14) | copy-start | bytes 6291460
  6.5 69.6 %all-gather.2.cloned.1.call-start = ((), (), s32[]{:S(2)}) async-start(), calls=%async_computation | async-start | bytes 3342336 | tf_op jit(solution)/shard_map/all_gather | solution.py:84
  10.6 3.1 %copy-start.2 = (bf16[192,512]{1,0:T(8,128)(2,1)S(1)}, bf16[192,512]{1,0:T(8,128)(2,1)}, u32[]{:S(2)}) copy-start(bf16[192,512]{1,0:T(8,128)(2,1)} %fusion.15) | copy-start | bytes 589828
  11.5 4.5 %copy-start.6 = (u32[32]{0:T(128)S(1)}, u32[32]{0:T(128)}, u32[]{:S(2)}) copy-start(u32[32]{0:T(128)} %constant.154) | copy-start | bytes 388
  11.5 5.6 %copy-start.4 = (s32[192]{0:T(256)S(1)}, s32[192]{0:T(256)}, u32[]{:S(2)}) copy-start(s32[192]{0:T(256)} %param.12) | copy-start | bytes 2308
  14.2 0.9 copy-start.3
  76.2 83.1 %copy-start.5 = (f32[512]{0:T(512)S(1)}, f32[512]{0:T(512)}, u32[]{:S(2)}) copy-start(f32[512]{0:T(512)} %param.16) | copy-start | bytes 6148
  93.9 5.7 %slice-start = ((bf16[1536,1024]{0,1:T(8,128)(2,1)}), bf16[1536,512]{0,1:T(8,128)(2,1)S(1)}, s32[]{:S(2)}) async-start(bf16[1536,1024]{0,1:T(8,128)(2,1)} %copy.14), calls=%async_computation.1 | async-start | bytes 3145728 | tf_op jit(solution)/shard_map/while/body/eval_jaxpr/slice | solution.py:80
  135.1 5.7 %slice-start = ((bf16[1536,1024]{0,1:T(8,128)(2,1)}), bf16[1536,512]{0,1:T(8,128)(2,1)S(1)}, s32[]{:S(2)}) async-start(bf16[1536,1024]{0,1:T(8,128)(2,1)} %copy.14), calls=%async_computation.1 | async-start | bytes 3145728 | tf_op jit(solution)/shard_map/while/body/eval_jaxpr/slice | solution.py:80
Sparse Core Ops, SparseCore 0:
  10.8 44.6 all-gather.1
where the time goes:
time: 169 us; the launch traced here: 168 us
  blocking collectives  57.3 us (34%)
  matrix products  48.4 us (29%)
  local copies, waits for them, and re-layouts  31.8 us (19%)
  other arithmetic  16.5 us (10%)
  between operations  14.1 us (8%)
    unnamed x1, blocking collectives  57.3 us
    dot_general x2, matrix products, attend(): jnp.einsum('hqk,khd->qhd', weight, v_heads, preferred_element_type=jnp.fl...  35.6 us
    another operation x4, local copies, waits for them, and re-layouts  18.8 us
    eq x2, other arithmetic, relative_bias(): bucket == bucket_id  11.4 us
    dot_general x2, matrix products, from_inputs(): jnp.dot(blocks[0], back_weight, preferred_element_type=jnp.float32)  10.3 us
    slice x2, local copies, waits for them, and re-layouts, from_inputs(): key_block = both_proj[:, :tok_width].astype(jnp.bfloat16)  5.41 us
    unnamed x19, local copies, waits for them, and re-layouts  3.41 us
  transfers between devices with their start and end apart: 1, of which 0 were waited for; matrix products, arithmetic and copies ran while one was open for 4% of the time, Pallas kernels for 0%

commit v1 on v0

v1 whole, which is shorter than its diff:
```python
import functools

import jax
import jax.numpy as jnp
from jax import lax
from jax.experimental import pallas as pl
from jax.experimental.pallas import tpu as pltpu
from jax.sharding import PartitionSpec as P

HEADS = 8
BUCKETS = 16
EPSILON = 1e-05
LANES = 128
TAIL = 16
HIDDEN = 64
BF16 = jnp.bfloat16
F32 = jnp.float32
I32 = jnp.int32
VMEM = pl.BlockSpec(memory_space=pltpu.VMEM)
SMEM = pl.BlockSpec(memory_space=pltpu.SMEM)


def layer_norm(values, gain):
    centered = values - jnp.mean(values, axis=-1, keepdims=True)
    spread = jnp.mean(centered * centered, axis=-1, keepdims=True)
    return centered * lax.rsqrt(spread + EPSILON) * gain


def call(kernel, outs, specs, args, flops, vmem=48 << 20):
    return pl.pallas_call(
        kernel,
        out_shape=outs,
        in_specs=specs,
        out_specs=jax.tree.map(lambda _: VMEM, outs),
        compiler_params=pltpu.CompilerParams(vmem_limit_bytes=vmem),
        cost_estimate=pl.CostEstimate(flops=flops, bytes_accessed=1 << 20, transcendentals=0),
    )(*args)


def norm_kernel(tokens_ref, stamps_ref, gain_ref, out_ref):
    rows, width = tokens_ref.shape
    out_ref[:rows, :] = layer_norm(tokens_ref[...].astype(F32), gain_ref[...]).astype(BF16)
    stamps = jnp.broadcast_to(stamps_ref[...], (TAIL, rows))
    byte = lax.broadcasted_iota(I32, (TAIL, rows), 0)
    part = jnp.where(byte < 4, lax.shift_right_logical(stamps, 8 * jnp.minimum(byte, 3)) & 255, 0)
    out_ref[rows:, :] = jnp.zeros((TAIL, width), BF16)
    out_ref[rows:, :rows] = part.astype(F32).astype(BF16)


def front_kernel(own_ref, stamps_ref, w_ref, bias_ref, q_ref, gate_ref, stamp_ref, table_ref):
    rows, width = q_ref.shape
    scale = 0.5 * (width // HEADS) ** -0.5
    normed = own_ref[:rows, :]
    gate = jnp.dot(normed, w_ref[:, :width], preferred_element_type=F32)
    gate_ref[...] = (gate / (1 + jnp.exp(-gate))).astype(BF16)
    queries = jnp.dot(normed, w_ref[:, width:], preferred_element_type=F32).astype(BF16)
    q_ref[...] = (queries.astype(F32) * scale).astype(BF16)
    pad = -rows % LANES
    stamps = jnp.concatenate([stamps_ref[...], jnp.zeros((1, pad), I32)], axis=1)
    stamp_ref[...] = jnp.broadcast_to(stamps, (LANES, rows + pad)).T[:rows, :]
    heads, buckets = bias_ref.shape
    bias = jnp.concatenate([bias_ref[...], jnp.zeros((heads, LANES - buckets), F32)], axis=1)
    lane = lax.broadcasted_iota(I32, (heads, LANES), 1)
    bucket = jnp.clip(lax.shift_right_logical(33 - jnp.minimum(lane, 32), 1), 0, buckets - 1)
    table = 0.5 * jnp.take_along_axis(bias, bucket, axis=1)
    table_ref[...] = jnp.where(lane < HIDDEN, table, -1e30)


def add_blocks(pos_ref, q_ref, stamp_ref, blocks, w_ref, table_ref, acc_ref):
    rows, width = q_ref.shape
    size = width // HEADS
    count = len(blocks)
    keys = count * rows
    normed = jnp.concatenate([b[:rows, :] for b in blocks], axis=0)
    key_rows = jnp.dot(normed, w_ref[:, :width], preferred_element_type=F32).astype(BF16)
    value_rows = jnp.dot(normed, w_ref[:, width:], preferred_element_type=F32).astype(BF16)
    stamps = []
    for b in blocks:
        part = b[rows : rows + TAIL, :rows].astype(F32).astype(I32)
        stamps.append(
            part[0:1] + part[1:2] * 256 + part[2:3] * 65536 + part[3:4] * 16777216
        )
    stamps = jnp.concatenate(stamps, axis=1)
    col = lax.broadcasted_iota(I32, (1, keys), 1)
    key_pos = pos_ref[1] + col
    for i in range(1, count):
        key_pos = jnp.where(col >= i * rows, pos_ref[1 + i] + col - i * rows, key_pos)
    row_pos = pos_ref[0] + lax.broadcasted_iota(I32, (rows, LANES), 0)
    index = []
    for j in range(keys // LANES):
        cut = slice(j * LANES, (j + 1) * LANES)
        elapsed = stamp_ref[...] - stamps[:, cut]
        index.append(jnp.where(key_pos[:, cut] <= row_pos, lax.clz(elapsed), HIDDEN))
    lane = lax.broadcasted_iota(I32, (1, LANES), 1)
    per = LANES // size
    for p in range(HEADS // per):
        cut = slice(p * LANES, (p + 1) * LANES)
        total = acc_ref[:, cut]
        for h in range(per):
            mine = (lane // size) == h
            q = jnp.where(mine, q_ref[:, cut], 0).astype(BF16)
            score = lax.dot_general(
                q, key_rows[:, cut], (((1,), (1,)), ((), ())), preferred_element_type=F32
            )
            head = p * per + h
            table = jnp.broadcast_to(table_ref[head : head + 1, :], (rows, LANES))
            bias = jnp.concatenate(
                [jnp.take_along_axis(table, i, axis=1) for i in index], axis=1
            )
            half = score + bias
            weight = (half * jnp.tanh(half) + half).astype(BF16)
            values = jnp.where(mine, value_rows[:, cut], 0).astype(BF16)
            total = total + jnp.dot(weight, values, preferred_element_type=F32)
        acc_ref[:, cut] = total


def attend_kernel(count, first, pos_ref, q_ref, stamp_ref, *refs):
    blocks, rest = refs[:count], refs[count:]
    if first:
        w_ref, table_ref, out_ref = rest
        out_ref[...] = jnp.zeros_like(out_ref)
    else:
        w_ref, table_ref, acc_ref, out_ref = rest
        out_ref[...] = acc_ref[...]

    @pl.when(pos_ref[1 + count] > 0)
    def _():
        add_blocks(pos_ref, q_ref, stamp_ref, blocks, w_ref, table_ref, out_ref)


def last_kernel(count, pos_ref, q_ref, stamp_ref, *refs):
    blocks, rest = refs[:count], refs[count:]
    w_ref, table_ref, acc_ref, gate_ref, gain_ref, wo_ref, tokens_ref, out_ref, sum_ref = rest
    sum_ref[...] = acc_ref[...]

    @pl.when(pos_ref[1 + count] > 0)
    def _():
        add_blocks(pos_ref, q_ref, stamp_ref, blocks, w_ref, table_ref, sum_ref)

    gated = layer_norm(sum_ref[...], gain_ref[...]) * gate_ref[...].astype(F32)
    mixed = jnp.dot(gated.astype(BF16), wo_ref[...], preferred_element_type=F32)
    out_ref[...] = (tokens_ref[...].astype(F32) + mixed).astype(BF16)


def body(shards, tokens, stamps, norm_gain, w_proj, rel_bias, attn_gain, w_out):
    me = lax.axis_index("pb")
    rows, width = tokens.shape
    near = 1
    while near < 4 and shards % (2 * near) == 0:
        near *= 2
    levels = shards // near
    flips = levels & (levels - 1) == 0
    stamps = stamps.reshape(1, rows)

    def swap(block, bit):
        return lax.ppermute(block, "pb", [(i, i ^ bit) for i in range(shards)])

    def far(block, step):
        if flips:
            return swap(block, step * near)
        return lax.ppermute(
            block, "pb", [(i, (i + step * near) % shards) for i in range(shards)]
        )

    def level_of(step):
        return (me // near) ^ step if flips else (me // near - step) % levels

    own = call(
        norm_kernel,
        jax.ShapeDtypeStruct((rows + TAIL, width), BF16),
        [VMEM] * 3,
        (tokens, stamps, norm_gain.reshape(1, width)),
        10 * rows * width,
    )
    groups = {}
    heads = [own] + [far(own, step) for step in range(levels - 1, 0, -1)]
    steps = [0] + list(range(levels - 1, 0, -1))
    for step, block in zip(steps, heads, strict=True):
        blocks = [(0, block)]
        bit = near // 2
        while bit:
            blocks = blocks + [(k ^ bit, swap(b, bit)) for k, b in blocks]
            bit //= 2
        groups[step] = blocks

    queries, gate, stamp_rows, table = call(
        front_kernel,
        (
            jax.ShapeDtypeStruct((rows, width), BF16),
            jax.ShapeDtypeStruct((rows, width), BF16),
            jax.ShapeDtypeStruct((rows, LANES), I32),
            jax.ShapeDtypeStruct((rel_bias.shape[0], LANES), F32),
        ),
        [VMEM] * 4,
        (own, stamps, w_proj[:, : 2 * width], rel_bias),
        4 * rows * width * width,
    )
    back = w_proj[:, 2 * width :]
    total = None
    for step in steps:
        blocks = groups[step]
        level = level_of(step)
        pos = jnp.stack(
            [me * rows]
            + [(level * near + ((me % near) ^ k)) * rows for k, _ in blocks]
            + [(level <= me // near).astype(I32)]
        ).astype(I32)
        count = len(blocks)
        specs = [SMEM] + [VMEM] * (4 + count)
        args = [pos, queries, stamp_rows, *(b for _, b in blocks), back, table]
        flops = 8 * count * rows * width * (width + rows)
        if total is not None:
            args.append(total)
            specs.append(VMEM)
        if step != steps[-1]:
            total = call(
                functools.partial(attend_kernel, count, total is None),
                jax.ShapeDtypeStruct((rows, width), F32),
                specs,
                args,
                flops,
            )
            continue
        args += [gate, attn_gain.reshape(1, width), w_out, tokens]
        return pl.pallas_call(
            functools.partial(last_kernel, count),
            out_shape=jax.ShapeDtypeStruct((rows, width), BF16),
            in_specs=specs + [VMEM] * 4,
            out_specs=VMEM,
            scratch_shapes=[pltpu.VMEM((rows, width), F32)],
            compiler_params=pltpu.CompilerParams(vmem_limit_bytes=48 << 20),
        )(*args)


def solution(mesh):
    return jax.shard_map(
        functools.partial(body, mesh.shape["pb"]),
        mesh=mesh,
        in_specs=(P(("groups", "pb"), None), P(("groups", "pb")), P(), P(), P(), P(), P()),
        out_specs=P(("groups", "pb"), None),
        check_vma=False,
    )
```

time: 169 us -> 50.8 us (0.30)
  blocking collectives: 57.3 us -> 0 us
  matrix products: 48.4 us -> 0 us
  local copies, waits for them, and re-layouts: 31.8 us -> 4.36 us
  Pallas kernels: 0 us -> 19.5 us
  other arithmetic: 16.5 us -> 0 us
  starting transfers between devices: 0.01 us -> 14.3 us
  between operations: 14.1 us -> 0.16 us
  waiting for transfers between devices: 0.04 us -> 11.6 us
    unnamed x1 -> x0, blocking collectives: 57.3 us -> none
    dot_general x6 -> x0, matrix products: 48.4 us -> none  [the longest x2 35.6 us: attend(): jnp.einsum('hqk,khd->qhd', weight, v_heads, preferred_element_type=jnp.fl...]
    pallas_call x0 -> x6, Pallas kernels: none -> 19.5 us  [the longest x5 14.2 us: call(): pl.pallas_call(kernel, out_shape=outs, in_specs=specs, out_specs=jax.tree...]
    another operation x4, local copies, waits for them, and re-layouts: 18.8 us -> 0.33 us  [body(): jnp.stack([me * rows] + [(level * near + (me % near ^ k)) * rows for k, _...]
    ppermute x0 -> x15, starting transfers between devices: none -> 14.3 us  [swap(): return lax.ppermute(block, 'pb', [(i, i ^ bit) for i in range(shards)])]
    ppermute x0 -> x15, waiting for transfers between devices: none -> 11.6 us  [swap(): return lax.ppermute(block, 'pb', [(i, i ^ bit) for i in range(shards)])]
    eq x2 -> x0, other arithmetic: 11.4 us -> none  [relative_bias(): bucket == bucket_id]
    slice x8 -> x1, local copies, waits for them, and re-layouts: 7.74 us -> 1.71 us  [body(): back = w_proj[:, 2 * width:]]
  transfers between devices with their start and end apart: 1 -> 15, of which waited for: 0 -> 4; matrix products, arithmetic and copies ran while one was open for 4% -> 4% of each run, Pallas kernels for 0% -> 28%
where the time goes in v1:
time: 50.8 us; the launch traced here: 49.9 us
  Pallas kernels  19.5 us (38%)
  starting transfers between devices  14.3 us (28%)
  waiting for transfers between devices  11.6 us (23%)
  local copies, waits for them, and re-layouts  4.36 us (9%)
    ppermute x15, starting transfers between devices, swap(): return lax.ppermute(block, 'pb', [(i, i ^ bit) for i in range(shards)])  14.3 us
    pallas_call x5, Pallas kernels, call(): pl.pallas_call(kernel, out_shape=outs, in_specs=specs, out_specs=jax.tree...  14.2 us
    ppermute x15, waiting for transfers between devices, swap(): return lax.ppermute(block, 'pb', [(i, i ^ bit) for i in range(shards)])  11.6 us
    pallas_call x1, Pallas kernels, body(): pl.pallas_call(functools.partial(last_kernel, count), out_shape=jax.Shape...  5.29 us
    unnamed x16, local copies, waits for them, and re-layouts  2.31 us
    slice x1, local copies, waits for them, and re-layouts, body(): back = w_proj[:, 2 * width:]  1.71 us
  transfers between devices with their start and end apart: 15, of which 4 were waited for; matrix products, arithmetic and copies ran while one was open for 4% of the time, Pallas kernels for 28%

profile of v1, /device:TPU:31, one launch (start us, length us, event | category | flops | bytes accessed | tf_op | source)
XLA Modules:
  0.0 49.9 jit_solution(5870346570510381217)
XLA Ops:
  0.0 0.0 copy-start
  0.0 0.9 %copy-done = bf16[192,512]{1,0:T(8,128)(2,1)S(1)} copy-done((bf16[192,512]{1,0:T(8,128)(2,1)S(1)}, bf16[192,512]{1,0:T(8,128)(2,1)}, u32[]{:S(2)}) %copy-start) | copy-done | bytes 196632
  0.9 0.0 copy-start.4
  0.9 0.7 %copy-done.4 = s32[192]{0:T(256)S(1)} copy-done((s32[192]{0:T(256)S(1)}, s32[192]{0:T(256)}, u32[]{:S(2)}) %copy-start.4) | copy-done | bytes 792
  1.6 0.0 copy-start.6
  1.6 0.7 %copy-done.6 = f32[512]{0:T(512)S(1)} copy-done((f32[512]{0:T(512)S(1)}, f32[512]{0:T(512)}, u32[]{:S(2)}) %copy-start.6) | copy-done | bytes 2072
  2.3 0.2 shard_map.73.own_ref.refs_0_
  2.5 0.3 collective-permute-start.12
  2.8 0.0 collective-permute-start.8
  2.8 1.3 %collective-permute-start.4 = (bf16[208,512]{1,0:T(8,128)(2,1)S(1)}, bf16[208,512]{1,0:T(8,128)(2,1)S(1)}, u32[]{:S(2)}, u32[]{:S(2)}) collective-permute-start(bf16[208,512]{1,0:T(8,128)(2,1)S(1)} %shard_map.73.own_ref.refs_0_), channel_id=1, source_target_pairs={{0,8},{1,9},{2,10},{3,11},{4,12},{5,13},{6,14},{7,15},{8,0},{9,1},... | collective-permute-start | bytes 638984 | tf_op jit(solution)/shard_map/ppermute | solution.py:156
  4.2 1.5 %collective-permute-start.13 = (bf16[208,512]{1,0:T(8,128)(2,1)S(1)}, bf16[208,512]{1,0:T(8,128)(2,1)S(1)}, u32[]{:S(2)}, u32[]{:S(2)}) collective-permute-start(bf16[208,512]{1,0:T(8,128)(2,1)S(1)} %shard_map.73.own_ref.refs_0_), channel_id=1, source_target_pairs={{0,1},{1,0},{2,3},{3,2},{4,5},{5,4},{6,7},{7,6},{8,9},{9,8},{10,11... | collective-permute-start | bytes 638984 | tf_op jit(solution)/shard_map/ppermute | solution.py:156
  5.7 2.2 %collective-permute-start = (bf16[208,512]{1,0:T(8,128)(2,1)S(1)}, bf16[208,512]{1,0:T(8,128)(2,1)S(1)}, u32[]{:S(2)}, u32[]{:S(2)}) collective-permute-start(bf16[208,512]{1,0:T(8,128)(2,1)S(1)} %shard_map.73.own_ref.refs_0_), channel_id=1, source_target_pairs={{0,4},{1,5},{2,6},{3,7},{4,0},{5,1},{6,2},{7,3},{8,12},{9,13},{10,... | collective-permute-start | bytes 638984 | tf_op jit(solution)/shard_map/ppermute | solution.py:156
  7.9 0.0 copy-start.3
  7.9 0.0 copy-start.5
  7.9 0.8 %collective-permute-done.12.refs_1_ = bf16[208,512]{1,0:T(8,128)(2,1)S(1)} collective-permute-done((bf16[208,512]{1,0:T(8,128)(2,1)S(1)}, bf16[208,512]{1,0:T(8,128)(2,1)S(1)}, u32[]{:S(2)}, u32[]{:S(2)}) %collective-permute-start.12) | collective-permute-done | bytes 213024 | tf_op jit(solution)/shard_map/ppermute | solution.py:156
  8.7 1.5 %collective-permute-start.14 = (bf16[208,512]{1,0:T(8,128)(2,1)S(1)}, bf16[208,512]{1,0:T(8,128)(2,1)}, u32[]{:S(2)}, u32[]{:S(2)}) collective-permute-start(bf16[208,512]{1,0:T(8,128)(2,1)S(1)} %collective-permute-done.12.refs_1_), channel_id=1, source_target_pairs={{0,1},{1,0},{2,3},{3,2},{4,5},{5,4},{6,7},{7,6},{8,9},{9,8},{10,11... | collective-permute-start | bytes 638984 | tf_op jit(solution)/shard_map/ppermute | solution.py:156
  10.3 0.2 collective-permute-done.8.refs_0_
  10.5 1.2 %collective-permute-start.9 = (bf16[208,512]{1,0:T(8,128)(2,1)S(1)}, bf16[208,512]{1,0:T(8,128)(2,1)S(1)}, u32[]{:S(2)}, u32[]{:S(2)}) collective-permute-start(bf16[208,512]{1,0:T(8,128)(2,1)S(1)} %collective-permute-done.8.refs_0_), channel_id=1, source_target_pairs={{0,2},{1,3},{2,0},{3,1},{4,6},{5,7},{6,4},{7,5},{8,10},{9,11},{10,... | collective-permute-start | bytes 638984 | tf_op jit(solution)/shard_map/ppermute | solution.py:156
  11.7 10.5 %collective-permute-done.4.refs_0_ = bf16[208,512]{1,0:T(8,128)(2,1)S(1)} collective-permute-done((bf16[208,512]{1,0:T(8,128)(2,1)S(1)}, bf16[208,512]{1,0:T(8,128)(2,1)S(1)}, u32[]{:S(2)}, u32[]{:S(2)}) %collective-permute-start.4) | collective-permute-done | bytes 213024 | tf_op jit(solution)/shard_map/ppermute | solution.py:156
  22.2 1.2 %collective-permute-start.5 = (bf16[208,512]{1,0:T(8,128)(2,1)S(1)}, bf16[208,512]{1,0:T(8,128)(2,1)S(1)}, u32[]{:S(2)}, u32[]{:S(2)}) collective-permute-start(bf16[208,512]{1,0:T(8,128)(2,1)S(1)} %collective-permute-done.4.refs_0_), channel_id=1, source_target_pairs={{0,2},{1,3},{2,0},{3,1},{4,6},{5,7},{6,4},{7,5},{8,10},{9,11},{10,... | collective-permute-start | bytes 638984 | tf_op jit(solution)/shard_map/ppermute | solution.py:156
  23.4 1.7 %fusion = (bf16[512,1024]{1,0:T(8,128)(2,1)S(1)}, bf16[512,1024]{1,0:T(8,128)(2,1)S(1)}) fusion(bf16[512,2048]{1,0:T(8,128)(2,1)} %param.10), kind=kLoop, calls=%fused_computation | loop fusion | bytes 4194304 | tf_op jit(solution)/shard_map/slice | solution.py:198
  25.2 0.0 copy-done.3
  25.2 0.0 copy-done.5
  25.2 0.4 shard_map.74
  25.6 0.0 collective-permute-done.13.refs_2_
  25.6 2.2 %collective-permute-start.10 = (bf16[208,512]{1,0:T(8,128)(2,1)S(1)}, bf16[208,512]{1,0:T(8,128)(2,1)}, u32[]{:S(2)}, u32[]{:S(2)}) collective-permute-start(bf16[208,512]{1,0:T(8,128)(2,1)S(1)} %collective-permute-done.8.refs_0_), channel_id=1, source_target_pairs={{0,1},{1,0},{2,3},{3,2},{4,5},{5,4},{6,7},{7,6},{8,9},{9,8},{10,11... | collective-permute-start | bytes 638984 | tf_op jit(solution)/shard_map/ppermute | solution.py:156
  27.8 0.0 collective-permute-done.refs_0_
  27.8 0.2 collective-permute-start.1
  28.0 0.0 collective-permute-done.9.refs_1_
  28.0 0.4 collective-permute-start.11
  28.4 0.1 stack.111.pos_ref
  28.5 0.1 stack.106.pos_ref
  28.6 0.1 stack.99.pos_ref
  28.7 0.1 stack.92.pos_ref
  28.7 0.0 collective-permute-done.14.refs_3_
  28.7 0.2 collective-permute-start.6
  28.9 0.0 collective-permute-done.5.refs_1_
  28.9 1.0 %collective-permute-start.7 = (bf16[208,512]{1,0:T(8,128)(2,1)S(1)}, bf16[208,512]{1,0:T(8,128)(2,1)S(1)}, u32[]{:S(2)}, u32[]{:S(2)}) collective-permute-start(bf16[208,512]{1,0:T(8,128)(2,1)S(1)} %collective-permute-done.5.refs_1_), channel_id=1, source_target_pairs={{0,1},{1,0},{2,3},{3,2},{4,5},{5,4},{6,7},{7,6},{8,9},{9,8},{10,11... | collective-permute-start | bytes 638984 | tf_op jit(solution)/shard_map/ppermute | solution.py:156
  29.9 4.5 %shard_map.75.refs_6_ = f32[192,512]{1,0:T(8,128)S(1)} custom-call(s32[6]{0:T(128)S(1)} %stack.111.pos_ref, bf16[192,512]{1,0:T(8,128)(2,1)S(1)} %get-tuple-element.9.q_ref, s32[192,128]{1,0:T(8,128)S(1)} %get-tuple-element.10.stamp_ref, bf16[208,512]{1,0:T(8,128)(2,1)S(1)} %shard_map.73.own_ref.refs_0_, ...), custom_call_target="tpu_custom_call" | custom-call | flops 2214592512 | bytes 1048576 | tf_op jit(solution)/shard_map/pallas_call | solution.py:30
  34.5 0.0 collective-permute-done.10.refs_2_
  34.5 0.1 collective-permute-start.2
  34.5 0.1 collective-permute-done.1.refs_1_
  34.6 0.9 %collective-permute-start.3 = (bf16[208,512]{1,0:T(8,128)(2,1)S(1)}, bf16[208,512]{1,0:T(8,128)(2,1)S(1)}, u32[]{:S(2)}, u32[]{:S(2)}) collective-permute-start(bf16[208,512]{1,0:T(8,128)(2,1)S(1)} %collective-permute-done.1.refs_1_), channel_id=1, source_target_pairs={{0,1},{1,0},{2,3},{3,2},{4,5},{5,4},{6,7},{7,6},{8,9},{9,8},{10,11... | collective-permute-start | bytes 638984 | tf_op jit(solution)/shard_map/ppermute | solution.py:156
  35.5 0.0 collective-permute-done.11.refs_3_
  35.5 4.7 %shard_map.76.refs_6_ = f32[192,512]{1,0:T(8,128)S(1)} custom-call(s32[6]{0:T(128)S(1)} %stack.106.pos_ref, bf16[192,512]{1,0:T(8,128)(2,1)S(1)} %get-tuple-element.9.q_ref, s32[192,128]{1,0:T(8,128)S(1)} %get-tuple-element.10.stamp_ref, bf16[208,512]{1,0:T(8,128)(2,1)S(1)} %collective-permute-done.8.refs_0_, ...), custom_call_target="tpu_custom_call" | custom-call | flops 2214592512 | bytes 1048576 | tf_op jit(solution)/shard_map/pallas_call | solution.py:30
  40.2 0.0 copy-start.1
  40.2 0.0 copy-start.2
  40.2 0.0 copy-start.7
  40.2 0.0 collective-permute-done.6.refs_2_
  40.2 0.0 collective-permute-done.7.refs_3_
  40.2 4.3 %shard_map.77.refs_6_ = f32[192,512]{1,0:T(8,128)S(1)} custom-call(s32[6]{0:T(128)S(1)} %stack.99.pos_ref, bf16[192,512]{1,0:T(8,128)(2,1)S(1)} %get-tuple-element.9.q_ref, s32[192,128]{1,0:T(8,128)S(1)} %get-tuple-element.10.stamp_ref, bf16[208,512]{1,0:T(8,128)(2,1)S(1)} %collective-permute-done.4.refs_0_, ...), custom_call_target="tpu_custom_call" | custom-call | flops 2214592512 | bytes 1048576 | tf_op jit(solution)/shard_map/pallas_call | solution.py:30
  44.6 0.0 collective-permute-done.2.refs_2_
  44.6 0.0 collective-permute-done.3.refs_3_
  44.6 0.0 copy-done.1
  44.6 0.0 copy-done.2
  44.6 0.0 copy-done.7
  44.6 5.3 %shard_map.78 = bf16[192,512]{1,0:T(8,128)(2,1)} custom-call(s32[6]{0:T(128)S(1)} %stack.92.pos_ref, bf16[192,512]{1,0:T(8,128)(2,1)S(1)} %get-tuple-element.9.q_ref, s32[192,128]{1,0:T(8,128)S(1)} %get-tuple-element.10.stamp_ref, bf16[208,512]{1,0:T(8,128)(2,1)S(1)} %collective-permute-done.refs_0_, bf16[208,512]{1,0:T(8,128)(2,1)S(1)} %collective-permute-done.1.refs_1_, ...), custom_call_target="tpu_custom_call" | custom-call | tf_op jit(solution)/shard_map/pallas_call | solution.py:225
Async XLA Ops:
  0.0 0.9 %copy-start = (bf16[192,512]{1,0:T(8,128)(2,1)S(1)}, bf16[192,512]{1,0:T(8,128)(2,1)}, u32[]{:S(2)}) copy-start(bf16[192,512]{1,0:T(8,128)(2,1)} %refs_10_.1) | copy-start | bytes 589828
  0.9 0.7 %copy-start.4 = (s32[192]{0:T(256)S(1)}, s32[192]{0:T(256)}, u32[]{:S(2)}) copy-start(s32[192]{0:T(256)} %param.8) | copy-start | bytes 2308
  1.6 0.7 %copy-start.6 = (f32[512]{0:T(512)S(1)}, f32[512]{0:T(512)}, u32[]{:S(2)}) copy-start(f32[512]{0:T(512)} %param.9) | copy-start | bytes 6148
  2.5 6.2 %collective-permute-start.12 = (bf16[208,512]{1,0:T(8,128)(2,1)S(1)}, bf16[208,512]{1,0:T(8,128)(2,1)S(1)}, u32[]{:S(2)}, u32[]{:S(2)}) collective-permute-start(bf16[208,512]{1,0:T(8,128)(2,1)S(1)} %shard_map.73.own_ref.refs_0_), channel_id=1, source_target_pairs={{0,2},{1,3},{2,0},{3,1},{4,6},{5,7},{6,4},{7,5},{8,10},{9,11},{10,... | collective-permute-start | bytes 638984 | tf_op jit(solution)/shard_map/ppermute | solution.py:156
  2.8 7.7 %collective-permute-start.8 = (bf16[208,512]{1,0:T(8,128)(2,1)S(1)}, bf16[208,512]{1,0:T(8,128)(2,1)S(1)}, u32[]{:S(2)}, u32[]{:S(2)}) collective-permute-start(bf16[208,512]{1,0:T(8,128)(2,1)S(1)} %shard_map.73.own_ref.refs_0_), channel_id=1, source_target_pairs={{0,12},{1,13},{2,14},{3,15},{4,8},{5,9},{6,10},{7,11},{8,4},{9,5},... | collective-permute-start | bytes 638984 | tf_op jit(solution)/shard_map/ppermute | solution.py:156
  2.8 19.4 %collective-permute-start.4 = (bf16[208,512]{1,0:T(8,128)(2,1)S(1)}, bf16[208,512]{1,0:T(8,128)(2,1)S(1)}, u32[]{:S(2)}, u32[]{:S(2)}) collective-permute-start(bf16[208,512]{1,0:T(8,128)(2,1)S(1)} %shard_map.73.own_ref.refs_0_), channel_id=1, source_target_pairs={{0,8},{1,9},{2,10},{3,11},{4,12},{5,13},{6,14},{7,15},{8,0},{9,1},... | collective-permute-start | bytes 638984 | tf_op jit(solution)/shard_map/ppermute | solution.py:156
  4.2 21.4 %collective-permute-start.13 = (bf16[208,512]{1,0:T(8,128)(2,1)S(1)}, bf16[208,512]{1,0:T(8,128)(2,1)S(1)}, u32[]{:S(2)}, u32[]{:S(2)}) collective-permute-start(bf16[208,512]{1,0:T(8,128)(2,1)S(1)} %shard_map.73.own_ref.refs_0_), channel_id=1, source_target_pairs={{0,1},{1,0},{2,3},{3,2},{4,5},{5,4},{6,7},{7,6},{8,9},{9,8},{10,11... | collective-permute-start | bytes 638984 | tf_op jit(solution)/shard_map/ppermute | solution.py:156
  5.7 22.1 %collective-permute-start = (bf16[208,512]{1,0:T(8,128)(2,1)S(1)}, bf16[208,512]{1,0:T(8,128)(2,1)S(1)}, u32[]{:S(2)}, u32[]{:S(2)}) collective-permute-start(bf16[208,512]{1,0:T(8,128)(2,1)S(1)} %shard_map.73.own_ref.refs_0_), channel_id=1, source_target_pairs={{0,4},{1,5},{2,6},{3,7},{4,0},{5,1},{6,2},{7,3},{8,12},{9,13},{10,... | collective-permute-start | bytes 638984 | tf_op jit(solution)/shard_map/ppermute | solution.py:156
  7.9 17.3 %copy-start.3 = (f32[8,16]{1,0:T(8,128)S(1)}, f32[8,16]{1,0:T(8,128)}, u32[]{:S(2)}) copy-start(f32[8,16]{1,0:T(8,128)} %bias_ref.1) | copy-start | bytes 1540
  7.9 17.3 %copy-start.5 = (s32[192]{0:T(256)S(1)}, s32[192]{0:T(256)}, u32[]{:S(2)}) copy-start(s32[192]{0:T(256)} %param.8) | copy-start | bytes 2308
  8.7 20.0 %collective-permute-start.14 = (bf16[208,512]{1,0:T(8,128)(2,1)S(1)}, bf16[208,512]{1,0:T(8,128)(2,1)}, u32[]{:S(2)}, u32[]{:S(2)}) collective-permute-start(bf16[208,512]{1,0:T(8,128)(2,1)S(1)} %collective-permute-done.12.refs_1_), channel_id=1, source_target_pairs={{0,1},{1,0},{2,3},{3,2},{4,5},{5,4},{6,7},{7,6},{8,9},{9,8},{10,11... | collective-permute-start | bytes 638984 | tf_op jit(solution)/shard_map/ppermute | solution.py:156
  10.5 17.5 %collective-permute-start.9 = (bf16[208,512]{1,0:T(8,128)(2,1)S(1)}, bf16[208,512]{1,0:T(8,128)(2,1)S(1)}, u32[]{:S(2)}, u32[]{:S(2)}) collective-permute-start(bf16[208,512]{1,0:T(8,128)(2,1)S(1)} %collective-permute-done.8.refs_0_), channel_id=1, source_target_pairs={{0,2},{1,3},{2,0},{3,1},{4,6},{5,7},{6,4},{7,5},{8,10},{9,11},{10,... | collective-permute-start | bytes 638984 | tf_op jit(solution)/shard_map/ppermute | solution.py:156
  22.2 6.7 %collective-permute-start.5 = (bf16[208,512]{1,0:T(8,128)(2,1)S(1)}, bf16[208,512]{1,0:T(8,128)(2,1)S(1)}, u32[]{:S(2)}, u32[]{:S(2)}) collective-permute-start(bf16[208,512]{1,0:T(8,128)(2,1)S(1)} %collective-permute-done.4.refs_0_), channel_id=1, source_target_pairs={{0,2},{1,3},{2,0},{3,1},{4,6},{5,7},{6,4},{7,5},{8,10},{9,11},{10,... | collective-permute-start | bytes 638984 | tf_op jit(solution)/shard_map/ppermute | solution.py:156
  25.6 8.9 %collective-permute-start.10 = (bf16[208,512]{1,0:T(8,128)(2,1)S(1)}, bf16[208,512]{1,0:T(8,128)(2,1)}, u32[]{:S(2)}, u32[]{:S(2)}) collective-permute-start(bf16[208,512]{1,0:T(8,128)(2,1)S(1)} %collective-permute-done.8.refs_0_), channel_id=1, source_target_pairs={{0,1},{1,0},{2,3},{3,2},{4,5},{5,4},{6,7},{7,6},{8,9},{9,8},{10,11... | collective-permute-start | bytes 638984 | tf_op jit(solution)/shard_map/ppermute | solution.py:156
  27.8 6.8 %collective-permute-start.1 = (bf16[208,512]{1,0:T(8,128)(2,1)S(1)}, bf16[208,512]{1,0:T(8,128)(2,1)S(1)}, u32[]{:S(2)}, u32[]{:S(2)}) collective-permute-start(bf16[208,512]{1,0:T(8,128)(2,1)S(1)} %collective-permute-done.refs_0_), channel_id=1, source_target_pairs={{0,2},{1,3},{2,0},{3,1},{4,6},{5,7},{6,4},{7,5},{8,10},{9,11},{10,... | collective-permute-start | bytes 638984 | tf_op jit(solution)/shard_map/ppermute | solution.py:156
  28.0 7.4 %collective-permute-start.11 = (bf16[208,512]{1,0:T(8,128)(2,1)S(1)}, bf16[208,512]{1,0:T(8,128)(2,1)}, u32[]{:S(2)}, u32[]{:S(2)}) collective-permute-start(bf16[208,512]{1,0:T(8,128)(2,1)S(1)} %collective-permute-done.9.refs_1_), channel_id=1, source_target_pairs={{0,1},{1,0},{2,3},{3,2},{4,5},{5,4},{6,7},{7,6},{8,9},{9,8},{10,11... | collective-permute-start | bytes 638984 | tf_op jit(solution)/shard_map/ppermute | solution.py:156
  28.7 11.5 %collective-permute-start.6 = (bf16[208,512]{1,0:T(8,128)(2,1)S(1)}, bf16[208,512]{1,0:T(8,128)(2,1)S(1)}, u32[]{:S(2)}, u32[]{:S(2)}) collective-permute-start(bf16[208,512]{1,0:T(8,128)(2,1)S(1)} %collective-permute-done.4.refs_0_), channel_id=1, source_target_pairs={{0,1},{1,0},{2,3},{3,2},{4,5},{5,4},{6,7},{7,6},{8,9},{9,8},{10,11... | collective-permute-start | bytes 638984 | tf_op jit(solution)/shard_map/ppermute | solution.py:156
  28.9 11.3 %collective-permute-start.7 = (bf16[208,512]{1,0:T(8,128)(2,1)S(1)}, bf16[208,512]{1,0:T(8,128)(2,1)S(1)}, u32[]{:S(2)}, u32[]{:S(2)}) collective-permute-start(bf16[208,512]{1,0:T(8,128)(2,1)S(1)} %collective-permute-done.5.refs_1_), channel_id=1, source_target_pairs={{0,1},{1,0},{2,3},{3,2},{4,5},{5,4},{6,7},{7,6},{8,9},{9,8},{10,11... | collective-permute-start | bytes 638984 | tf_op jit(solution)/shard_map/ppermute | solution.py:156
  34.5 10.1 %collective-permute-start.2 = (bf16[208,512]{1,0:T(8,128)(2,1)S(1)}, bf16[208,512]{1,0:T(8,128)(2,1)S(1)}, u32[]{:S(2)}, u32[]{:S(2)}) collective-permute-start(bf16[208,512]{1,0:T(8,128)(2,1)S(1)} %collective-permute-done.refs_0_), channel_id=1, source_target_pairs={{0,1},{1,0},{2,3},{3,2},{4,5},{5,4},{6,7},{7,6},{8,9},{9,8},{10,11... | collective-permute-start | bytes 638984 | tf_op jit(solution)/shard_map/ppermute | solution.py:156
  34.6 10.0 %collective-permute-start.3 = (bf16[208,512]{1,0:T(8,128)(2,1)S(1)}, bf16[208,512]{1,0:T(8,128)(2,1)S(1)}, u32[]{:S(2)}, u32[]{:S(2)}) collective-permute-start(bf16[208,512]{1,0:T(8,128)(2,1)S(1)} %collective-permute-done.1.refs_1_), channel_id=1, source_target_pairs={{0,1},{1,0},{2,3},{3,2},{4,5},{5,4},{6,7},{7,6},{8,9},{9,8},{10,11... | collective-permute-start | bytes 638984 | tf_op jit(solution)/shard_map/ppermute | solution.py:156
  40.2 4.4 %copy-start.1 = (bf16[192,512]{1,0:T(8,128)(2,1)S(1)}, bf16[192,512]{1,0:T(8,128)(2,1)}, u32[]{:S(2)}) copy-start(bf16[192,512]{1,0:T(8,128)(2,1)} %refs_10_.1) | copy-start | bytes 589828
  40.2 4.4 %copy-start.2 = (bf16[512,512]{1,0:T(8,128)(2,1)S(1)}, bf16[512,512]{1,0:T(8,128)(2,1)}, u32[]{:S(2)}) copy-start(bf16[512,512]{1,0:T(8,128)(2,1)} %refs_9_.1) | copy-start | bytes 1572868
  40.2 4.4 %copy-start.7 = (f32[512]{0:T(512)S(1)}, f32[512]{0:T(512)}, u32[]{:S(2)}) copy-start(f32[512]{0:T(512)} %param.12) | copy-start | bytes 6148

commit v2 on v1

v2 whole, which is shorter than its diff:
```python
import functools

import jax
import jax.numpy as jnp
from jax import lax
from jax.experimental import pallas as pl
from jax.experimental.pallas import tpu as pltpu
from jax.sharding import PartitionSpec as P

HEADS = 8
BUCKETS = 16
EPSILON = 1e-05
LANES = 128
TAIL = 16
HIDDEN = 64
BF16 = jnp.bfloat16
F32 = jnp.float32
I32 = jnp.int32
VMEM = pl.BlockSpec(memory_space=pltpu.VMEM)
SMEM = pl.BlockSpec(memory_space=pltpu.SMEM)
HBM = pl.BlockSpec(memory_space=pltpu.HBM)
VMEM_LIMIT = 12 << 20


def layer_norm(values, gain):
    centered = values - jnp.mean(values, axis=-1, keepdims=True)
    spread = jnp.mean(centered * centered, axis=-1, keepdims=True)
    return centered * lax.rsqrt(spread + EPSILON) * gain


def norm_kernel(tokens_hbm, stamps_hbm, gain_hbm, out_ref, tokens_ref, stamps_ref, gain_ref, sems):
    copies = [
        pltpu.make_async_copy(src, dst, sems.at[i])
        for i, (src, dst) in enumerate(
            ((tokens_hbm, tokens_ref), (stamps_hbm, stamps_ref), (gain_hbm, gain_ref))
        )
    ]
    for copy in copies:
        copy.start()
    for copy in copies:
        copy.wait()
    rows, width = tokens_ref.shape
    out_ref[:rows, :] = layer_norm(tokens_ref[...].astype(F32), gain_ref[...]).astype(BF16)
    stamps = jnp.broadcast_to(stamps_ref[...], (TAIL, rows))
    byte = lax.broadcasted_iota(I32, (TAIL, rows), 0)
    part = jnp.where(byte < 4, lax.shift_right_logical(stamps, 8 * jnp.minimum(byte, 3)) & 255, 0)
    out_ref[rows:, :] = jnp.zeros((TAIL, width), BF16)
    out_ref[rows:, :rows] = part.astype(F32).astype(BF16)


def stamps_of(block):
    rows = block.shape[0] - TAIL
    part = block[rows:, :rows].astype(F32).astype(I32)
    return part[0:1] + part[1:2] * 256 + part[2:3] * 65536 + part[3:4] * 16777216


def down_rows(stamps):
    rows = stamps.shape[1]
    pad = -rows % LANES
    stamps = jnp.concatenate([stamps, jnp.zeros((1, pad), I32)], axis=1)
    return jnp.broadcast_to(stamps, (LANES, rows + pad)).T[:rows, :]


def queries_of(normed, weight):
    width = normed.shape[1]
    scale = 0.5 * (width // HEADS) ** -0.5
    queries = jnp.dot(normed, weight, preferred_element_type=F32)
    return (queries.astype(BF16).astype(F32) * scale).astype(BF16)


def relay_kernel(own_ref, other_ref, out_ref):
    del other_ref
    out_ref[...] = own_ref[...]


def front_kernel(own_ref, w_ref, bias_ref, q_ref, gate_ref, stamp_ref, table_ref):
    rows, width = q_ref.shape
    stamp_ref[...] = down_rows(stamps_of(own_ref))
    normed = own_ref[:rows, :]
    gate = jnp.dot(normed, w_ref[:, :width], preferred_element_type=F32)
    gate_ref[...] = (gate / (1 + jnp.exp(-gate))).astype(BF16)
    q_ref[...] = queries_of(normed, w_ref[:, width : 2 * width])
    heads, buckets = bias_ref.shape
    bias = jnp.concatenate([bias_ref[...], jnp.zeros((heads, LANES - buckets), F32)], axis=1)
    lane = lax.broadcasted_iota(I32, (heads, LANES), 1)
    bucket = jnp.clip(lax.shift_right_logical(33 - jnp.minimum(lane, 32), 1), 0, buckets - 1)
    table = 0.5 * jnp.take_along_axis(bias, bucket, axis=1)
    table_ref[...] = jnp.where(lane < HIDDEN, table, -1e30)


def add_blocks(first_row, first_keys, q_ref, stamp_ref, blocks, w_ref, table_ref, acc_ref):
    rows, width = q_ref.shape
    size = width // HEADS
    count = len(blocks)
    keys = count * rows
    normed = jnp.concatenate([b[:rows, :] for b in blocks], axis=0)
    key_rows = jnp.dot(normed, w_ref[:, 2 * width : 3 * width], preferred_element_type=F32).astype(BF16)
    value_rows = jnp.dot(normed, w_ref[:, 3 * width :], preferred_element_type=F32).astype(BF16)
    stamps = jnp.concatenate([stamps_of(b) for b in blocks], axis=1)
    col = lax.broadcasted_iota(I32, (1, keys), 1)
    key_pos = first_keys[0] + col
    for i in range(1, count):
        key_pos = jnp.where(col >= i * rows, first_keys[i] + col - i * rows, key_pos)
    row_pos = first_row + lax.broadcasted_iota(I32, (rows, LANES), 0)
    index = []
    for j in range(keys // LANES):
        cut = slice(j * LANES, (j + 1) * LANES)
        elapsed = stamp_ref[...] - stamps[:, cut]
        index.append(jnp.where(key_pos[:, cut] <= row_pos, lax.clz(elapsed), HIDDEN))
    lane = lax.broadcasted_iota(I32, (1, LANES), 1)
    per = LANES // size
    for p in range(HEADS // per):
        cut = slice(p * LANES, (p + 1) * LANES)
        total = acc_ref[:, cut]
        for h in range(per):
            mine = (lane // size) == h
            q = jnp.where(mine, q_ref[:, cut], 0).astype(BF16)
            score = lax.dot_general(
                q, key_rows[:, cut], (((1,), (1,)), ((), ())), preferred_element_type=F32
            )
            head = p * per + h
            table = jnp.broadcast_to(table_ref[head : head + 1, :], (rows, LANES))
            bias = jnp.concatenate(
                [jnp.take_along_axis(table, i, axis=1) for i in index], axis=1
            )
            half = score + bias
            weight = (half * jnp.tanh(half) + half).astype(BF16)
            values = jnp.where(mine, value_rows[:, cut], 0).astype(BF16)
            total = total + jnp.dot(weight, values, preferred_element_type=F32)
        acc_ref[:, cut] = total


def add_sets(sizes, pos_ref, q_ref, stamp_ref, blocks, w_ref, table_ref, acc_ref):
    at, done = 1, 0
    for size in sizes:
        keys = [pos_ref[at + 1 + i] for i in range(size)]
        part = blocks[done : done + size]

        @pl.when(pos_ref[at] > 0)
        def _(keys=keys, part=part):
            add_blocks(pos_ref[0], keys, q_ref, stamp_ref, part, w_ref, table_ref, acc_ref)

        at, done = at + 1 + size, done + size


def attend_kernel(sizes, first, pos_ref, q_ref, stamp_ref, *refs):
    count = sum(sizes)
    blocks, rest = refs[:count], refs[count:]
    if first:
        w_ref, table_ref, out_ref, tick_ref = rest
        out_ref[...] = jnp.zeros_like(out_ref)
    else:
        w_ref, table_ref, acc_ref, _, out_ref, tick_ref = rest
        out_ref[...] = acc_ref[...]
    add_sets(sizes, pos_ref, q_ref, stamp_ref, blocks, w_ref, table_ref, out_ref)
    tick_ref[...] = jnp.zeros_like(tick_ref)


def return_kernel(count, pos_ref, asked_ref, *refs):
    blocks, rest = refs[:count], refs[count:]
    w_ref, table_ref, out_ref, tick_ref, q_ref, stamp_ref, sum_ref = rest
    tick_ref[...] = jnp.zeros_like(tick_ref)

    @pl.when(pos_ref[1] > 0)
    def _():
        rows = out_ref.shape[0]
        q_ref[...] = queries_of(asked_ref[:rows, :], w_ref[:, w_ref.shape[1] // 4 : w_ref.shape[1] // 2])
        stamp_ref[...] = down_rows(stamps_of(asked_ref))
        sum_ref[...] = jnp.zeros_like(sum_ref)
        add_sets((count,), pos_ref, q_ref, stamp_ref, blocks, w_ref, table_ref, sum_ref)
        out_ref[...] = sum_ref[...].astype(BF16)


def last_kernel(sum_ref, given_ref, gate_ref, gain_ref, wo_ref, tokens_ref, out_ref):
    attended = sum_ref[...] + given_ref[...].astype(F32)
    gated = layer_norm(attended, gain_ref[...]) * gate_ref[...].astype(F32)
    mixed = jnp.dot(gated.astype(BF16), wo_ref[...], preferred_element_type=F32)
    out_ref[...] = (tokens_ref[...].astype(F32) + mixed).astype(BF16)


def pin_kernel(block_ref, tick_ref, out_ref):
    del block_ref, tick_ref, out_ref


def pin(block, tick):
    return pl.pallas_call(
        pin_kernel,
        out_shape=jax.ShapeDtypeStruct(block.shape, block.dtype),
        in_specs=[pl.BlockSpec(memory_space=pl.ANY)] * 2,
        out_specs=pl.BlockSpec(memory_space=pl.ANY),
        input_output_aliases={0: 0},
        compiler_params=pltpu.CompilerParams(vmem_limit_bytes=1 << 20),
    )(block, tick)


def body(shards, tokens, stamps, norm_gain, w_proj, rel_bias, attn_gain, w_out):
    me = lax.axis_index("pb")
    rows, width = tokens.shape
    near = 4
    levels = shards // near
    level, spot = me // near, me % near

    def swap(block, bit):
        return lax.ppermute(block, "pb", [(i, i ^ bit) for i in range(shards)])

    def hop(block, pairs):
        return lax.ppermute(
            block, "pb", [(a * near + i, b * near + i) for a, b in pairs for i in range(near)]
        )

    own = pl.pallas_call(
        norm_kernel,
        out_shape=jax.ShapeDtypeStruct((rows + TAIL, width), BF16),
        in_specs=[HBM] * 3,
        out_specs=VMEM,
        scratch_shapes=[
            pltpu.VMEM((rows, width), BF16),
            pltpu.VMEM((1, rows), I32),
            pltpu.VMEM((1, width), F32),
            pltpu.SemaphoreType.DMA((3,)),
        ],
        compiler_params=pltpu.CompilerParams(vmem_limit_bytes=56 << 20),
    )(tokens, stamps.reshape(1, rows), norm_gain.reshape(1, width))

    far = {}
    for step in range(levels - 2, 0, -1):
        pairs = [(z, z + step) for z in range(levels - step)]
        if step == levels - 2:
            pairs.append((levels - 1, 0))
        far[step] = hop(own, pairs)
    by_core = swap(own, 1)
    own = pl.pallas_call(
        relay_kernel,
        out_shape=jax.ShapeDtypeStruct(own.shape, BF16),
        in_specs=[VMEM] * 2,
        out_specs=VMEM,
        compiler_params=pltpu.CompilerParams(vmem_limit_bytes=2 << 20),
    )(own, by_core)
    by_y = swap(own, 2)
    queries, gate, stamp_rows, table = pl.pallas_call(
        front_kernel,
        out_shape=(
            jax.ShapeDtypeStruct((rows, width), BF16),
            jax.ShapeDtypeStruct((rows, width), BF16),
            jax.ShapeDtypeStruct((rows, LANES), I32),
            jax.ShapeDtypeStruct((rel_bias.shape[0], LANES), F32),
        ),
        in_specs=[VMEM] * 3,
        out_specs=(VMEM,) * 4,
        compiler_params=pltpu.CompilerParams(vmem_limit_bytes=VMEM_LIMIT),
        cost_estimate=pl.CostEstimate(
            flops=4 * rows * width * width, bytes_accessed=5 << 18, transcendentals=0
        ),
    )(own, w_proj, rel_bias)

    def row_of(step, bits):
        return ((level - step) * near + (spot ^ bits)) * rows

    def positions(sets):
        pos = [me * rows]
        for step, blocks in sets:
            seen = [row_of(step, bits) for bits, _ in blocks]
            flag = functools.reduce(jnp.minimum, seen) <= me * rows
            pos += [(flag & (level >= step)).astype(I32), *seen]
        return jnp.stack(pos).astype(I32)

    tick_shape = jax.ShapeDtypeStruct((8, LANES), F32)

    def attend(sets, total, *more, weight=8):
        sizes = tuple(len(blocks) for _, blocks in sets)
        blocks = [b for _, part in sets for _, b in part]
        args = [positions(sets), queries, stamp_rows, *blocks, w_proj, table]
        args += [] if total is None else [total]
        args += more
        flops = weight * len(blocks) * rows * width * (width + rows)
        return pl.pallas_call(
            functools.partial(attend_kernel, sizes, total is None),
            out_shape=(jax.ShapeDtypeStruct((rows, width), F32), tick_shape),
            in_specs=[SMEM] + [VMEM] * (len(args) - 1),
            out_specs=(VMEM, VMEM),
            compiler_params=pltpu.CompilerParams(vmem_limit_bytes=VMEM_LIMIT),
            cost_estimate=pl.CostEstimate(
                flops=flops, bytes_accessed=weight << 17, transcendentals=0
            ),
        )(*args)

    total, tick = attend([(0, [(0, own), (1, by_core)])], None)
    by_y = pin(by_y, tick)
    by_both = swap(by_y, 1)
    total, tick = attend([(0, [(2, by_y), (3, by_both)])], total, tick)
    here = [(0, own), (1, by_core), (2, by_y), (3, by_both)]
    across = {}
    for step in sorted(far):
        block = far[step]
        if step == levels - 2:
            block = far[step] = pin(block, tick)
        across[step] = swap(block, 2)
        beside = swap(block, 1)
        if step == levels - 2:
            pos = jnp.stack(
                [((levels - 1) * near + spot) * rows, (level == 0).astype(I32)]
                + [(spot ^ bits) * rows for bits, _ in here]
            ).astype(I32)
            returned, tick = pl.pallas_call(
                functools.partial(return_kernel, near),
                out_shape=(jax.ShapeDtypeStruct((rows, width), BF16), tick_shape),
                in_specs=[SMEM] + [VMEM] * (near + 3),
                out_specs=(VMEM, VMEM),
                scratch_shapes=[
                    pltpu.VMEM((rows, width), BF16),
                    pltpu.VMEM((rows, LANES), I32),
                    pltpu.VMEM((rows, width), F32),
                ],
                compiler_params=pltpu.CompilerParams(vmem_limit_bytes=VMEM_LIMIT),
                cost_estimate=pl.CostEstimate(
                    flops=32 * rows * width * (width + rows),
                    bytes_accessed=1 << 20,
                    transcendentals=0,
                ),
            )(pos, block, *(b for _, b in here), w_proj, table)
            given = hop(returned, [(0, levels - 1)])
        far[step] = [(0, block), (1, beside)]
    ticks = []
    for step in sorted(far):
        total, tick = attend([(step, far[step])], total, tick)
        ticks.append(tick)
    for step, done in zip(sorted(far), ticks, strict=True):
        block = pin(across[step], done)
        sets = [(step, [(2, block), (3, swap(block, 1))])]
        total, tick = attend(sets, total, tick, weight=1)
    return pl.pallas_call(
        last_kernel,
        out_shape=jax.ShapeDtypeStruct((rows, width), BF16),
        in_specs=[VMEM] * 6,
        out_specs=VMEM,
        compiler_params=pltpu.CompilerParams(vmem_limit_bytes=VMEM_LIMIT),
    )(total, given, gate, attn_gain.reshape(1, width), w_out, tokens)


def solution(mesh):
    return jax.shard_map(
        functools.partial(body, mesh.shape["pb"]),
        mesh=mesh,
        in_specs=(P(("groups", "pb"), None), P(("groups", "pb")), P(), P(), P(), P(), P()),
        out_specs=P(("groups", "pb"), None),
        check_vma=False,
    )
```

time: 50.8 us -> 41.8 us (0.82)
  the two profiles are of different devices: /device:TPU:31 before, /device:TPU:19 now
where the time goes in v2:
time: 41.8 us; the launch traced here: 41.5 us
  Pallas kernels  17.6 us (42%)
  starting transfers between devices  14.4 us (34%)
  local copies, waits for them, and re-layouts  4.5 us (11%)
  waiting for transfers between devices  4.33 us (10%)
  other arithmetic  0.46 us (1%)
    pallas_call x6, Pallas kernels, attend(): pl.pallas_call(functools.partial(attend_kernel, sizes, total is None), ou...  13.6 us
    ppermute x9, starting transfers between devices, swap(): return lax.ppermute(block, 'pb', [(i, i ^ bit) for i in range(shards)])  8.59 us
    ppermute x3, starting transfers between devices, hop(): lax.ppermute(block, 'pb', [(a * near + i, b * near + i) for a, b in pairs...  5.77 us
    unnamed x14, local copies, waits for them, and re-layouts  4.42 us
    ppermute x3, waiting for transfers between devices, hop(): lax.ppermute(block, 'pb', [(a * near + i, b * near + i) for a, b in pairs...  4.3 us
    pallas_call x1, Pallas kernels, body(): pl.pallas_call(norm_kernel, out_shape=jax.ShapeDtypeStruct((rows + TAIL,...  1.85 us
    pallas_call x1, Pallas kernels, body(): pl.pallas_call(last_kernel, out_shape=jax.ShapeDtypeStruct((rows, width),...  1.12 us
  transfers between devices with their start and end apart: 12, of which 1 were waited for; matrix products, arithmetic and copies ran while one was open for 1% of the time, Pallas kernels for 35%

profile of v2, /device:TPU:19, one launch (start us, length us, event | category | flops | bytes accessed | tf_op | source)
XLA Modules:
  0.0 41.5 jit_solution(9871141280948963758)
XLA Ops:
  0.0 1.9 %shard_map.73.own_ref = bf16[208,512]{1,0:T(8,128)(2,1)} custom-call(bf16[192,512]{1,0:T(8,128)(2,1)} %tokens_ref.1, s32[1,192]{1,0:T(1,128)} %bitcast.30, f32[1,512]{1,0:T(1,128)} %bitcast.29), custom_call_target="tpu_custom_call" | custom-call | tf_op jit(solution)/shard_map/pallas_call | solution.py:211
  1.9 0.7 %collective-permute-start = (bf16[208,512]{1,0:T(8,128)(2,1)}, bf16[208,512]{1,0:T(8,128)(2,1)S(1)}, u32[]{:S(2)}, u32[]{:S(2)}) collective-permute-start(bf16[208,512]{1,0:T(8,128)(2,1)} %shard_map.73.own_ref), channel_id=1, source_target_pairs={{0,1},{1,0},{2,3},{3,2},{4,5},{5,4},{6,7},{7,6},{8,9},{9,8},{10,11... | collective-permute-start | bytes 638984 | tf_op jit(solution)/shard_map/ppermute | solution.py:204
  2.6 1.3 %collective-permute-start.1 = (bf16[208,512]{1,0:T(8,128)(2,1)}, bf16[208,512]{1,0:T(8,128)(2,1)S(1)}, u32[]{:S(2)}, u32[]{:S(2)}) collective-permute-start(bf16[208,512]{1,0:T(8,128)(2,1)} %shard_map.73.own_ref), channel_id=1, source_target_pairs={{0,8},{1,9},{2,10},{3,11},{4,12},{5,13},{6,14},{7,15},{12,0},{13,1... | collective-permute-start | bytes 638984 | tf_op jit(solution)/shard_map/ppermute | solution.py:207
  3.9 3.8 %collective-permute-start.6 = (bf16[208,512]{1,0:T(8,128)(2,1)}, bf16[208,512]{1,0:T(8,128)(2,1)S(1)}, u32[]{:S(2)}, u32[]{:S(2)}) collective-permute-start(bf16[208,512]{1,0:T(8,128)(2,1)} %shard_map.73.own_ref), channel_id=1, source_target_pairs={{0,4},{1,5},{2,6},{3,7},{4,8},{5,9},{6,10},{7,11},{8,12},{9,13},{1... | collective-permute-start | bytes 638984 | tf_op jit(solution)/shard_map/ppermute | solution.py:207
  7.8 0.1 stack.155.pos_ref
  7.9 0.1 pad_add_fusion.2.pos_ref
  8.0 0.0 collective-permute-done.other_ref.refs_1_
  8.0 0.0 copy-start.2
  8.0 0.9 %copy-done.2 = bf16[208,512]{1,0:T(8,128)(2,1)S(1)} copy-done((bf16[208,512]{1,0:T(8,128)(2,1)S(1)}, bf16[208,512]{1,0:T(8,128)(2,1)}, u32[]{:S(2)}) %copy-start.2) | copy-done | bytes 213016
  9.0 1.3 %collective-permute-start.2 = (bf16[208,512]{1,0:T(8,128)(2,1)S(1)}, bf16[208,512]{1,0:T(8,128)(2,1)S(1)}, u32[]{:S(2)}, u32[]{:S(2)}) collective-permute-start(bf16[208,512]{1,0:T(8,128)(2,1)S(1)} %shard_map.74.own_ref.refs_0_), channel_id=1, source_target_pairs={{0,2},{1,3},{2,0},{3,1},{4,6},{5,7},{6,4},{7,5},{8,10},{9,11},{10,... | collective-permute-start | bytes 638984 | tf_op jit(solution)/shard_map/ppermute | solution.py:204
  10.3 0.1 pad_add_fusion.1.pos_ref
  10.3 0.0 copy-start
  10.3 1.6 %copy-done = bf16[512,2048]{1,0:T(8,128)(2,1)S(1)} copy-done((bf16[512,2048]{1,0:T(8,128)(2,1)S(1)}, bf16[512,2048]{1,0:T(8,128)(2,1)}, u32[]{:S(2)}) %copy-start) | copy-done | bytes 2097176
  11.9 0.0 copy-start.5
  11.9 0.7 %copy-done.5 = f32[8,16]{1,0:T(8,128)S(1)} copy-done((f32[8,16]{1,0:T(8,128)S(1)}, f32[8,16]{1,0:T(8,128)}, u32[]{:S(2)}) %copy-start.5) | copy-done | bytes 536
  12.6 0.0 copy-start.1
  12.6 0.4 shard_map.75
  13.0 1.2 %copy-done.1 = bf16[512,2048]{1,0:T(8,128)(2,1)S(1)} copy-done((bf16[512,2048]{1,0:T(8,128)(2,1)S(1)}, bf16[512,2048]{1,0:T(8,128)(2,1)}, u32[]{:S(2)}) %copy-start.1) | copy-done | bytes 2097176
  14.2 2.4 %shard_map.76 = (f32[192,512]{1,0:T(8,128)S(1)}, f32[8,128]{1,0:T(8,128)S(1)}) custom-call(s32[4]{0:T(128)S(1)} %pad_add_fusion.2.pos_ref, bf16[192,512]{1,0:T(8,128)(2,1)S(1)} %get-tuple-element.22.q_ref, s32[192,128]{1,0:T(8,128)S(1)} %get-tuple-element.23.stamp_ref, bf16[208,512]{1,0:T(8,128)(2,1)S(1)} %shard_map.74.own_ref.refs_0_, ...), custom_call_target="tpu_custom_call" | custom-call | flops 1107296256 | bytes 1048576 | tf_op jit(solution)/shard_map/pallas_call | solution.py:276
  16.7 0.0 collective-permute-done.2.block_ref
  16.7 0.9 %collective-permute-start.3 = (bf16[208,512]{1,0:T(8,128)(2,1)S(1)}, bf16[208,512]{1,0:T(8,128)(2,1)S(1)}, u32[]{:S(2)}, u32[]{:S(2)}) collective-permute-start(bf16[208,512]{1,0:T(8,128)(2,1)S(1)} %shard_map.77.refs_0_.refs_2_), channel_id=1, source_target_pairs={{0,1},{1,0},{2,3},{3,2},{4,5},{5,4},{6,7},{7,6},{8,9},{9,8},{10,11... | collective-permute-start | bytes 638984 | tf_op jit(solution)/shard_map/ppermute | solution.py:204
  17.5 0.1 pad_add_fusion.4.pos_ref
  17.6 0.1 pad_add_fusion.3.pos_ref
  17.7 4.3 %collective-permute-done.6.refs_0_ = bf16[208,512]{1,0:T(8,128)(2,1)S(1)} collective-permute-done((bf16[208,512]{1,0:T(8,128)(2,1)}, bf16[208,512]{1,0:T(8,128)(2,1)S(1)}, u32[]{:S(2)}, u32[]{:S(2)}) %collective-permute-start.6) | collective-permute-done | bytes 213024 | tf_op jit(solution)/shard_map/ppermute | solution.py:207
  22.0 0.4 %collective-permute-start.7 = (bf16[208,512]{1,0:T(8,128)(2,1)S(1)}, bf16[208,512]{1,0:T(8,128)(2,1)S(1)}, u32[]{:S(2)}, u32[]{:S(2)}) collective-permute-start(bf16[208,512]{1,0:T(8,128)(2,1)S(1)} %collective-permute-done.6.refs_0_), channel_id=1, source_target_pairs={{0,1},{1,0},{2,3},{3,2},{4,5},{5,4},{6,7},{7,6},{8,9},{9,8},{10,11... | collective-permute-start | bytes 638984 | tf_op jit(solution)/shard_map/ppermute | solution.py:204
  22.4 1.2 %collective-permute-start.9 = (bf16[208,512]{1,0:T(8,128)(2,1)S(1)}, bf16[208,512]{1,0:T(8,128)(2,1)S(1)}, u32[]{:S(2)}, u32[]{:S(2)}) collective-permute-start(bf16[208,512]{1,0:T(8,128)(2,1)S(1)} %collective-permute-done.6.refs_0_), channel_id=1, source_target_pairs={{0,2},{1,3},{2,0},{3,1},{4,6},{5,7},{6,4},{7,5},{8,10},{9,11},{10,... | collective-permute-start | bytes 638984 | tf_op jit(solution)/shard_map/ppermute | solution.py:204
  23.7 0.0 collective-permute-done.3.refs_1_.refs_3_
  23.7 0.6 %shard_map.78 = (f32[192,512]{1,0:T(8,128)S(1)}, f32[8,128]{1,0:T(8,128)S(1)}) custom-call(s32[4]{0:T(128)S(1)} %pad_add_fusion.1.pos_ref, bf16[192,512]{1,0:T(8,128)(2,1)S(1)} %get-tuple-element.22.q_ref, s32[192,128]{1,0:T(8,128)S(1)} %get-tuple-element.23.stamp_ref, bf16[208,512]{1,0:T(8,128)(2,1)S(1)} %shard_map.77.refs_0_.refs_2_, ...), custom_call_target="tpu_custom_call" | custom-call | flops 1107296256 | bytes 1048576 | tf_op jit(solution)/shard_map/pallas_call | solution.py:276
  24.3 0.0 collective-permute-done.1.block_ref
  24.3 0.4 %collective-permute-start.5 = (bf16[208,512]{1,0:T(8,128)(2,1)S(1)}, bf16[208,512]{1,0:T(8,128)(2,1)S(1)}, u32[]{:S(2)}, u32[]{:S(2)}) collective-permute-start(bf16[208,512]{1,0:T(8,128)(2,1)S(1)} %shard_map.79.asked_ref.refs_0_), channel_id=1, source_target_pairs={{0,1},{1,0},{2,3},{3,2},{4,5},{5,4},{6,7},{7,6},{8,9},{9,8},{10,11... | collective-permute-start | bytes 638984 | tf_op jit(solution)/shard_map/ppermute | solution.py:204
  24.7 2.1 %collective-permute-start.4 = (bf16[208,512]{1,0:T(8,128)(2,1)S(1)}, bf16[208,512]{1,0:T(8,128)(2,1)S(1)}, u32[]{:S(2)}, u32[]{:S(2)}) collective-permute-start(bf16[208,512]{1,0:T(8,128)(2,1)S(1)} %shard_map.79.asked_ref.refs_0_), channel_id=1, source_target_pairs={{0,2},{1,3},{2,0},{3,1},{4,6},{5,7},{6,4},{7,5},{8,10},{9,11},{10,... | collective-permute-start | bytes 638984 | tf_op jit(solution)/shard_map/ppermute | solution.py:204
  26.8 0.5 %shard_map.80 = (bf16[192,512]{1,0:T(8,128)(2,1)S(1)}, f32[8,128]{1,0:T(8,128)S(1)}) custom-call(s32[6]{0:T(128)S(1)} %stack.155.pos_ref, bf16[208,512]{1,0:T(8,128)(2,1)S(1)} %shard_map.79.asked_ref.refs_0_, bf16[208,512]{1,0:T(8,128)(2,1)S(1)} %shard_map.74.own_ref.refs_0_, bf16[208,512]{1,0:T(8,128)(2,1)S(1)} %collective-permute-done.other_ref.refs_1_, ...), custom_call_target="tpu_custom_call" | custom-call | flops 2214592512 | bytes 1048576 | tf_op jit(solution)/shard_map/pallas_call | solution.py:304
  27.3 0.0 collective-permute-done.7.refs_1_
  27.4 2.5 %shard_map.81 = (f32[192,512]{1,0:T(8,128)S(1)}, f32[8,128]{1,0:T(8,128)S(1)}) custom-call(s32[4]{0:T(128)S(1)} %pad_add_fusion.4.pos_ref, bf16[192,512]{1,0:T(8,128)(2,1)S(1)} %get-tuple-element.22.q_ref, s32[192,128]{1,0:T(8,128)S(1)} %get-tuple-element.23.stamp_ref, bf16[208,512]{1,0:T(8,128)(2,1)S(1)} %collective-permute-done.6.refs_0_, ...), custom_call_target="tpu_custom_call" | custom-call | flops 1107296256 | bytes 1048576 | tf_op jit(solution)/shard_map/pallas_call | solution.py:276
  29.8 0.0 collective-permute-done.9.block_ref
  29.9 0.7 %collective-permute-start.10 = (bf16[208,512]{1,0:T(8,128)(2,1)S(1)}, bf16[208,512]{1,0:T(8,128)(2,1)S(1)}, u32[]{:S(2)}, u32[]{:S(2)}) collective-permute-start(bf16[208,512]{1,0:T(8,128)(2,1)S(1)} %shard_map.84.refs_0_), channel_id=1, source_target_pairs={{0,1},{1,0},{2,3},{3,2},{4,5},{5,4},{6,7},{7,6},{8,9},{9,8},{10,11... | collective-permute-start | bytes 638984 | tf_op jit(solution)/shard_map/ppermute | solution.py:204
  30.6 0.7 %collective-permute-start.11 = (bf16[192,512]{1,0:T(8,128)(2,1)S(1)}, bf16[192,512]{1,0:T(8,128)(2,1)S(1)}, u32[]{:S(2)}, u32[]{:S(2)}) collective-permute-start(bf16[192,512]{1,0:T(8,128)(2,1)S(1)} %get-tuple-element.37), channel_id=1, source_target_pairs={{0,12},{1,13},{2,14},{3,15},{16,28},{17,29},{18,30},{19,31}} | collective-permute-start | bytes 589832 | tf_op jit(solution)/shard_map/ppermute | solution.py:207
  31.2 0.0 collective-permute-done.5.refs_1_
  31.2 2.6 %shard_map.82 = (f32[192,512]{1,0:T(8,128)S(1)}, f32[8,128]{1,0:T(8,128)S(1)}) custom-call(s32[4]{0:T(128)S(1)} %pad_add_fusion.3.pos_ref, bf16[192,512]{1,0:T(8,128)(2,1)S(1)} %get-tuple-element.22.q_ref, s32[192,128]{1,0:T(8,128)S(1)} %get-tuple-element.23.stamp_ref, bf16[208,512]{1,0:T(8,128)(2,1)S(1)} %shard_map.79.asked_ref.refs_0_, ...), custom_call_target="tpu_custom_call" | custom-call | flops 1107296256 | bytes 1048576 | tf_op jit(solution)/shard_map/pallas_call | solution.py:276
  33.9 0.0 collective-permute-done.4.block_ref
  33.9 0.8 %collective-permute-start.8 = (bf16[208,512]{1,0:T(8,128)(2,1)S(1)}, bf16[208,512]{1,0:T(8,128)(2,1)S(1)}, u32[]{:S(2)}, u32[]{:S(2)}) collective-permute-start(bf16[208,512]{1,0:T(8,128)(2,1)S(1)} %shard_map.83.refs_0_), channel_id=1, source_target_pairs={{0,1},{1,0},{2,3},{3,2},{4,5},{5,4},{6,7},{7,6},{8,9},{9,8},{10,11... | collective-permute-start | bytes 638984 | tf_op jit(solution)/shard_map/ppermute | solution.py:204
  34.7 0.1 pad_add_fusion.5.pos_ref
  34.7 0.1 pad_add_fusion.pos_ref
  34.8 0.0 collective-permute-done.10.refs_1_
  34.8 2.4 %shard_map.85 = (f32[192,512]{1,0:T(8,128)S(1)}, f32[8,128]{1,0:T(8,128)S(1)}) custom-call(s32[4]{0:T(128)S(1)} %pad_add_fusion.5.pos_ref, bf16[192,512]{1,0:T(8,128)(2,1)S(1)} %get-tuple-element.22.q_ref, s32[192,128]{1,0:T(8,128)S(1)} %get-tuple-element.23.stamp_ref, bf16[208,512]{1,0:T(8,128)(2,1)S(1)} %shard_map.84.refs_0_, ...), custom_call_target="tpu_custom_call" | custom-call | flops 138412032 | bytes 131072 | tf_op jit(solution)/shard_map/pallas_call | solution.py:276
  37.3 0.0 copy-start.3
  37.3 0.0 copy-start.4
  37.3 0.0 copy-start.6
  37.3 0.0 collective-permute-done.8.refs_1_
  37.3 3.0 %shard_map.86 = (f32[192,512]{1,0:T(8,128)S(1)}, f32[8,128]{1,0:T(8,128)}) custom-call(s32[4]{0:T(128)S(1)} %pad_add_fusion.pos_ref, bf16[192,512]{1,0:T(8,128)(2,1)S(1)} %get-tuple-element.22.q_ref, s32[192,128]{1,0:T(8,128)S(1)} %get-tuple-element.23.stamp_ref, bf16[208,512]{1,0:T(8,128)(2,1)S(1)} %shard_map.83.refs_0_, ...), custom_call_target="tpu_custom_call" | custom-call | flops 138412032 | bytes 131072 | tf_op jit(solution)/shard_map/pallas_call | solution.py:276
  40.4 0.0 collective-permute-done.11.given_ref
  40.4 0.0 copy-done.3
  40.4 0.0 copy-done.4
  40.4 0.0 copy-done.6
  40.4 1.1 %shard_map.87 = bf16[192,512]{1,0:T(8,128)(2,1)} custom-call(f32[192,512]{1,0:T(8,128)S(1)} %get-tuple-element.36.sum_ref, bf16[192,512]{1,0:T(8,128)(2,1)S(1)} %collective-permute-done.11.given_ref, bf16[192,512]{1,0:T(8,128)(2,1)S(1)} %get-tuple-element.38.gate_ref, f32[1,512]{1,0:T(1,128)S(1)} %bitcast.28, bf16[512,512]{1,0:T(8,128)(2,1)S(1)} %copy-done.4, ...), custom_call_target="tpu_custom_call" | custom-call | tf_op jit(solution)/shard_map/pallas_call | solution.py:331
  (5 shorter events, 0.0 us)
Async XLA Ops:
  1.9 6.1 %collective-permute-start = (bf16[208,512]{1,0:T(8,128)(2,1)}, bf16[208,512]{1,0:T(8,128)(2,1)S(1)}, u32[]{:S(2)}, u32[]{:S(2)}) collective-permute-start(bf16[208,512]{1,0:T(8,128)(2,1)} %shard_map.73.own_ref), channel_id=1, source_target_pairs={{0,1},{1,0},{2,3},{3,2},{4,5},{5,4},{6,7},{7,6},{8,9},{9,8},{10,11... | collective-permute-start | bytes 638984 | tf_op jit(solution)/shard_map/ppermute | solution.py:204
  2.6 21.7 %collective-permute-start.1 = (bf16[208,512]{1,0:T(8,128)(2,1)}, bf16[208,512]{1,0:T(8,128)(2,1)S(1)}, u32[]{:S(2)}, u32[]{:S(2)}) collective-permute-start(bf16[208,512]{1,0:T(8,128)(2,1)} %shard_map.73.own_ref), channel_id=1, source_target_pairs={{0,8},{1,9},{2,10},{3,11},{4,12},{5,13},{6,14},{7,15},{12,0},{13,1... | collective-permute-start | bytes 638984 | tf_op jit(solution)/shard_map/ppermute | solution.py:207
  3.9 18.1 %collective-permute-start.6 = (bf16[208,512]{1,0:T(8,128)(2,1)}, bf16[208,512]{1,0:T(8,128)(2,1)S(1)}, u32[]{:S(2)}, u32[]{:S(2)}) collective-permute-start(bf16[208,512]{1,0:T(8,128)(2,1)} %shard_map.73.own_ref), channel_id=1, source_target_pairs={{0,4},{1,5},{2,6},{3,7},{4,8},{5,9},{6,10},{7,11},{8,12},{9,13},{1... | collective-permute-start | bytes 638984 | tf_op jit(solution)/shard_map/ppermute | solution.py:207
  8.0 0.9 %copy-start.2 = (bf16[208,512]{1,0:T(8,128)(2,1)S(1)}, bf16[208,512]{1,0:T(8,128)(2,1)}, u32[]{:S(2)}) copy-start(bf16[208,512]{1,0:T(8,128)(2,1)} %shard_map.73.own_ref) | copy-start | bytes 638980
  9.0 7.7 %collective-permute-start.2 = (bf16[208,512]{1,0:T(8,128)(2,1)S(1)}, bf16[208,512]{1,0:T(8,128)(2,1)S(1)}, u32[]{:S(2)}, u32[]{:S(2)}) collective-permute-start(bf16[208,512]{1,0:T(8,128)(2,1)S(1)} %shard_map.74.own_ref.refs_0_), channel_id=1, source_target_pairs={{0,2},{1,3},{2,0},{3,1},{4,6},{5,7},{6,4},{7,5},{8,10},{9,11},{10,... | collective-permute-start | bytes 638984 | tf_op jit(solution)/shard_map/ppermute | solution.py:204
  10.3 1.6 %copy-start = (bf16[512,2048]{1,0:T(8,128)(2,1)S(1)}, bf16[512,2048]{1,0:T(8,128)(2,1)}, u32[]{:S(2)}) copy-start(bf16[512,2048]{1,0:T(8,128)(2,1)} %refs_2_.11) | copy-start | bytes 6291460
  11.9 0.7 %copy-start.5 = (f32[8,16]{1,0:T(8,128)S(1)}, f32[8,16]{1,0:T(8,128)}, u32[]{:S(2)}) copy-start(f32[8,16]{1,0:T(8,128)} %bias_ref.1) | copy-start | bytes 1540
  12.6 1.6 %copy-start.1 = (bf16[512,2048]{1,0:T(8,128)(2,1)S(1)}, bf16[512,2048]{1,0:T(8,128)(2,1)}, u32[]{:S(2)}) copy-start(bf16[512,2048]{1,0:T(8,128)(2,1)} %refs_2_.11) | copy-start | bytes 6291460
  16.7 7.0 %collective-permute-start.3 = (bf16[208,512]{1,0:T(8,128)(2,1)S(1)}, bf16[208,512]{1,0:T(8,128)(2,1)S(1)}, u32[]{:S(2)}, u32[]{:S(2)}) collective-permute-start(bf16[208,512]{1,0:T(8,128)(2,1)S(1)} %shard_map.77.refs_0_.refs_2_), channel_id=1, source_target_pairs={{0,1},{1,0},{2,3},{3,2},{4,5},{5,4},{6,7},{7,6},{8,9},{9,8},{10,11... | collective-permute-start | bytes 638984 | tf_op jit(solution)/shard_map/ppermute | solution.py:204
  22.0 5.4 %collective-permute-start.7 = (bf16[208,512]{1,0:T(8,128)(2,1)S(1)}, bf16[208,512]{1,0:T(8,128)(2,1)S(1)}, u32[]{:S(2)}, u32[]{:S(2)}) collective-permute-start(bf16[208,512]{1,0:T(8,128)(2,1)S(1)} %collective-permute-done.6.refs_0_), channel_id=1, source_target_pairs={{0,1},{1,0},{2,3},{3,2},{4,5},{5,4},{6,7},{7,6},{8,9},{9,8},{10,11... | collective-permute-start | bytes 638984 | tf_op jit(solution)/shard_map/ppermute | solution.py:204
  22.4 7.4 %collective-permute-start.9 = (bf16[208,512]{1,0:T(8,128)(2,1)S(1)}, bf16[208,512]{1,0:T(8,128)(2,1)S(1)}, u32[]{:S(2)}, u32[]{:S(2)}) collective-permute-start(bf16[208,512]{1,0:T(8,128)(2,1)S(1)} %collective-permute-done.6.refs_0_), channel_id=1, source_target_pairs={{0,2},{1,3},{2,0},{3,1},{4,6},{5,7},{6,4},{7,5},{8,10},{9,11},{10,... | collective-permute-start | bytes 638984 | tf_op jit(solution)/shard_map/ppermute | solution.py:204
  24.3 7.0 %collective-permute-start.5 = (bf16[208,512]{1,0:T(8,128)(2,1)S(1)}, bf16[208,512]{1,0:T(8,128)(2,1)S(1)}, u32[]{:S(2)}, u32[]{:S(2)}) collective-permute-start(bf16[208,512]{1,0:T(8,128)(2,1)S(1)} %shard_map.79.asked_ref.refs_0_), channel_id=1, source_target_pairs={{0,1},{1,0},{2,3},{3,2},{4,5},{5,4},{6,7},{7,6},{8,9},{9,8},{10,11... | collective-permute-start | bytes 638984 | tf_op jit(solution)/shard_map/ppermute | solution.py:204
  24.7 9.2 %collective-permute-start.4 = (bf16[208,512]{1,0:T(8,128)(2,1)S(1)}, bf16[208,512]{1,0:T(8,128)(2,1)S(1)}, u32[]{:S(2)}, u32[]{:S(2)}) collective-permute-start(bf16[208,512]{1,0:T(8,128)(2,1)S(1)} %shard_map.79.asked_ref.refs_0_), channel_id=1, source_target_pairs={{0,2},{1,3},{2,0},{3,1},{4,6},{5,7},{6,4},{7,5},{8,10},{9,11},{10,... | collective-permute-start | bytes 638984 | tf_op jit(solution)/shard_map/ppermute | solution.py:204
  29.9 5.0 %collective-permute-start.10 = (bf16[208,512]{1,0:T(8,128)(2,1)S(1)}, bf16[208,512]{1,0:T(8,128)(2,1)S(1)}, u32[]{:S(2)}, u32[]{:S(2)}) collective-permute-start(bf16[208,512]{1,0:T(8,128)(2,1)S(1)} %shard_map.84.refs_0_), channel_id=1, source_target_pairs={{0,1},{1,0},{2,3},{3,2},{4,5},{5,4},{6,7},{7,6},{8,9},{9,8},{10,11... | collective-permute-start | bytes 638984 | tf_op jit(solution)/shard_map/ppermute | solution.py:204
  30.6 9.8 %collective-permute-start.11 = (bf16[192,512]{1,0:T(8,128)(2,1)S(1)}, bf16[192,512]{1,0:T(8,128)(2,1)S(1)}, u32[]{:S(2)}, u32[]{:S(2)}) collective-permute-start(bf16[192,512]{1,0:T(8,128)(2,1)S(1)} %get-tuple-element.37), channel_id=1, source_target_pairs={{0,12},{1,13},{2,14},{3,15},{16,28},{17,29},{18,30},{19,31}} | collective-permute-start | bytes 589832 | tf_op jit(solution)/shard_map/ppermute | solution.py:207
  33.9 3.4 %collective-permute-start.8 = (bf16[208,512]{1,0:T(8,128)(2,1)S(1)}, bf16[208,512]{1,0:T(8,128)(2,1)S(1)}, u32[]{:S(2)}, u32[]{:S(2)}) collective-permute-start(bf16[208,512]{1,0:T(8,128)(2,1)S(1)} %shard_map.83.refs_0_), channel_id=1, source_target_pairs={{0,1},{1,0},{2,3},{3,2},{4,5},{5,4},{6,7},{7,6},{8,9},{9,8},{10,11... | collective-permute-start | bytes 638984 | tf_op jit(solution)/shard_map/ppermute | solution.py:204
  37.3 3.1 %copy-start.3 = (bf16[192,512]{1,0:T(8,128)(2,1)S(1)}, bf16[192,512]{1,0:T(8,128)(2,1)}, u32[]{:S(2)}) copy-start(bf16[192,512]{1,0:T(8,128)(2,1)} %tokens_ref.1) | copy-start | bytes 589828
  37.3 3.1 %copy-start.4 = (bf16[512,512]{1,0:T(8,128)(2,1)S(1)}, bf16[512,512]{1,0:T(8,128)(2,1)}, u32[]{:S(2)}) copy-start(bf16[512,512]{1,0:T(8,128)(2,1)} %wo_ref.1) | copy-start | bytes 1572868
  37.3 3.1 %copy-start.6 = (f32[512]{0:T(512)S(1)}, f32[512]{0:T(512)}, u32[]{:S(2)}) copy-start(f32[512]{0:T(512)} %param.12) | copy-start | bytes 6148

commit v3 on v2

v3 whole, which is shorter than its diff:
```python
import functools

import jax
import jax.numpy as jnp
from jax import lax
from jax.experimental import pallas as pl
from jax.experimental.pallas import tpu as pltpu
from jax.sharding import PartitionSpec as P

HEADS = 8
BUCKETS = 16
EPSILON = 1e-05
LANES = 128
TAIL = 16
COST = (4, 16, 16, 32, 32, 1, 0)
FIXED = 15
BF16 = jnp.bfloat16
F32 = jnp.float32
I32 = jnp.int32
VMEM = pl.BlockSpec(memory_space=pltpu.VMEM)
SMEM = pl.BlockSpec(memory_space=pltpu.SMEM)
HBM = pl.BlockSpec(memory_space=pltpu.HBM)
VMEM_LIMIT = 12 << 20


def layer_norm(values, gain):
    centered = values - jnp.mean(values, axis=-1, keepdims=True)
    spread = jnp.mean(centered * centered, axis=-1, keepdims=True)
    return centered * lax.rsqrt(spread + EPSILON) * gain


def norm_kernel(tokens_hbm, stamps_hbm, gain_hbm, out_ref, tokens_ref, stamps_ref, gain_ref, sems):
    copies = [
        pltpu.make_async_copy(src, dst, sems.at[i])
        for i, (src, dst) in enumerate(
            ((tokens_hbm, tokens_ref), (stamps_hbm, stamps_ref), (gain_hbm, gain_ref))
        )
    ]
    for copy in copies:
        copy.start()
    for copy in copies:
        copy.wait()
    rows, width = tokens_ref.shape
    out_ref[:rows, :] = layer_norm(tokens_ref[...].astype(F32), gain_ref[...]).astype(BF16)
    stamps = jnp.broadcast_to(stamps_ref[...], (TAIL, rows))
    byte = lax.broadcasted_iota(I32, (TAIL, rows), 0)
    part = jnp.where(byte < 4, lax.shift_right_logical(stamps, 8 * jnp.minimum(byte, 3)) & 255, 0)
    out_ref[rows:, :] = jnp.zeros((TAIL, width), BF16)
    out_ref[rows:, :rows] = part.astype(F32).astype(BF16)


def stamps_of(block):
    rows = block.shape[0] - TAIL
    part = block[rows:, :rows].astype(F32).astype(I32)
    return part[0:1] + part[1:2] * 256 + part[2:3] * 65536 + part[3:4] * 16777216


def down_rows(stamps):
    rows = stamps.shape[1]
    pad = -rows % LANES
    stamps = jnp.concatenate([stamps, jnp.zeros((1, pad), I32)], axis=1)
    return jnp.broadcast_to(stamps, (LANES, rows + pad)).T[:rows, :]


def queries_of(normed, weight):
    width = normed.shape[1]
    scale = 0.5 * (width // HEADS) ** -0.5
    queries = jnp.dot(normed, weight, preferred_element_type=F32)
    return (queries.astype(BF16).astype(F32) * scale).astype(BF16)


def relay_kernel(own_ref, other_ref, out_ref):
    del other_ref
    out_ref[...] = own_ref[...]


def front_kernel(own_ref, w_ref, bias_ref, q_ref, gate_ref, stamp_ref, table_ref):
    rows, width = q_ref.shape
    stamp_ref[...] = down_rows(stamps_of(own_ref))
    normed = own_ref[:rows, :]
    gate = jnp.dot(normed, w_ref[:, :width], preferred_element_type=F32)
    gate_ref[...] = (gate / (1 + jnp.exp(-gate))).astype(BF16)
    q_ref[...] = queries_of(normed, w_ref[:, width : 2 * width])
    heads, buckets = bias_ref.shape
    bias = jnp.concatenate([bias_ref[...], jnp.zeros((heads, LANES - buckets), F32)], axis=1)
    lane = lax.broadcasted_iota(I32, (heads, LANES), 1)
    bucket = jnp.clip(lax.shift_right_logical(33 - jnp.minimum(lane, 32), 1), 0, buckets - 1)
    half = 0.5 * jnp.take_along_axis(bias, bucket, axis=1)
    for p in range(heads // 2):
        low = jnp.floor(half[2 * p + 1 : 2 * p + 2] * 2.0**FIXED + 0.5)
        high = jnp.floor(half[2 * p : 2 * p + 1] * 2.0**FIXED - low * 2.0**-16 + 0.5)
        table_ref[p : p + 1, :] = high.astype(I32) * 65536 + low.astype(I32)


def add_blocks(q_ref, stamp_ref, blocks, w_ref, table_ref, acc_ref, out_ref, hide=None, more_ref=None):
    rows, width = q_ref.shape
    size = width // HEADS
    keys = len(blocks) * rows
    normed = jnp.concatenate([b[:rows, :] for b in blocks], axis=0)
    key_rows = jnp.dot(
        normed, w_ref[:, 2 * width : 3 * width], preferred_element_type=F32
    ).astype(BF16)
    value_rows = jnp.dot(normed, w_ref[:, 3 * width :], preferred_element_type=F32).astype(BF16)
    stamps = jnp.concatenate([stamps_of(b) for b in blocks], axis=1)
    cuts = [slice(j * LANES, (j + 1) * LANES) for j in range(keys // LANES)]
    index = [lax.clz(stamp_ref[...] - stamps[:, cut]) for cut in cuts]
    head = lax.broadcasted_iota(I32, (1, LANES), 1) // size
    zero = jnp.zeros((), BF16)
    for p in range(HEADS // 2):
        pair = slice(p * LANES, (p + 1) * LANES)
        both = jnp.concatenate(
            [jnp.where(head == h, key_rows[:, pair], zero) for h in (0, 1)], axis=0
        )
        score = lax.dot_general(
            q_ref[:, pair], both, (((1,), (1,)), ((), ())), preferred_element_type=F32
        )
        table = jnp.broadcast_to(table_ref[p : p + 1, :], (rows, LANES))
        words = [jnp.take_along_axis(table, i, axis=1) for i in index]
        weight = []
        for h in (0, 1):
            for j, word in enumerate(words):
                code = lax.shift_left(word, 16) if h else word
                at = h * keys + j * LANES
                half = score[:, at : at + LANES] + code.astype(F32) * 2.0 ** (-16 - FIXED)
                if hide is not None:
                    half = half + hide[j]
                weight.append((half * jnp.tanh(half) + half).astype(BF16))
        values = jnp.concatenate(
            [jnp.where(head == h, value_rows[:, pair], zero) for h in (0, 1)], axis=0
        )
        mixed = jnp.dot(
            jnp.concatenate(weight, axis=1), values, preferred_element_type=F32
        )
        if acc_ref is not None:
            mixed = acc_ref[:, pair] + mixed
        if more_ref is not None:
            mixed = more_ref[:, pair].astype(F32) + mixed
        out_ref[:, pair] = mixed.astype(out_ref.dtype)


def place(near):
    me = lax.axis_index("pb")
    return me // near, me % near


def own_kernel(q_ref, stamp_ref, own_ref, other_ref, w_ref, table_ref, out_ref, tick_ref):
    rows = q_ref.shape[0]
    core = lax.axis_index("pb") % 2
    col = lax.broadcasted_iota(I32, (1, 2 * rows), 1)
    key = jnp.where(col < rows, core * rows + col, (1 - core) * rows + col - rows)
    query = core * rows + lax.broadcasted_iota(I32, (rows, LANES), 0)
    hide = [
        jnp.where(key[:, at : at + LANES] <= query, 0.0, -1e30)
        for at in range(0, 2 * rows, LANES)
    ]
    blocks = (own_ref, other_ref)
    add_blocks(q_ref, stamp_ref, blocks, w_ref, table_ref, None, out_ref, hide)
    tick_ref[...] = jnp.zeros_like(tick_ref)


def attend_kernel(near, step, given, tell, q_ref, stamp_ref, *refs):
    blocks = refs[:2]
    w_ref, table_ref, acc_ref = refs[2:5]
    out_ref = refs[-2] if tell else refs[-1]
    more_ref = refs[5] if given else None
    level, spot = place(near)
    seen = level >= step if step else spot >= near // 2

    @pl.when(seen)
    def _():
        add_blocks(
            q_ref, stamp_ref, blocks, w_ref, table_ref, acc_ref, out_ref, more_ref=more_ref
        )

    @pl.when(jnp.logical_not(seen))
    def _():
        kept = acc_ref[...]
        out_ref[...] = kept + more_ref[...].astype(F32) if given else kept

    if tell:
        refs[-1][...] = jnp.zeros_like(refs[-1])


def return_kernel(near, asked_ref, *refs):
    blocks = refs[:near]
    w_ref, table_ref, out_ref, tick_ref, q_ref, stamp_ref = refs[near:]
    tick_ref[...] = jnp.zeros_like(tick_ref)

    @pl.when(place(near)[0] == 0)
    def _():
        rows, width = out_ref.shape
        q_ref[...] = queries_of(asked_ref[:rows, :], w_ref[:, width : 2 * width])
        stamp_ref[...] = down_rows(stamps_of(asked_ref))
        add_blocks(q_ref, stamp_ref, blocks, w_ref, table_ref, None, out_ref)


def last_kernel(near, steps, q_ref, stamp_ref, *refs):
    count = 2 * len(steps)
    blocks = refs[:count]
    w_ref, table_ref, acc_ref, gate_ref, gain_ref, wo_ref, tokens_ref = refs[count:-2]
    out_ref, sum_ref = refs[-2:]
    level = place(near)[0]
    for i in range(len(steps) + 1):
        low = level >= steps[i - 1] if i else True
        high = level < steps[i] if i < len(steps) else True

        @pl.when(jnp.logical_and(low, high))
        def _(i=i):
            if i == 0:
                sum_ref[...] = acc_ref[...]
            else:
                seen = blocks[: 2 * i]
                add_blocks(q_ref, stamp_ref, seen, w_ref, table_ref, acc_ref, sum_ref)

    gated = layer_norm(sum_ref[...], gain_ref[...]) * gate_ref[...].astype(F32)
    mixed = jnp.dot(gated.astype(BF16), wo_ref[...], preferred_element_type=F32)
    out_ref[...] = (tokens_ref[...].astype(F32) + mixed).astype(BF16)


def pin_kernel(block_ref, tick_ref, out_ref):
    del block_ref, tick_ref, out_ref


def pin(block, tick):
    return pl.pallas_call(
        pin_kernel,
        out_shape=jax.ShapeDtypeStruct(block.shape, block.dtype),
        in_specs=[pl.BlockSpec(memory_space=pl.ANY)] * 2,
        out_specs=pl.BlockSpec(memory_space=pl.ANY),
        input_output_aliases={0: 0},
        compiler_params=pltpu.CompilerParams(vmem_limit_bytes=1 << 20),
    )(block, tick)


def body(shards, tokens, stamps, norm_gain, w_proj, rel_bias, attn_gain, w_out):
    rows, width = tokens.shape
    near = 4
    levels = shards // near

    def swap(block, bit):
        return lax.ppermute(block, "pb", [(i, i ^ bit) for i in range(shards)])

    def hop(block, pairs):
        return lax.ppermute(
            block, "pb", [(a * near + i, b * near + i) for a, b in pairs for i in range(near)]
        )

    own = pl.pallas_call(
        norm_kernel,
        out_shape=jax.ShapeDtypeStruct((rows + TAIL, width), BF16),
        in_specs=[HBM] * 3,
        out_specs=VMEM,
        scratch_shapes=[
            pltpu.VMEM((rows, width), BF16),
            pltpu.VMEM((1, rows), I32),
            pltpu.VMEM((1, width), F32),
            pltpu.SemaphoreType.DMA((3,)),
        ],
        compiler_params=pltpu.CompilerParams(vmem_limit_bytes=56 << 20),
    )(tokens, stamps.reshape(1, rows), norm_gain.reshape(1, width))

    far = {}
    for step in range(levels - 2, 0, -1):
        pairs = [(z, z + step) for z in range(levels - step)]
        if step == levels - 2:
            pairs.append((levels - 1, 0))
        far[step] = hop(own, pairs)
    by_core = swap(own, 1)
    own = pl.pallas_call(
        relay_kernel,
        out_shape=jax.ShapeDtypeStruct(own.shape, BF16),
        in_specs=[VMEM] * 2,
        out_specs=VMEM,
        compiler_params=pltpu.CompilerParams(vmem_limit_bytes=2 << 20),
        cost_estimate=pl.CostEstimate(
            flops=COST[6] * rows * width * width, bytes_accessed=0, transcendentals=0
        ),
    )(own, by_core)
    by_y = swap(own, 2)
    queries, gate, stamp_rows, table = pl.pallas_call(
        front_kernel,
        out_shape=(
            jax.ShapeDtypeStruct((rows, width), BF16),
            jax.ShapeDtypeStruct((rows, width), BF16),
            jax.ShapeDtypeStruct((rows, LANES), I32),
            jax.ShapeDtypeStruct((rel_bias.shape[0] // 2, LANES), I32),
        ),
        in_specs=[VMEM] * 3,
        out_specs=(VMEM,) * 4,
        compiler_params=pltpu.CompilerParams(vmem_limit_bytes=VMEM_LIMIT),
        cost_estimate=pl.CostEstimate(
            flops=4 * COST[0] * rows * width * width, bytes_accessed=0, transcendentals=0
        ),
    )(own, w_proj, rel_bias)

    tick_shape = jax.ShapeDtypeStruct((8, LANES), F32)
    params = pltpu.CompilerParams(vmem_limit_bytes=VMEM_LIMIT)

    def attend(step, blocks, total, *more, weight, given=False, tell=True):
        flops = weight * 2 * rows * width * (width + rows)
        args = [queries, stamp_rows, *blocks, w_proj, table]
        args += [] if total is None else [total]
        args += more
        return pl.pallas_call(
            own_kernel
            if total is None
            else functools.partial(attend_kernel, near, step, given, tell),
            out_shape=(jax.ShapeDtypeStruct((rows, width), F32), tick_shape)[: 1 + tell],
            in_specs=[VMEM] * len(args),
            out_specs=(VMEM, VMEM)[: 1 + tell],
            compiler_params=params,
            cost_estimate=pl.CostEstimate(
                flops=flops, bytes_accessed=0, transcendentals=0
            ),
        )(*args)

    total, tick = attend(0, [own, by_core], None, weight=COST[1])
    began = tick
    by_y = pin(by_y, tick)
    by_both = swap(by_y, 1)
    (total,) = attend(0, [by_y, by_both], total, weight=COST[2], tell=False)
    across = {}
    for step in sorted(far):
        block = pin(far[step], began) if step == levels - 2 else far[step]
        across[step] = swap(block, 2)
        far[step] = [block, swap(block, 1)]
    returned, tick = pl.pallas_call(
        functools.partial(return_kernel, near),
        out_shape=(jax.ShapeDtypeStruct((rows, width), BF16), tick_shape),
        in_specs=[VMEM] * (near + 3),
        out_specs=(VMEM, VMEM),
        scratch_shapes=[pltpu.VMEM((rows, width), BF16), pltpu.VMEM((rows, LANES), I32)],
        compiler_params=params,
        cost_estimate=pl.CostEstimate(
            flops=COST[3] * rows * width * (width + rows), bytes_accessed=0, transcendentals=0
        ),
    )(far[levels - 2][0], own, by_core, by_y, by_both, w_proj, table)
    given = hop(returned, [(0, levels - 1)])
    steps = sorted(far)
    for step in steps:
        extra = (given,) if step == steps[-1] else (tick,)
        total, done = attend(
            step, far[step], total, *extra, weight=COST[4], given=step == steps[-1]
        )
        tick = done if step == steps[0] else tick
    sets = {}
    for step in steps:
        block = pin(across[step], tick)
        sets[step] = [block, swap(block, 1)]
    for step in steps[:-2]:
        (total,) = attend(step, sets[step], total, weight=COST[5], tell=False)
    blocks = [block for step in steps[-2:] for block in sets[step]]
    args = [queries, stamp_rows, *blocks, w_proj, table, total, gate]
    args += [attn_gain.reshape(1, width), w_out, tokens]
    return pl.pallas_call(
        functools.partial(last_kernel, near, steps[-2:]),
        out_shape=jax.ShapeDtypeStruct((rows, width), BF16),
        in_specs=[VMEM] * len(args),
        out_specs=VMEM,
        scratch_shapes=[pltpu.VMEM((rows, width), F32)],
        compiler_params=params,
    )(*args)


def solution(mesh):
    return jax.shard_map(
        functools.partial(body, mesh.shape["pb"]),
        mesh=mesh,
        in_specs=(P(("groups", "pb"), None), P(("groups", "pb")), P(), P(), P(), P(), P()),
        out_specs=P(("groups", "pb"), None),
        check_vma=False,
    )
```

time: 41.8 us -> 36.6 us (0.88)
  the two profiles are of different devices: /device:TPU:19 before, /device:TPU:31 now
where the time goes in v3:
time: 36.6 us; the launch traced here: 36.1 us
  Pallas kernels  12.9 us (35%)
  starting transfers between devices  10.8 us (30%)
  waiting for transfers between devices  7.85 us (21%)
  local copies, waits for them, and re-layouts  4.41 us (12%)
    pallas_call x4, Pallas kernels, attend(): pl.pallas_call(own_kernel if total is None else functools.partial(attend_...  6.8 us
    ppermute x9, starting transfers between devices, swap(): return lax.ppermute(block, 'pb', [(i, i ^ bit) for i in range(shards)])  6.31 us
    ppermute x9, waiting for transfers between devices, swap(): return lax.ppermute(block, 'pb', [(i, i ^ bit) for i in range(shards)])  5.05 us
    ppermute x3, starting transfers between devices, hop(): lax.ppermute(block, 'pb', [(a * near + i, b * near + i) for a, b in pairs...  4.48 us
    unnamed x14, local copies, waits for them, and re-layouts  4.41 us
    pallas_call x1, Pallas kernels, body(): pl.pallas_call(functools.partial(last_kernel, near, steps[-2:]), out_shap...  3.84 us
    ppermute x3, waiting for transfers between devices, hop(): lax.ppermute(block, 'pb', [(a * near + i, b * near + i) for a, b in pairs...  2.81 us
    pallas_call x1, Pallas kernels, body(): pl.pallas_call(norm_kernel, out_shape=jax.ShapeDtypeStruct((rows + TAIL,...  1.86 us
  transfers between devices with their start and end apart: 12, of which 4 were waited for; matrix products, arithmetic and copies ran while one was open for 0% of the time, Pallas kernels for 20%

profile of v3, /device:TPU:31, one launch (start us, length us, event | category | flops | bytes accessed | tf_op | source)
XLA Modules:
  0.0 36.1 jit_solution(6274691945434809706)
XLA Ops:
  0.0 1.9 %shard_map.73.own_ref = bf16[208,512]{1,0:T(8,128)(2,1)} custom-call(bf16[192,512]{1,0:T(8,128)(2,1)} %refs_10_.1, s32[1,192]{1,0:T(1,128)} %bitcast.5, f32[1,512]{1,0:T(1,128)} %bitcast.4), custom_call_target="tpu_custom_call" | custom-call | tf_op jit(solution)/shard_map/pallas_call | solution.py:248
  1.9 0.7 %collective-permute-start = (bf16[208,512]{1,0:T(8,128)(2,1)}, bf16[208,512]{1,0:T(8,128)(2,1)S(1)}, u32[]{:S(2)}, u32[]{:S(2)}) collective-permute-start(bf16[208,512]{1,0:T(8,128)(2,1)} %shard_map.73.own_ref), channel_id=1, source_target_pairs={{0,1},{1,0},{2,3},{3,2},{4,5},{5,4},{6,7},{7,6},{8,9},{9,8},{10,11... | collective-permute-start | bytes 638984 | tf_op jit(solution)/shard_map/ppermute | solution.py:241
  2.6 1.9 %collective-permute-start.6 = (bf16[208,512]{1,0:T(8,128)(2,1)}, bf16[208,512]{1,0:T(8,128)(2,1)S(1)}, u32[]{:S(2)}, u32[]{:S(2)}) collective-permute-start(bf16[208,512]{1,0:T(8,128)(2,1)} %shard_map.73.own_ref), channel_id=1, source_target_pairs={{0,8},{1,9},{2,10},{3,11},{4,12},{5,13},{6,14},{7,15},{12,0},{13,1... | collective-permute-start | bytes 638984 | tf_op jit(solution)/shard_map/ppermute | solution.py:244
  4.5 1.3 %collective-permute-start.1 = (bf16[208,512]{1,0:T(8,128)(2,1)}, bf16[208,512]{1,0:T(8,128)(2,1)S(1)}, u32[]{:S(2)}, u32[]{:S(2)}) collective-permute-start(bf16[208,512]{1,0:T(8,128)(2,1)} %shard_map.73.own_ref), channel_id=1, source_target_pairs={{0,4},{1,5},{2,6},{3,7},{4,8},{5,9},{6,10},{7,11},{8,12},{9,13},{1... | collective-permute-start | bytes 638984 | tf_op jit(solution)/shard_map/ppermute | solution.py:244
  5.8 0.0 collective-permute-done.other_ref.refs_1_
  5.8 0.0 copy-start.2
  5.8 0.9 %copy-done.2 = bf16[208,512]{1,0:T(8,128)(2,1)S(1)} copy-done((bf16[208,512]{1,0:T(8,128)(2,1)S(1)}, bf16[208,512]{1,0:T(8,128)(2,1)}, u32[]{:S(2)}) %copy-start.2) | copy-done | bytes 213016
  6.8 0.3 collective-permute-start.4
  7.1 0.0 copy-start
  7.1 1.6 %copy-done = bf16[512,2048]{1,0:T(8,128)(2,1)S(1)} copy-done((bf16[512,2048]{1,0:T(8,128)(2,1)S(1)}, bf16[512,2048]{1,0:T(8,128)(2,1)}, u32[]{:S(2)}) %copy-start) | copy-done | bytes 2097176
  8.7 0.0 copy-start.6
  8.7 0.7 %copy-done.6 = f32[8,16]{1,0:T(8,128)S(1)} copy-done((f32[8,16]{1,0:T(8,128)S(1)}, f32[8,16]{1,0:T(8,128)}, u32[]{:S(2)}) %copy-start.6) | copy-done | bytes 536
  9.4 0.0 copy-start.1
  9.4 0.4 %shard_map.75 = (bf16[192,512]{1,0:T(8,128)(2,1)S(1)}, bf16[192,512]{1,0:T(8,128)(2,1)S(1)}, s32[192,128]{1,0:T(8,128)S(1)}, s32[4,128]{1,0:T(4,128)S(1)}) custom-call(bf16[208,512]{1,0:T(8,128)(2,1)S(1)} %shard_map.74.own_ref.refs_0_, bf16[512,2048]{1,0:T(8,128)(2,1)S(1)} %copy-done, f32[8,16]{1,0:T(8,128)S(1)} %copy-done.6), custom_call_target="tpu_custom_call" | custom-call | flops 805306368 | tf_op jit(solution)/shard_map/pallas_call | solution.py:280
  9.8 1.2 %copy-done.1 = bf16[512,2048]{1,0:T(8,128)(2,1)S(1)} copy-done((bf16[512,2048]{1,0:T(8,128)(2,1)S(1)}, bf16[512,2048]{1,0:T(8,128)(2,1)}, u32[]{:S(2)}) %copy-start.1) | copy-done | bytes 2097176
  11.0 1.6 %shard_map.76 = (f32[192,512]{1,0:T(8,128)S(1)}, f32[8,128]{1,0:T(8,128)S(1)}) custom-call(bf16[192,512]{1,0:T(8,128)(2,1)S(1)} %get-tuple-element.16.q_ref, s32[192,128]{1,0:T(8,128)S(1)} %get-tuple-element.17.stamp_ref, bf16[208,512]{1,0:T(8,128)(2,1)S(1)} %shard_map.74.own_ref.refs_0_, bf16[208,512]{1,0:T(8,128)(2,1)S(1)} %collective-permute-done.other_ref.refs_1_, ...), custom_call_target="tpu_custom_call" | custom-call | flops 2214592512 | tf_op jit(solution)/shard_map/pallas_call | solution.py:304
  12.5 0.9 %collective-permute-done.4.block_ref = bf16[208,512]{1,0:T(8,128)(2,1)S(1)} collective-permute-done((bf16[208,512]{1,0:T(8,128)(2,1)S(1)}, bf16[208,512]{1,0:T(8,128)(2,1)S(1)}, u32[]{:S(2)}, u32[]{:S(2)}) %collective-permute-start.4) | collective-permute-done | bytes 213024 | tf_op jit(solution)/shard_map/ppermute | solution.py:241
  13.5 1.0 %collective-permute-start.5 = (bf16[208,512]{1,0:T(8,128)(2,1)S(1)}, bf16[208,512]{1,0:T(8,128)(2,1)S(1)}, u32[]{:S(2)}, u32[]{:S(2)}) collective-permute-start(bf16[208,512]{1,0:T(8,128)(2,1)S(1)} %shard_map.77.refs_0_.refs_2_), channel_id=1, source_target_pairs={{0,1},{1,0},{2,3},{3,2},{4,5},{5,4},{6,7},{7,6},{8,9},{9,8},{10,11... | collective-permute-start | bytes 638984 | tf_op jit(solution)/shard_map/ppermute | solution.py:241
  14.5 2.8 %collective-permute-done.6.block_ref = bf16[208,512]{1,0:T(8,128)(2,1)S(1)} collective-permute-done((bf16[208,512]{1,0:T(8,128)(2,1)}, bf16[208,512]{1,0:T(8,128)(2,1)S(1)}, u32[]{:S(2)}, u32[]{:S(2)}) %collective-permute-start.6) | collective-permute-done | bytes 213024 | tf_op jit(solution)/shard_map/ppermute | solution.py:244
  17.3 0.5 %collective-permute-start.10 = (bf16[208,512]{1,0:T(8,128)(2,1)S(1)}, bf16[208,512]{1,0:T(8,128)(2,1)S(1)}, u32[]{:S(2)}, u32[]{:S(2)}) collective-permute-start(bf16[208,512]{1,0:T(8,128)(2,1)S(1)} %shard_map.79.asked_ref.refs_0_), channel_id=1, source_target_pairs={{0,1},{1,0},{2,3},{3,2},{4,5},{5,4},{6,7},{7,6},{8,9},{9,8},{10,11... | collective-permute-start | bytes 638984 | tf_op jit(solution)/shard_map/ppermute | solution.py:241
  17.8 0.2 collective-permute-start.8
  18.1 0.0 collective-permute-done.1.refs_0_
  18.1 0.7 %collective-permute-start.3 = (bf16[208,512]{1,0:T(8,128)(2,1)S(1)}, bf16[208,512]{1,0:T(8,128)(2,1)S(1)}, u32[]{:S(2)}, u32[]{:S(2)}) collective-permute-start(bf16[208,512]{1,0:T(8,128)(2,1)S(1)} %collective-permute-done.1.refs_0_), channel_id=1, source_target_pairs={{0,1},{1,0},{2,3},{3,2},{4,5},{5,4},{6,7},{7,6},{8,9},{9,8},{10,11... | collective-permute-start | bytes 638984 | tf_op jit(solution)/shard_map/ppermute | solution.py:241
  18.8 0.8 %collective-permute-start.2 = (bf16[208,512]{1,0:T(8,128)(2,1)S(1)}, bf16[208,512]{1,0:T(8,128)(2,1)S(1)}, u32[]{:S(2)}, u32[]{:S(2)}) collective-permute-start(bf16[208,512]{1,0:T(8,128)(2,1)S(1)} %collective-permute-done.1.refs_0_), channel_id=1, source_target_pairs={{0,2},{1,3},{2,0},{3,1},{4,6},{5,7},{6,4},{7,5},{8,10},{9,11},{10,... | collective-permute-start | bytes 638984 | tf_op jit(solution)/shard_map/ppermute | solution.py:241
  19.6 0.0 collective-permute-done.5.refs_1_.refs_3_
  19.6 1.3 %collective-permute-start.11 = (bf16[192,512]{1,0:T(8,128)(2,1)S(1)}, bf16[192,512]{1,0:T(8,128)(2,1)S(1)}, u32[]{:S(2)}, u32[]{:S(2)}) collective-permute-start(bf16[192,512]{1,0:T(8,128)(2,1)S(1)} %get-tuple-element.24), channel_id=1, source_target_pairs={{0,12},{1,13},{2,14},{3,15},{16,28},{17,29},{18,30},{19,31}} | collective-permute-start | bytes 589832 | tf_op jit(solution)/shard_map/ppermute | solution.py:244
  20.9 1.5 %shard_map.78.refs_4_ = f32[192,512]{1,0:T(8,128)S(1)} custom-call(bf16[192,512]{1,0:T(8,128)(2,1)S(1)} %get-tuple-element.16.q_ref, s32[192,128]{1,0:T(8,128)S(1)} %get-tuple-element.17.stamp_ref, bf16[208,512]{1,0:T(8,128)(2,1)S(1)} %shard_map.77.refs_0_.refs_2_, bf16[208,512]{1,0:T(8,128)(2,1)S(1)} %collective-permute-done.5.refs_1_.refs_3_, ...), custom_call_target="tpu_custom_call" | custom-call | flops 2214592512 | tf_op jit(solution)/shard_map/pallas_call | solution.py:304
  22.4 0.0 collective-permute-done.3.refs_1_
  22.4 1.5 %shard_map.81 = (f32[192,512]{1,0:T(8,128)S(1)}, f32[8,128]{1,0:T(8,128)S(1)}) custom-call(bf16[192,512]{1,0:T(8,128)(2,1)S(1)} %get-tuple-element.16.q_ref, s32[192,128]{1,0:T(8,128)S(1)} %get-tuple-element.17.stamp_ref, bf16[208,512]{1,0:T(8,128)(2,1)S(1)} %collective-permute-done.1.refs_0_, bf16[208,512]{1,0:T(8,128)(2,1)S(1)} %collective-permute-done.3.refs_1_, ...), custom_call_target="tpu_custom_call" | custom-call | flops 4429185024 | tf_op jit(solution)/shard_map/pallas_call | solution.py:304
  24.0 0.7 %collective-permute-done.8.block_ref = bf16[208,512]{1,0:T(8,128)(2,1)S(1)} collective-permute-done((bf16[208,512]{1,0:T(8,128)(2,1)S(1)}, bf16[208,512]{1,0:T(8,128)(2,1)S(1)}, u32[]{:S(2)}, u32[]{:S(2)}) %collective-permute-start.8) | collective-permute-done | bytes 213024 | tf_op jit(solution)/shard_map/ppermute | solution.py:241
  24.7 1.2 %collective-permute-start.9 = (bf16[208,512]{1,0:T(8,128)(2,1)S(1)}, bf16[208,512]{1,0:T(8,128)(2,1)S(1)}, u32[]{:S(2)}, u32[]{:S(2)}) collective-permute-start(bf16[208,512]{1,0:T(8,128)(2,1)S(1)} %shard_map.83.refs_2_), channel_id=1, source_target_pairs={{0,1},{1,0},{2,3},{3,2},{4,5},{5,4},{6,7},{7,6},{8,9},{9,8},{10,11... | collective-permute-start | bytes 638984 | tf_op jit(solution)/shard_map/ppermute | solution.py:241
  25.9 3.4 %collective-permute-done.2.block_ref = bf16[208,512]{1,0:T(8,128)(2,1)S(1)} collective-permute-done((bf16[208,512]{1,0:T(8,128)(2,1)S(1)}, bf16[208,512]{1,0:T(8,128)(2,1)S(1)}, u32[]{:S(2)}, u32[]{:S(2)}) %collective-permute-start.2) | collective-permute-done | bytes 213024 | tf_op jit(solution)/shard_map/ppermute | solution.py:241
  29.3 0.8 %collective-permute-start.7 = (bf16[208,512]{1,0:T(8,128)(2,1)S(1)}, bf16[208,512]{1,0:T(8,128)(2,1)S(1)}, u32[]{:S(2)}, u32[]{:S(2)}) collective-permute-start(bf16[208,512]{1,0:T(8,128)(2,1)S(1)} %shard_map.82.refs_0_), channel_id=1, source_target_pairs={{0,1},{1,0},{2,3},{3,2},{4,5},{5,4},{6,7},{7,6},{8,9},{9,8},{10,11... | collective-permute-start | bytes 638984 | tf_op jit(solution)/shard_map/ppermute | solution.py:241
  30.1 0.0 collective-permute-done.10.refs_1_
  30.1 0.0 collective-permute-done.11.refs_5_
  30.1 0.0 copy-start.3
  30.1 0.0 copy-start.4
  30.1 0.0 copy-start.5
  30.1 2.1 %shard_map.84 = (f32[192,512]{1,0:T(8,128)S(1)}, f32[8,128]{1,0:T(8,128)}) custom-call(bf16[192,512]{1,0:T(8,128)(2,1)S(1)} %get-tuple-element.16.q_ref, s32[192,128]{1,0:T(8,128)S(1)} %get-tuple-element.17.stamp_ref, bf16[208,512]{1,0:T(8,128)(2,1)S(1)} %shard_map.79.asked_ref.refs_0_, bf16[208,512]{1,0:T(8,128)(2,1)S(1)} %collective-permute-done.10.refs_1_, ...), custom_call_target="tpu_custom_call" | custom-call | flops 4429185024 | tf_op jit(solution)/shard_map/pallas_call | solution.py:304
  32.2 0.0 collective-permute-done.9.refs_3_
  32.2 0.0 collective-permute-done.7.refs_1_
  32.2 0.0 copy-done.3
  32.2 0.0 copy-done.4
  32.3 0.0 copy-done.5
  32.3 3.8 %shard_map.85 = bf16[192,512]{1,0:T(8,128)(2,1)} custom-call(bf16[192,512]{1,0:T(8,128)(2,1)S(1)} %get-tuple-element.16.q_ref, s32[192,128]{1,0:T(8,128)S(1)} %get-tuple-element.17.stamp_ref, bf16[208,512]{1,0:T(8,128)(2,1)S(1)} %shard_map.82.refs_0_, bf16[208,512]{1,0:T(8,128)(2,1)S(1)} %collective-permute-done.7.refs_1_, ...), custom_call_target="tpu_custom_call" | custom-call | tf_op jit(solution)/shard_map/pallas_call | solution.py:355
  (6 shorter events, 0.0 us)
Async XLA Ops:
  1.9 4.0 %collective-permute-start = (bf16[208,512]{1,0:T(8,128)(2,1)}, bf16[208,512]{1,0:T(8,128)(2,1)S(1)}, u32[]{:S(2)}, u32[]{:S(2)}) collective-permute-start(bf16[208,512]{1,0:T(8,128)(2,1)} %shard_map.73.own_ref), channel_id=1, source_target_pairs={{0,1},{1,0},{2,3},{3,2},{4,5},{5,4},{6,7},{7,6},{8,9},{9,8},{10,11... | collective-permute-start | bytes 638984 | tf_op jit(solution)/shard_map/ppermute | solution.py:241
  2.6 14.7 %collective-permute-start.6 = (bf16[208,512]{1,0:T(8,128)(2,1)}, bf16[208,512]{1,0:T(8,128)(2,1)S(1)}, u32[]{:S(2)}, u32[]{:S(2)}) collective-permute-start(bf16[208,512]{1,0:T(8,128)(2,1)} %shard_map.73.own_ref), channel_id=1, source_target_pairs={{0,8},{1,9},{2,10},{3,11},{4,12},{5,13},{6,14},{7,15},{12,0},{13,1... | collective-permute-start | bytes 638984 | tf_op jit(solution)/shard_map/ppermute | solution.py:244
  4.5 13.5 %collective-permute-start.1 = (bf16[208,512]{1,0:T(8,128)(2,1)}, bf16[208,512]{1,0:T(8,128)(2,1)S(1)}, u32[]{:S(2)}, u32[]{:S(2)}) collective-permute-start(bf16[208,512]{1,0:T(8,128)(2,1)} %shard_map.73.own_ref), channel_id=1, source_target_pairs={{0,4},{1,5},{2,6},{3,7},{4,8},{5,9},{6,10},{7,11},{8,12},{9,13},{1... | collective-permute-start | bytes 638984 | tf_op jit(solution)/shard_map/ppermute | solution.py:244
  5.8 0.9 %copy-start.2 = (bf16[208,512]{1,0:T(8,128)(2,1)S(1)}, bf16[208,512]{1,0:T(8,128)(2,1)}, u32[]{:S(2)}) copy-start(bf16[208,512]{1,0:T(8,128)(2,1)} %shard_map.73.own_ref) | copy-start | bytes 638980
  6.8 6.7 %collective-permute-start.4 = (bf16[208,512]{1,0:T(8,128)(2,1)S(1)}, bf16[208,512]{1,0:T(8,128)(2,1)S(1)}, u32[]{:S(2)}, u32[]{:S(2)}) collective-permute-start(bf16[208,512]{1,0:T(8,128)(2,1)S(1)} %shard_map.74.own_ref.refs_0_), channel_id=1, source_target_pairs={{0,2},{1,3},{2,0},{3,1},{4,6},{5,7},{6,4},{7,5},{8,10},{9,11},{10,... | collective-permute-start | bytes 638984 | tf_op jit(solution)/shard_map/ppermute | solution.py:241
  7.1 1.6 %copy-start = (bf16[512,2048]{1,0:T(8,128)(2,1)S(1)}, bf16[512,2048]{1,0:T(8,128)(2,1)}, u32[]{:S(2)}) copy-start(bf16[512,2048]{1,0:T(8,128)(2,1)} %refs_4_.3) | copy-start | bytes 6291460
  8.7 0.7 %copy-start.6 = (f32[8,16]{1,0:T(8,128)S(1)}, f32[8,16]{1,0:T(8,128)}, u32[]{:S(2)}) copy-start(f32[8,16]{1,0:T(8,128)} %bias_ref.1) | copy-start | bytes 1540
  9.4 1.6 %copy-start.1 = (bf16[512,2048]{1,0:T(8,128)(2,1)S(1)}, bf16[512,2048]{1,0:T(8,128)(2,1)}, u32[]{:S(2)}) copy-start(bf16[512,2048]{1,0:T(8,128)(2,1)} %refs_4_.3) | copy-start | bytes 6291460
  13.5 6.1 %collective-permute-start.5 = (bf16[208,512]{1,0:T(8,128)(2,1)S(1)}, bf16[208,512]{1,0:T(8,128)(2,1)S(1)}, u32[]{:S(2)}, u32[]{:S(2)}) collective-permute-start(bf16[208,512]{1,0:T(8,128)(2,1)S(1)} %shard_map.77.refs_0_.refs_2_), channel_id=1, source_target_pairs={{0,1},{1,0},{2,3},{3,2},{4,5},{5,4},{6,7},{7,6},{8,9},{9,8},{10,11... | collective-permute-start | bytes 638984 | tf_op jit(solution)/shard_map/ppermute | solution.py:241
  17.3 12.7 %collective-permute-start.10 = (bf16[208,512]{1,0:T(8,128)(2,1)S(1)}, bf16[208,512]{1,0:T(8,128)(2,1)S(1)}, u32[]{:S(2)}, u32[]{:S(2)}) collective-permute-start(bf16[208,512]{1,0:T(8,128)(2,1)S(1)} %shard_map.79.asked_ref.refs_0_), channel_id=1, source_target_pairs={{0,1},{1,0},{2,3},{3,2},{4,5},{5,4},{6,7},{7,6},{8,9},{9,8},{10,11... | collective-permute-start | bytes 638984 | tf_op jit(solution)/shard_map/ppermute | solution.py:241
  17.8 6.9 %collective-permute-start.8 = (bf16[208,512]{1,0:T(8,128)(2,1)S(1)}, bf16[208,512]{1,0:T(8,128)(2,1)S(1)}, u32[]{:S(2)}, u32[]{:S(2)}) collective-permute-start(bf16[208,512]{1,0:T(8,128)(2,1)S(1)} %shard_map.79.asked_ref.refs_0_), channel_id=1, source_target_pairs={{0,2},{1,3},{2,0},{3,1},{4,6},{5,7},{6,4},{7,5},{8,10},{9,11},{10,... | collective-permute-start | bytes 638984 | tf_op jit(solution)/shard_map/ppermute | solution.py:241
  18.1 4.4 %collective-permute-start.3 = (bf16[208,512]{1,0:T(8,128)(2,1)S(1)}, bf16[208,512]{1,0:T(8,128)(2,1)S(1)}, u32[]{:S(2)}, u32[]{:S(2)}) collective-permute-start(bf16[208,512]{1,0:T(8,128)(2,1)S(1)} %collective-permute-done.1.refs_0_), channel_id=1, source_target_pairs={{0,1},{1,0},{2,3},{3,2},{4,5},{5,4},{6,7},{7,6},{8,9},{9,8},{10,11... | collective-permute-start | bytes 638984 | tf_op jit(solution)/shard_map/ppermute | solution.py:241
  18.8 10.5 %collective-permute-start.2 = (bf16[208,512]{1,0:T(8,128)(2,1)S(1)}, bf16[208,512]{1,0:T(8,128)(2,1)S(1)}, u32[]{:S(2)}, u32[]{:S(2)}) collective-permute-start(bf16[208,512]{1,0:T(8,128)(2,1)S(1)} %collective-permute-done.1.refs_0_), channel_id=1, source_target_pairs={{0,2},{1,3},{2,0},{3,1},{4,6},{5,7},{6,4},{7,5},{8,10},{9,11},{10,... | collective-permute-start | bytes 638984 | tf_op jit(solution)/shard_map/ppermute | solution.py:241
  19.6 10.5 %collective-permute-start.11 = (bf16[192,512]{1,0:T(8,128)(2,1)S(1)}, bf16[192,512]{1,0:T(8,128)(2,1)S(1)}, u32[]{:S(2)}, u32[]{:S(2)}) collective-permute-start(bf16[192,512]{1,0:T(8,128)(2,1)S(1)} %get-tuple-element.24), channel_id=1, source_target_pairs={{0,12},{1,13},{2,14},{3,15},{16,28},{17,29},{18,30},{19,31}} | collective-permute-start | bytes 589832 | tf_op jit(solution)/shard_map/ppermute | solution.py:244
  24.7 7.5 %collective-permute-start.9 = (bf16[208,512]{1,0:T(8,128)(2,1)S(1)}, bf16[208,512]{1,0:T(8,128)(2,1)S(1)}, u32[]{:S(2)}, u32[]{:S(2)}) collective-permute-start(bf16[208,512]{1,0:T(8,128)(2,1)S(1)} %shard_map.83.refs_2_), channel_id=1, source_target_pairs={{0,1},{1,0},{2,3},{3,2},{4,5},{5,4},{6,7},{7,6},{8,9},{9,8},{10,11... | collective-permute-start | bytes 638984 | tf_op jit(solution)/shard_map/ppermute | solution.py:241
  29.3 3.0 %collective-permute-start.7 = (bf16[208,512]{1,0:T(8,128)(2,1)S(1)}, bf16[208,512]{1,0:T(8,128)(2,1)S(1)}, u32[]{:S(2)}, u32[]{:S(2)}) collective-permute-start(bf16[208,512]{1,0:T(8,128)(2,1)S(1)} %shard_map.82.refs_0_), channel_id=1, source_target_pairs={{0,1},{1,0},{2,3},{3,2},{4,5},{5,4},{6,7},{7,6},{8,9},{9,8},{10,11... | collective-permute-start | bytes 638984 | tf_op jit(solution)/shard_map/ppermute | solution.py:241
  30.1 2.2 %copy-start.3 = (bf16[192,512]{1,0:T(8,128)(2,1)S(1)}, bf16[192,512]{1,0:T(8,128)(2,1)}, u32[]{:S(2)}) copy-start(bf16[192,512]{1,0:T(8,128)(2,1)} %refs_10_.1) | copy-start | bytes 589828
  30.1 2.2 %copy-start.4 = (bf16[512,512]{1,0:T(8,128)(2,1)S(1)}, bf16[512,512]{1,0:T(8,128)(2,1)}, u32[]{:S(2)}) copy-start(bf16[512,512]{1,0:T(8,128)(2,1)} %refs_9_.1) | copy-start | bytes 1572868
  30.1 2.2 %copy-start.5 = (f32[512]{0:T(512)S(1)}, f32[512]{0:T(512)}, u32[]{:S(2)}) copy-start(f32[512]{0:T(512)} %param.12) | copy-start | bytes 6148

commit v4 on v3

--- a/solution.py
+++ b/solution.py
@@ -12,7 +12,7 @@
 EPSILON = 1e-05
 LANES = 128
 TAIL = 16
-COST = (4, 16, 16, 32, 32, 1, 0)
+COST = (4, 16, 16, 32, 0, 32, 100)
 FIXED = 15
 BF16 = jnp.bfloat16
 F32 = jnp.float32
@@ -74,7 +74,11 @@
     out_ref[...] = own_ref[...]
 
 
-def front_kernel(own_ref, w_ref, bias_ref, q_ref, gate_ref, stamp_ref, table_ref):
+def front_kernel(own_ref, w_ref, bias_ref, tokens_ref, wo_ref, gain_ref, *refs):
+    q_ref, gate_ref, stamp_ref, table_ref, tokens_out, wo_out, gain_out = refs
+    gain_out[...] = gain_ref[...]
+    tokens_out[...] = tokens_ref[...]
+    wo_out[...] = wo_ref[...]
     rows, width = q_ref.shape
     stamp_ref[...] = down_rows(stamps_of(own_ref))
     normed = own_ref[:rows, :]
@@ -92,7 +96,7 @@
         table_ref[p : p + 1, :] = high.astype(I32) * 65536 + low.astype(I32)
 
 
-def add_blocks(q_ref, stamp_ref, blocks, w_ref, table_ref, acc_ref, out_ref, hide=None, more_ref=None):
+def add_blocks(q_ref, stamp_ref, blocks, w_ref, table_ref, acc_ref, out_ref, hide=None):
     rows, width = q_ref.shape
     size = width // HEADS
     keys = len(blocks) * rows
@@ -133,8 +137,6 @@
         )
         if acc_ref is not None:
             mixed = acc_ref[:, pair] + mixed
-        if more_ref is not None:
-            mixed = more_ref[:, pair].astype(F32) + mixed
         out_ref[:, pair] = mixed.astype(out_ref.dtype)
 
 
@@ -158,24 +160,20 @@
     tick_ref[...] = jnp.zeros_like(tick_ref)
 
 
-def attend_kernel(near, step, given, tell, q_ref, stamp_ref, *refs):
+def attend_kernel(near, step, tell, q_ref, stamp_ref, *refs):
     blocks = refs[:2]
     w_ref, table_ref, acc_ref = refs[2:5]
     out_ref = refs[-2] if tell else refs[-1]
-    more_ref = refs[5] if given else None
     level, spot = place(near)
     seen = level >= step if step else spot >= near // 2
 
     @pl.when(seen)
     def _():
-        add_blocks(
-            q_ref, stamp_ref, blocks, w_ref, table_ref, acc_ref, out_ref, more_ref=more_ref
-        )
+        add_blocks(q_ref, stamp_ref, blocks, w_ref, table_ref, acc_ref, out_ref)
 
     @pl.when(jnp.logical_not(seen))
     def _():
-        kept = acc_ref[...]
-        out_ref[...] = kept + more_ref[...].astype(F32) if given else kept
+        out_ref[...] = acc_ref[...]
 
     if tell:
         refs[-1][...] = jnp.zeros_like(refs[-1])
@@ -215,6 +213,10 @@
     gated = layer_norm(sum_ref[...], gain_ref[...]) * gate_ref[...].astype(F32)
     mixed = jnp.dot(gated.astype(BF16), wo_ref[...], preferred_element_type=F32)
     out_ref[...] = (tokens_ref[...].astype(F32) + mixed).astype(BF16)
+
+
+def sum_kernel(sum_ref, more_ref, out_ref):
+    out_ref[...] = sum_ref[...] + more_ref[...].astype(F32)
 
 
 def pin_kernel(block_ref, tick_ref, out_ref):
@@ -262,7 +264,7 @@
     far = {}
     for step in range(levels - 2, 0, -1):
         pairs = [(z, z + step) for z in range(levels - step)]
-        if step == levels - 2:
+        if step == 1:
             pairs.append((levels - 1, 0))
         far[step] = hop(own, pairs)
     by_core = swap(own, 1)
@@ -277,26 +279,29 @@
         ),
     )(own, by_core)
     by_y = swap(own, 2)
-    queries, gate, stamp_rows, table = pl.pallas_call(
+    queries, gate, stamp_rows, table, tokens, w_out, attn_gain = pl.pallas_call(
         front_kernel,
         out_shape=(
             jax.ShapeDtypeStruct((rows, width), BF16),
             jax.ShapeDtypeStruct((rows, width), BF16),
             jax.ShapeDtypeStruct((rows, LANES), I32),
             jax.ShapeDtypeStruct((rel_bias.shape[0] // 2, LANES), I32),
-        ),
-        in_specs=[VMEM] * 3,
-        out_specs=(VMEM,) * 4,
+            jax.ShapeDtypeStruct(tokens.shape, BF16),
+            jax.ShapeDtypeStruct(w_out.shape, BF16),
+            jax.ShapeDtypeStruct((1, width), F32),
+        ),
+        in_specs=[VMEM] * 6,
+        out_specs=(VMEM,) * 7,
         compiler_params=pltpu.CompilerParams(vmem_limit_bytes=VMEM_LIMIT),
         cost_estimate=pl.CostEstimate(
             flops=4 * COST[0] * rows * width * width, bytes_accessed=0, transcendentals=0
         ),
-    )(own, w_proj, rel_bias)
+    )(own, w_proj, rel_bias, tokens, w_out, attn_gain.reshape(1, width))
 
     tick_shape = jax.ShapeDtypeStruct((8, LANES), F32)
     params = pltpu.CompilerParams(vmem_limit_bytes=VMEM_LIMIT)
 
-    def attend(step, blocks, total, *more, weight, given=False, tell=True):
+    def attend(step, blocks, total, *more, weight, tell=True):
         flops = weight * 2 * rows * width * (width + rows)
         args = [queries, stamp_rows, *blocks, w_proj, table]
         args += [] if total is None else [total]
@@ -304,7 +309,7 @@
         return pl.pallas_call(
             own_kernel
             if total is None
-            else functools.partial(attend_kernel, near, step, given, tell),
+            else functools.partial(attend_kernel, near, step, tell),
             out_shape=(jax.ShapeDtypeStruct((rows, width), F32), tick_shape)[: 1 + tell],
             in_specs=[VMEM] * len(args),
             out_specs=(VMEM, VMEM)[: 1 + tell],
@@ -320,10 +325,12 @@
     by_both = swap(by_y, 1)
     (total,) = attend(0, [by_y, by_both], total, weight=COST[2], tell=False)
     across = {}
-    for step in sorted(far):
-        block = pin(far[step], began) if step == levels - 2 else far[step]
+
+    def pass_on(step, block):
         across[step] = swap(block, 2)
         far[step] = [block, swap(block, 1)]
+
+    pass_on(1, pin(far[1], began))
     returned, tick = pl.pallas_call(
         functools.partial(return_kernel, near),
         out_shape=(jax.ShapeDtypeStruct((rows, width), BF16), tick_shape),
@@ -334,24 +341,35 @@
         cost_estimate=pl.CostEstimate(
             flops=COST[3] * rows * width * (width + rows), bytes_accessed=0, transcendentals=0
         ),
-    )(far[levels - 2][0], own, by_core, by_y, by_both, w_proj, table)
+    )(far[1][0], own, by_core, by_y, by_both, w_proj, table)
     given = hop(returned, [(0, levels - 1)])
     steps = sorted(far)
+    for step in steps[1:]:
+        pass_on(step, far[step])
     for step in steps:
-        extra = (given,) if step == steps[-1] else (tick,)
-        total, done = attend(
-            step, far[step], total, *extra, weight=COST[4], given=step == steps[-1]
-        )
-        tick = done if step == steps[0] else tick
+        last = step == steps[-1]
+        extra = (tick,) if step == 1 else ()
+        total, *told = attend(step, far[step], total, *extra, weight=COST[4], tell=last)
+    (tick,) = told
     sets = {}
     for step in steps:
         block = pin(across[step], tick)
         sets[step] = [block, swap(block, 1)]
     for step in steps[:-2]:
         (total,) = attend(step, sets[step], total, weight=COST[5], tell=False)
+    total = pl.pallas_call(
+        sum_kernel,
+        out_shape=jax.ShapeDtypeStruct((rows, width), F32),
+        in_specs=[VMEM] * 2,
+        out_specs=VMEM,
+        compiler_params=pltpu.CompilerParams(vmem_limit_bytes=2 << 20),
+        cost_estimate=pl.CostEstimate(
+            flops=COST[5] * rows * width * width, bytes_accessed=0, transcendentals=0
+        ),
+    )(total, given)
     blocks = [block for step in steps[-2:] for block in sets[step]]
     args = [queries, stamp_rows, *blocks, w_proj, table, total, gate]
-    args += [attn_gain.reshape(1, width), w_out, tokens]
+    args += [attn_gain, w_out, tokens]
     return pl.pallas_call(
         functools.partial(last_kernel, near, steps[-2:]),
         out_shape=jax.ShapeDtypeStruct((rows, width), BF16),

time: 36.6 us -> 35.3 us (0.964)
  the two profiles are of different devices: /device:TPU:31 before, /device:TPU:24 now
where the time goes in v4:
time: 35.3 us; the launch traced here: 35.1 us
  waiting for transfers between devices  14.4 us (41%)
  Pallas kernels  11 us (31%)
  starting transfers between devices  8.51 us (24%)
  local copies, waits for them, and re-layouts  0.96 us (3%)
    ppermute x3, waiting for transfers between devices, hop(): lax.ppermute(block, 'pb', [(a * near + i, b * near + i) for a, b in pairs...  8.8 us
    ppermute x9, starting transfers between devices, swap(): return lax.ppermute(block, 'pb', [(i, i ^ bit) for i in range(shards)])  5.75 us
    ppermute x9, waiting for transfers between devices, swap(): return lax.ppermute(block, 'pb', [(i, i ^ bit) for i in range(shards)])  5.64 us
    pallas_call x4, Pallas kernels, attend(): pl.pallas_call(own_kernel if total is None else functools.partial(attend_...  4.72 us
    pallas_call x1, Pallas kernels, body(): pl.pallas_call(functools.partial(last_kernel, near, steps[-2:]), out_shap...  3.85 us
    ppermute x3, starting transfers between devices, hop(): lax.ppermute(block, 'pb', [(a * near + i, b * near + i) for a, b in pairs...  2.76 us
    pallas_call x1, Pallas kernels, body(): pl.pallas_call(norm_kernel, out_shape=jax.ShapeDtypeStruct((rows + TAIL,...  1.88 us
    unnamed x12, local copies, waits for them, and re-layouts  0.96 us
  transfers between devices with their start and end apart: 12, of which 5 were waited for; matrix products, arithmetic and copies ran while one was open for 0% of the time, Pallas kernels for 15%

profile of v4, /device:TPU:24, one launch (start us, length us, event | category | flops | bytes accessed | tf_op | source)
XLA Modules:
  0.0 35.1 jit_solution(14507135005173161472)
XLA Ops:
  0.0 0.0 copy-start.4
  0.0 0.0 copy-start.5
  0.0 1.9 %shard_map.73.own_ref = bf16[208,512]{1,0:T(8,128)(2,1)} custom-call(bf16[192,512]{1,0:T(8,128)(2,1)} %tokens_ref.1, s32[1,192]{1,0:T(1,128)} %bitcast.5, f32[1,512]{1,0:T(1,128)} %bitcast.4), custom_call_target="tpu_custom_call" | custom-call | tf_op jit(solution)/shard_map/pallas_call | solution.py:250
  1.9 0.0 copy-start
  1.9 0.0 copy-start.1
  1.9 0.0 copy-start.2
  1.9 0.1 collective-permute-start
  2.0 0.1 collective-permute-start.1
  2.1 1.4 %collective-permute-start.3 = (bf16[208,512]{1,0:T(8,128)(2,1)}, bf16[208,512]{1,0:T(8,128)(2,1)S(1)}, u32[]{:S(2)}, u32[]{:S(2)}) collective-permute-start(bf16[208,512]{1,0:T(8,128)(2,1)} %shard_map.73.own_ref), channel_id=1, source_target_pairs={{0,8},{1,9},{2,10},{3,11},{4,12},{5,13},{6,14},{7,15},{16,24},{17,... | collective-permute-start | bytes 638984 | tf_op jit(solution)/shard_map/ppermute | solution.py:246
  3.5 0.2 collective-permute-done.other_ref.refs_1_
  3.7 0.0 copy-start.3
  3.7 0.9 %copy-done.3 = bf16[208,512]{1,0:T(8,128)(2,1)S(1)} copy-done((bf16[208,512]{1,0:T(8,128)(2,1)S(1)}, bf16[208,512]{1,0:T(8,128)(2,1)}, u32[]{:S(2)}) %copy-start.3) | copy-done | bytes 213016
  4.6 1.6 %collective-permute-start.6 = (bf16[208,512]{1,0:T(8,128)(2,1)S(1)}, bf16[208,512]{1,0:T(8,128)(2,1)S(1)}, u32[]{:S(2)}, u32[]{:S(2)}) collective-permute-start(bf16[208,512]{1,0:T(8,128)(2,1)S(1)} %shard_map.74.own_ref.refs_0_), channel_id=1, source_target_pairs={{0,2},{1,3},{2,0},{3,1},{4,6},{5,7},{6,4},{7,5},{8,10},{9,11},{10,... | collective-permute-start | bytes 638984 | tf_op jit(solution)/shard_map/ppermute | solution.py:243
  6.2 0.0 copy-done.4
  6.3 0.0 copy-done.5
  6.3 0.0 copy-done
  6.3 0.0 copy-done.1
  6.3 0.0 copy-done.2
  6.3 0.5 %shard_map.75 = (bf16[192,512]{1,0:T(8,128)(2,1)S(1)}, bf16[192,512]{1,0:T(8,128)(2,1)S(1)}, s32[192,128]{1,0:T(8,128)S(1)}, s32[4,128]{1,0:T(4,128)S(1)}, bf16[...) custom-call(bf16[208,512]{1,0:T(8,128)(2,1)S(1)} %shard_map.74.own_ref.refs_0_, ...), custom_call_target="tpu_custom_call" | custom-call | flops 805306368 | tf_op jit(solution)/shard_map/pallas_call | solution.py:282
  6.7 1.6 %shard_map.76 = (f32[192,512]{1,0:T(8,128)S(1)}, f32[8,128]{1,0:T(8,128)S(1)}) custom-call(bf16[192,512]{1,0:T(8,128)(2,1)S(1)} %get-tuple-element.18.q_ref, s32[192,128]{1,0:T(8,128)S(1)} %get-tuple-element.19.stamp_ref, bf16[208,512]{1,0:T(8,128)(2,1)S(1)} %shard_map.74.own_ref.refs_0_, bf16[208,512]{1,0:T(8,128)(2,1)S(1)} %collective-permute-done.other_ref.refs_1_, ...), custom_call_target="tpu_custom_call" | custom-call | flops 2214592512 | tf_op jit(solution)/shard_map/pallas_call | solution.py:309
  8.3 3.8 %collective-permute-done.6.block_ref = bf16[208,512]{1,0:T(8,128)(2,1)S(1)} collective-permute-done((bf16[208,512]{1,0:T(8,128)(2,1)S(1)}, bf16[208,512]{1,0:T(8,128)(2,1)S(1)}, u32[]{:S(2)}, u32[]{:S(2)}) %collective-permute-start.6) | collective-permute-done | bytes 213024 | tf_op jit(solution)/shard_map/ppermute | solution.py:243
  12.1 0.0 collective-permute-start.7
  12.1 0.0 collective-permute-done.1.block_ref
  12.1 0.5 %collective-permute-start.5 = (bf16[208,512]{1,0:T(8,128)(2,1)S(1)}, bf16[208,512]{1,0:T(8,128)(2,1)S(1)}, u32[]{:S(2)}, u32[]{:S(2)}) collective-permute-start(bf16[208,512]{1,0:T(8,128)(2,1)S(1)} %shard_map.77.asked_ref.refs_0_), channel_id=1, source_target_pairs={{0,1},{1,0},{2,3},{3,2},{4,5},{5,4},{6,7},{7,6},{8,9},{9,8},{10,11... | collective-permute-start | bytes 638984 | tf_op jit(solution)/shard_map/ppermute | solution.py:243
  12.6 1.5 %collective-permute-start.2 = (bf16[208,512]{1,0:T(8,128)(2,1)S(1)}, bf16[208,512]{1,0:T(8,128)(2,1)S(1)}, u32[]{:S(2)}, u32[]{:S(2)}) collective-permute-start(bf16[208,512]{1,0:T(8,128)(2,1)S(1)} %shard_map.77.asked_ref.refs_0_), channel_id=1, source_target_pairs={{0,2},{1,3},{2,0},{3,1},{4,6},{5,7},{6,4},{7,5},{8,10},{9,11},{10,... | collective-permute-start | bytes 638984 | tf_op jit(solution)/shard_map/ppermute | solution.py:243
  14.2 4.7 %collective-permute-done.3.refs_0_ = bf16[208,512]{1,0:T(8,128)(2,1)S(1)} collective-permute-done((bf16[208,512]{1,0:T(8,128)(2,1)}, bf16[208,512]{1,0:T(8,128)(2,1)S(1)}, u32[]{:S(2)}, u32[]{:S(2)}) %collective-permute-start.3) | collective-permute-done | bytes 213024 | tf_op jit(solution)/shard_map/ppermute | solution.py:246
  18.9 0.0 collective-permute-start.4
  18.9 1.5 %collective-permute-start.9 = (bf16[208,512]{1,0:T(8,128)(2,1)S(1)}, bf16[208,512]{1,0:T(8,128)(2,1)S(1)}, u32[]{:S(2)}, u32[]{:S(2)}) collective-permute-start(bf16[208,512]{1,0:T(8,128)(2,1)S(1)} %collective-permute-done.3.refs_0_), channel_id=1, source_target_pairs={{0,2},{1,3},{2,0},{3,1},{4,6},{5,7},{6,4},{7,5},{8,10},{9,11},{10,... | collective-permute-start | bytes 638984 | tf_op jit(solution)/shard_map/ppermute | solution.py:243
  20.4 0.0 collective-permute-done.7.refs_1_.refs_3_
  20.4 1.3 %collective-permute-start.11 = (bf16[192,512]{1,0:T(8,128)(2,1)S(1)}, bf16[192,512]{1,0:T(8,128)(2,1)S(1)}, u32[]{:S(2)}, u32[]{:S(2)}) collective-permute-start(bf16[192,512]{1,0:T(8,128)(2,1)S(1)} %get-tuple-element.26), channel_id=1, source_target_pairs={{0,12},{1,13},{2,14},{3,15},{16,28},{17,29},{18,30},{19,31}} | collective-permute-start | bytes 589832 | tf_op jit(solution)/shard_map/ppermute | solution.py:246
  21.8 0.0 collective-permute-done.5.refs_1_
  21.8 1.5 %shard_map.81.refs_4_ = f32[192,512]{1,0:T(8,128)S(1)} custom-call(bf16[192,512]{1,0:T(8,128)(2,1)S(1)} %get-tuple-element.18.q_ref, s32[192,128]{1,0:T(8,128)S(1)} %get-tuple-element.19.stamp_ref, bf16[208,512]{1,0:T(8,128)(2,1)S(1)} %shard_map.77.asked_ref.refs_0_, bf16[208,512]{1,0:T(8,128)(2,1)S(1)} %collective-permute-done.5.refs_1_, ...), custom_call_target="tpu_custom_call" | custom-call | tf_op jit(solution)/shard_map/pallas_call | solution.py:309
  23.3 0.0 collective-permute-done.4.refs_1_
  23.3 1.5 %shard_map.82 = (f32[192,512]{1,0:T(8,128)S(1)}, f32[8,128]{1,0:T(8,128)S(1)}) custom-call(bf16[192,512]{1,0:T(8,128)(2,1)S(1)} %get-tuple-element.18.q_ref, s32[192,128]{1,0:T(8,128)S(1)} %get-tuple-element.19.stamp_ref, bf16[208,512]{1,0:T(8,128)(2,1)S(1)} %collective-permute-done.3.refs_0_, bf16[208,512]{1,0:T(8,128)(2,1)S(1)} %collective-permute-done.4.refs_1_, ...), custom_call_target="tpu_custom_call" | custom-call | tf_op jit(solution)/shard_map/pallas_call | solution.py:309
  24.9 1.7 %collective-permute-done.9.block_ref = bf16[208,512]{1,0:T(8,128)(2,1)S(1)} collective-permute-done((bf16[208,512]{1,0:T(8,128)(2,1)S(1)}, bf16[208,512]{1,0:T(8,128)(2,1)S(1)}, u32[]{:S(2)}, u32[]{:S(2)}) %collective-permute-start.9) | collective-permute-done | bytes 213024 | tf_op jit(solution)/shard_map/ppermute | solution.py:243
  26.6 0.0 collective-permute-start.10
  26.6 0.0 collective-permute-done.2.block_ref
  26.6 0.5 %collective-permute-start.8 = (bf16[208,512]{1,0:T(8,128)(2,1)S(1)}, bf16[208,512]{1,0:T(8,128)(2,1)S(1)}, u32[]{:S(2)}, u32[]{:S(2)}) collective-permute-start(bf16[208,512]{1,0:T(8,128)(2,1)S(1)} %shard_map.83.refs_0_), channel_id=1, source_target_pairs={{0,1},{1,0},{2,3},{3,2},{4,5},{5,4},{6,7},{7,6},{8,9},{9,8},{10,11... | collective-permute-start | bytes 638984 | tf_op jit(solution)/shard_map/ppermute | solution.py:243
  27.1 4.1 %collective-permute-done.11.more_ref = bf16[192,512]{1,0:T(8,128)(2,1)S(1)} collective-permute-done((bf16[192,512]{1,0:T(8,128)(2,1)S(1)}, bf16[192,512]{1,0:T(8,128)(2,1)S(1)}, u32[]{:S(2)}, u32[]{:S(2)}) %collective-permute-start.11) | collective-permute-done | bytes 196640 | tf_op jit(solution)/shard_map/ppermute | solution.py:246
  31.1 0.1 shard_map.85.refs_6_
  31.2 0.0 collective-permute-done.10.refs_3_
  31.2 0.0 collective-permute-done.8.refs_1_
  31.2 3.8 %shard_map.86 = bf16[192,512]{1,0:T(8,128)(2,1)} custom-call(bf16[192,512]{1,0:T(8,128)(2,1)S(1)} %get-tuple-element.18.q_ref, s32[192,128]{1,0:T(8,128)S(1)} %get-tuple-element.19.stamp_ref, bf16[208,512]{1,0:T(8,128)(2,1)S(1)} %shard_map.83.refs_0_, bf16[208,512]{1,0:T(8,128)(2,1)S(1)} %collective-permute-done.8.refs_1_, ...), custom_call_target="tpu_custom_call" | custom-call | tf_op jit(solution)/shard_map/pallas_call | solution.py:373
  (7 shorter events, 0.1 us)
Async XLA Ops:
  0.0 6.3 %copy-start.4 = (f32[8,16]{1,0:T(8,128)S(1)}, f32[8,16]{1,0:T(8,128)}, u32[]{:S(2)}) copy-start(f32[8,16]{1,0:T(8,128)} %bias_ref.1) | copy-start | bytes 1540
  0.0 6.3 %copy-start.5 = (f32[512]{0:T(512)S(1)}, f32[512]{0:T(512)}, u32[]{:S(2)}) copy-start(f32[512]{0:T(512)} %param.12) | copy-start | bytes 6148
  1.9 4.4 %copy-start = (bf16[512,2048]{1,0:T(8,128)(2,1)S(1)}, bf16[512,2048]{1,0:T(8,128)(2,1)}, u32[]{:S(2)}) copy-start(bf16[512,2048]{1,0:T(8,128)(2,1)} %refs_4_.3) | copy-start | bytes 6291460
  1.9 4.4 %copy-start.1 = (bf16[192,512]{1,0:T(8,128)(2,1)S(1)}, bf16[192,512]{1,0:T(8,128)(2,1)}, u32[]{:S(2)}) copy-start(bf16[192,512]{1,0:T(8,128)(2,1)} %tokens_ref.1) | copy-start | bytes 589828
  1.9 4.3 %copy-start.2 = (bf16[512,512]{1,0:T(8,128)(2,1)S(1)}, bf16[512,512]{1,0:T(8,128)(2,1)}, u32[]{:S(2)}) copy-start(bf16[512,512]{1,0:T(8,128)(2,1)} %wo_ref.1) | copy-start | bytes 1572868
  1.9 1.7 %collective-permute-start = (bf16[208,512]{1,0:T(8,128)(2,1)}, bf16[208,512]{1,0:T(8,128)(2,1)S(1)}, u32[]{:S(2)}, u32[]{:S(2)}) collective-permute-start(bf16[208,512]{1,0:T(8,128)(2,1)} %shard_map.73.own_ref), channel_id=1, source_target_pairs={{0,1},{1,0},{2,3},{3,2},{4,5},{5,4},{6,7},{7,6},{8,9},{9,8},{10,11... | collective-permute-start | bytes 638984 | tf_op jit(solution)/shard_map/ppermute | solution.py:243
  2.0 10.1 %collective-permute-start.1 = (bf16[208,512]{1,0:T(8,128)(2,1)}, bf16[208,512]{1,0:T(8,128)(2,1)S(1)}, u32[]{:S(2)}, u32[]{:S(2)}) collective-permute-start(bf16[208,512]{1,0:T(8,128)(2,1)} %shard_map.73.own_ref), channel_id=1, source_target_pairs={{0,4},{1,5},{2,6},{3,7},{4,8},{5,9},{6,10},{7,11},{8,12},{9,13},{1... | collective-permute-start | bytes 638984 | tf_op jit(solution)/shard_map/ppermute | solution.py:246
  2.1 16.8 %collective-permute-start.3 = (bf16[208,512]{1,0:T(8,128)(2,1)}, bf16[208,512]{1,0:T(8,128)(2,1)S(1)}, u32[]{:S(2)}, u32[]{:S(2)}) collective-permute-start(bf16[208,512]{1,0:T(8,128)(2,1)} %shard_map.73.own_ref), channel_id=1, source_target_pairs={{0,8},{1,9},{2,10},{3,11},{4,12},{5,13},{6,14},{7,15},{16,24},{17,... | collective-permute-start | bytes 638984 | tf_op jit(solution)/shard_map/ppermute | solution.py:246
  3.7 0.9 %copy-start.3 = (bf16[208,512]{1,0:T(8,128)(2,1)S(1)}, bf16[208,512]{1,0:T(8,128)(2,1)}, u32[]{:S(2)}) copy-start(bf16[208,512]{1,0:T(8,128)(2,1)} %shard_map.73.own_ref) | copy-start | bytes 638980
  4.6 7.5 %collective-permute-start.6 = (bf16[208,512]{1,0:T(8,128)(2,1)S(1)}, bf16[208,512]{1,0:T(8,128)(2,1)S(1)}, u32[]{:S(2)}, u32[]{:S(2)}) collective-permute-start(bf16[208,512]{1,0:T(8,128)(2,1)S(1)} %shard_map.74.own_ref.refs_0_), channel_id=1, source_target_pairs={{0,2},{1,3},{2,0},{3,1},{4,6},{5,7},{6,4},{7,5},{8,10},{9,11},{10,... | collective-permute-start | bytes 638984 | tf_op jit(solution)/shard_map/ppermute | solution.py:243
  12.1 8.3 %collective-permute-start.7 = (bf16[208,512]{1,0:T(8,128)(2,1)S(1)}, bf16[208,512]{1,0:T(8,128)(2,1)S(1)}, u32[]{:S(2)}, u32[]{:S(2)}) collective-permute-start(bf16[208,512]{1,0:T(8,128)(2,1)S(1)} %shard_map.78.refs_0_.refs_2_), channel_id=1, source_target_pairs={{0,1},{1,0},{2,3},{3,2},{4,5},{5,4},{6,7},{7,6},{8,9},{9,8},{10,11... | collective-permute-start | bytes 638984 | tf_op jit(solution)/shard_map/ppermute | solution.py:243
  12.1 9.6 %collective-permute-start.5 = (bf16[208,512]{1,0:T(8,128)(2,1)S(1)}, bf16[208,512]{1,0:T(8,128)(2,1)S(1)}, u32[]{:S(2)}, u32[]{:S(2)}) collective-permute-start(bf16[208,512]{1,0:T(8,128)(2,1)S(1)} %shard_map.77.asked_ref.refs_0_), channel_id=1, source_target_pairs={{0,1},{1,0},{2,3},{3,2},{4,5},{5,4},{6,7},{7,6},{8,9},{9,8},{10,11... | collective-permute-start | bytes 638984 | tf_op jit(solution)/shard_map/ppermute | solution.py:243
  12.6 13.9 %collective-permute-start.2 = (bf16[208,512]{1,0:T(8,128)(2,1)S(1)}, bf16[208,512]{1,0:T(8,128)(2,1)S(1)}, u32[]{:S(2)}, u32[]{:S(2)}) collective-permute-start(bf16[208,512]{1,0:T(8,128)(2,1)S(1)} %shard_map.77.asked_ref.refs_0_), channel_id=1, source_target_pairs={{0,2},{1,3},{2,0},{3,1},{4,6},{5,7},{6,4},{7,5},{8,10},{9,11},{10,... | collective-permute-start | bytes 638984 | tf_op jit(solution)/shard_map/ppermute | solution.py:243
  18.9 4.4 %collective-permute-start.4 = (bf16[208,512]{1,0:T(8,128)(2,1)S(1)}, bf16[208,512]{1,0:T(8,128)(2,1)S(1)}, u32[]{:S(2)}, u32[]{:S(2)}) collective-permute-start(bf16[208,512]{1,0:T(8,128)(2,1)S(1)} %collective-permute-done.3.refs_0_), channel_id=1, source_target_pairs={{0,1},{1,0},{2,3},{3,2},{4,5},{5,4},{6,7},{7,6},{8,9},{9,8},{10,11... | collective-permute-start | bytes 638984 | tf_op jit(solution)/shard_map/ppermute | solution.py:243
  18.9 7.7 %collective-permute-start.9 = (bf16[208,512]{1,0:T(8,128)(2,1)S(1)}, bf16[208,512]{1,0:T(8,128)(2,1)S(1)}, u32[]{:S(2)}, u32[]{:S(2)}) collective-permute-start(bf16[208,512]{1,0:T(8,128)(2,1)S(1)} %collective-permute-done.3.refs_0_), channel_id=1, source_target_pairs={{0,2},{1,3},{2,0},{3,1},{4,6},{5,7},{6,4},{7,5},{8,10},{9,11},{10,... | collective-permute-start | bytes 638984 | tf_op jit(solution)/shard_map/ppermute | solution.py:243
  20.4 10.7 %collective-permute-start.11 = (bf16[192,512]{1,0:T(8,128)(2,1)S(1)}, bf16[192,512]{1,0:T(8,128)(2,1)S(1)}, u32[]{:S(2)}, u32[]{:S(2)}) collective-permute-start(bf16[192,512]{1,0:T(8,128)(2,1)S(1)} %get-tuple-element.26), channel_id=1, source_target_pairs={{0,12},{1,13},{2,14},{3,15},{16,28},{17,29},{18,30},{19,31}} | collective-permute-start | bytes 589832 | tf_op jit(solution)/shard_map/ppermute | solution.py:246
  26.6 4.6 %collective-permute-start.10 = (bf16[208,512]{1,0:T(8,128)(2,1)S(1)}, bf16[208,512]{1,0:T(8,128)(2,1)S(1)}, u32[]{:S(2)}, u32[]{:S(2)}) collective-permute-start(bf16[208,512]{1,0:T(8,128)(2,1)S(1)} %shard_map.84.refs_2_), channel_id=1, source_target_pairs={{0,1},{1,0},{2,3},{3,2},{4,5},{5,4},{6,7},{7,6},{8,9},{9,8},{10,11... | collective-permute-start | bytes 638984 | tf_op jit(solution)/shard_map/ppermute | solution.py:243
  26.6 4.6 %collective-permute-start.8 = (bf16[208,512]{1,0:T(8,128)(2,1)S(1)}, bf16[208,512]{1,0:T(8,128)(2,1)S(1)}, u32[]{:S(2)}, u32[]{:S(2)}) collective-permute-start(bf16[208,512]{1,0:T(8,128)(2,1)S(1)} %shard_map.83.refs_0_), channel_id=1, source_target_pairs={{0,1},{1,0},{2,3},{3,2},{4,5},{5,4},{6,7},{7,6},{8,9},{9,8},{10,11... | collective-permute-start | bytes 638984 | tf_op jit(solution)/shard_map/ppermute | solution.py:243

commit v5 on v4

--- a/solution.py
+++ b/solution.py
@@ -12,7 +12,7 @@
 EPSILON = 1e-05
 LANES = 128
 TAIL = 16
-COST = (4, 16, 16, 32, 0, 32, 100)
+COST = (4, 16, 16, 32, 0, 0, 100)
 FIXED = 15
 BF16 = jnp.bfloat16
 F32 = jnp.float32
@@ -186,17 +186,18 @@
 
     @pl.when(place(near)[0] == 0)
     def _():
-        rows, width = out_ref.shape
+        rows, width = q_ref.shape
         q_ref[...] = queries_of(asked_ref[:rows, :], w_ref[:, width : 2 * width])
         stamp_ref[...] = down_rows(stamps_of(asked_ref))
-        add_blocks(q_ref, stamp_ref, blocks, w_ref, table_ref, None, out_ref)
-
-
-def last_kernel(near, steps, q_ref, stamp_ref, *refs):
+        out = out_ref.at[pl.ds(0, rows)]
+        add_blocks(q_ref, stamp_ref, blocks, w_ref, table_ref, None, out)
+        out_ref[rows:, :] = jnp.zeros((out_ref.shape[0] - rows, width), BF16)
+
+
+def sets_kernel(near, steps, q_ref, stamp_ref, *refs):
     count = 2 * len(steps)
     blocks = refs[:count]
-    w_ref, table_ref, acc_ref, gate_ref, gain_ref, wo_ref, tokens_ref = refs[count:-2]
-    out_ref, sum_ref = refs[-2:]
+    w_ref, table_ref, acc_ref, out_ref = refs[count:]
     level = place(near)[0]
     for i in range(len(steps) + 1):
         low = level >= steps[i - 1] if i else True
@@ -205,18 +206,17 @@
         @pl.when(jnp.logical_and(low, high))
         def _(i=i):
             if i == 0:
-                sum_ref[...] = acc_ref[...]
+                out_ref[...] = acc_ref[...]
             else:
                 seen = blocks[: 2 * i]
-                add_blocks(q_ref, stamp_ref, seen, w_ref, table_ref, acc_ref, sum_ref)
-
-    gated = layer_norm(sum_ref[...], gain_ref[...]) * gate_ref[...].astype(F32)
+                add_blocks(q_ref, stamp_ref, seen, w_ref, table_ref, acc_ref, out_ref)
+
+
+def last_kernel(sum_ref, more_ref, gate_ref, gain_ref, wo_ref, tokens_ref, out_ref):
+    attended = sum_ref[...] + more_ref[: sum_ref.shape[0], :].astype(F32)
+    gated = layer_norm(attended, gain_ref[...]) * gate_ref[...].astype(F32)
     mixed = jnp.dot(gated.astype(BF16), wo_ref[...], preferred_element_type=F32)
     out_ref[...] = (tokens_ref[...].astype(F32) + mixed).astype(BF16)
-
-
-def sum_kernel(sum_ref, more_ref, out_ref):
-    out_ref[...] = sum_ref[...] + more_ref[...].astype(F32)
 
 
 def pin_kernel(block_ref, tick_ref, out_ref):
@@ -333,7 +333,7 @@
     pass_on(1, pin(far[1], began))
     returned, tick = pl.pallas_call(
         functools.partial(return_kernel, near),
-        out_shape=(jax.ShapeDtypeStruct((rows, width), BF16), tick_shape),
+        out_shape=(jax.ShapeDtypeStruct((rows + 2 * TAIL, width), BF16), tick_shape),
         in_specs=[VMEM] * (near + 3),
         out_specs=(VMEM, VMEM),
         scratch_shapes=[pltpu.VMEM((rows, width), BF16), pltpu.VMEM((rows, LANES), I32)],
@@ -357,27 +357,25 @@
         sets[step] = [block, swap(block, 1)]
     for step in steps[:-2]:
         (total,) = attend(step, sets[step], total, weight=COST[5], tell=False)
+    blocks = [block for step in steps[-2:] for block in sets[step]]
+    args = [queries, stamp_rows, *blocks, w_proj, table, total]
     total = pl.pallas_call(
-        sum_kernel,
+        functools.partial(sets_kernel, near, steps[-2:]),
         out_shape=jax.ShapeDtypeStruct((rows, width), F32),
-        in_specs=[VMEM] * 2,
+        in_specs=[VMEM] * len(args),
         out_specs=VMEM,
-        compiler_params=pltpu.CompilerParams(vmem_limit_bytes=2 << 20),
+        compiler_params=params,
         cost_estimate=pl.CostEstimate(
             flops=COST[5] * rows * width * width, bytes_accessed=0, transcendentals=0
         ),
-    )(total, given)
-    blocks = [block for step in steps[-2:] for block in sets[step]]
-    args = [queries, stamp_rows, *blocks, w_proj, table, total, gate]
-    args += [attn_gain, w_out, tokens]
+    )(*args)
     return pl.pallas_call(
-        functools.partial(last_kernel, near, steps[-2:]),
+        last_kernel,
         out_shape=jax.ShapeDtypeStruct((rows, width), BF16),
-        in_specs=[VMEM] * len(args),
+        in_specs=[VMEM] * 6,
         out_specs=VMEM,
-        scratch_shapes=[pltpu.VMEM((rows, width), F32)],
         compiler_params=params,
-    )(*args)
+    )(total, given, gate, attn_gain, w_out, tokens)
 
 
 def solution(mesh):

time: 35.3 us -> 33.9 us (0.960)
  the two profiles are of different devices: /device:TPU:24 before, /device:TPU:0 now
where the time goes in v5:
time: 33.9 us; the launch traced here: 33.7 us
  starting transfers between devices  16.8 us (50%)
  Pallas kernels  8.02 us (24%)
  waiting for transfers between devices  7.79 us (23%)
  local copies, waits for them, and re-layouts  0.98 us (3%)
    ppermute x3, starting transfers between devices, hop(): lax.ppermute(block, 'pb', [(a * near + i, b * near + i) for a, b in pairs...  11.6 us
    ppermute x9, waiting for transfers between devices, swap(): return lax.ppermute(block, 'pb', [(i, i ^ bit) for i in range(shards)])  7.17 us
    ppermute x9, starting transfers between devices, swap(): return lax.ppermute(block, 'pb', [(i, i ^ bit) for i in range(shards)])  5.14 us
    pallas_call x1, Pallas kernels, body(): pl.pallas_call(functools.partial(return_kernel, near), out_shape=(jax.Sha...  2.63 us
    pallas_call x1, Pallas kernels, body(): pl.pallas_call(norm_kernel, out_shape=jax.ShapeDtypeStruct((rows + TAIL,...  1.88 us
    pallas_call x4, Pallas kernels, attend(): pl.pallas_call(own_kernel if total is None else functools.partial(attend_...  1.72 us
    pallas_call x1, Pallas kernels, body(): pl.pallas_call(last_kernel, out_shape=jax.ShapeDtypeStruct((rows, width),...  1.12 us
    unnamed x12, local copies, waits for them, and re-layouts  0.98 us
  transfers between devices with their start and end apart: 12, of which 5 were waited for; matrix products, arithmetic and copies ran while one was open for 0% of the time, Pallas kernels for 15%

profile of v5, /device:TPU:0, one launch (start us, length us, event | category | flops | bytes accessed | tf_op | source)
XLA Modules:
  0.0 33.7 jit_solution(16642276127508063592)
XLA Ops:
  0.0 0.0 copy-start.4
  0.0 0.0 copy-start.5
  0.0 1.9 %shard_map.73.own_ref = bf16[208,512]{1,0:T(8,128)(2,1)} custom-call(bf16[192,512]{1,0:T(8,128)(2,1)} %tokens_ref.1, s32[1,192]{1,0:T(1,128)} %bitcast.5, f32[1,512]{1,0:T(1,128)} %bitcast.4), custom_call_target="tpu_custom_call" | custom-call | tf_op jit(solution)/shard_map/pallas_call | solution.py:250
  1.9 0.0 copy-start
  1.9 0.0 copy-start.1
  1.9 0.0 copy-start.2
  1.9 0.5 %collective-permute-start = (bf16[208,512]{1,0:T(8,128)(2,1)}, bf16[208,512]{1,0:T(8,128)(2,1)S(1)}, u32[]{:S(2)}, u32[]{:S(2)}) collective-permute-start(bf16[208,512]{1,0:T(8,128)(2,1)} %shard_map.73.own_ref), channel_id=1, source_target_pairs={{0,1},{1,0},{2,3},{3,2},{4,5},{5,4},{6,7},{7,6},{8,9},{9,8},{10,11... | collective-permute-start | bytes 638984 | tf_op jit(solution)/shard_map/ppermute | solution.py:243
  2.4 2.6 %collective-permute-start.1 = (bf16[208,512]{1,0:T(8,128)(2,1)}, bf16[208,512]{1,0:T(8,128)(2,1)S(1)}, u32[]{:S(2)}, u32[]{:S(2)}) collective-permute-start(bf16[208,512]{1,0:T(8,128)(2,1)} %shard_map.73.own_ref), channel_id=1, source_target_pairs={{0,4},{1,5},{2,6},{3,7},{4,8},{5,9},{6,10},{7,11},{8,12},{9,13},{1... | collective-permute-start | bytes 638984 | tf_op jit(solution)/shard_map/ppermute | solution.py:246
  5.1 4.5 %collective-permute-start.3 = (bf16[208,512]{1,0:T(8,128)(2,1)}, bf16[208,512]{1,0:T(8,128)(2,1)S(1)}, u32[]{:S(2)}, u32[]{:S(2)}) collective-permute-start(bf16[208,512]{1,0:T(8,128)(2,1)} %shard_map.73.own_ref), channel_id=1, source_target_pairs={{0,8},{1,9},{2,10},{3,11},{4,12},{5,13},{6,14},{7,15},{16,24},{17,... | collective-permute-start | bytes 638984 | tf_op jit(solution)/shard_map/ppermute | solution.py:246
  9.6 0.0 collective-permute-done.other_ref.refs_1_
  9.6 0.0 copy-start.3
  9.6 1.0 %copy-done.3 = bf16[208,512]{1,0:T(8,128)(2,1)S(1)} copy-done((bf16[208,512]{1,0:T(8,128)(2,1)S(1)}, bf16[208,512]{1,0:T(8,128)(2,1)}, u32[]{:S(2)}) %copy-start.3) | copy-done | bytes 213016
  10.6 1.6 %collective-permute-start.6 = (bf16[208,512]{1,0:T(8,128)(2,1)S(1)}, bf16[208,512]{1,0:T(8,128)(2,1)S(1)}, u32[]{:S(2)}, u32[]{:S(2)}) collective-permute-start(bf16[208,512]{1,0:T(8,128)(2,1)S(1)} %shard_map.74.own_ref.refs_0_), channel_id=1, source_target_pairs={{0,2},{1,3},{2,0},{3,1},{4,6},{5,7},{6,4},{7,5},{8,10},{9,11},{10,... | collective-permute-start | bytes 638984 | tf_op jit(solution)/shard_map/ppermute | solution.py:243
  12.2 0.0 copy-done.4
  12.2 0.0 copy-done.5
  12.2 0.0 copy-done
  12.2 0.0 copy-done.1
  12.2 0.0 copy-done.2
  12.2 0.4 %shard_map.75 = (bf16[192,512]{1,0:T(8,128)(2,1)S(1)}, bf16[192,512]{1,0:T(8,128)(2,1)S(1)}, s32[192,128]{1,0:T(8,128)S(1)}, s32[4,128]{1,0:T(4,128)S(1)}, bf16[...) custom-call(bf16[208,512]{1,0:T(8,128)(2,1)S(1)} %shard_map.74.own_ref.refs_0_, ...), custom_call_target="tpu_custom_call" | custom-call | flops 805306368 | tf_op jit(solution)/shard_map/pallas_call | solution.py:282
  12.6 1.6 %shard_map.76 = (f32[192,512]{1,0:T(8,128)S(1)}, f32[8,128]{1,0:T(8,128)S(1)}) custom-call(bf16[192,512]{1,0:T(8,128)(2,1)S(1)} %get-tuple-element.18.q_ref, s32[192,128]{1,0:T(8,128)S(1)} %get-tuple-element.19.stamp_ref, bf16[208,512]{1,0:T(8,128)(2,1)S(1)} %shard_map.74.own_ref.refs_0_, bf16[208,512]{1,0:T(8,128)(2,1)S(1)} %collective-permute-done.other_ref.refs_1_, ...), custom_call_target="tpu_custom_call" | custom-call | flops 2214592512 | tf_op jit(solution)/shard_map/pallas_call | solution.py:309
  14.2 3.5 %collective-permute-done.6.block_ref = bf16[208,512]{1,0:T(8,128)(2,1)S(1)} collective-permute-done((bf16[208,512]{1,0:T(8,128)(2,1)S(1)}, bf16[208,512]{1,0:T(8,128)(2,1)S(1)}, u32[]{:S(2)}, u32[]{:S(2)}) %collective-permute-start.6) | collective-permute-done | bytes 213024 | tf_op jit(solution)/shard_map/ppermute | solution.py:243
  17.7 0.0 collective-permute-start.7
  17.7 0.0 collective-permute-done.1.block_ref
  17.7 0.5 %collective-permute-start.5 = (bf16[208,512]{1,0:T(8,128)(2,1)S(1)}, bf16[208,512]{1,0:T(8,128)(2,1)S(1)}, u32[]{:S(2)}, u32[]{:S(2)}) collective-permute-start(bf16[208,512]{1,0:T(8,128)(2,1)S(1)} %shard_map.77.asked_ref.refs_0_), channel_id=1, source_target_pairs={{0,1},{1,0},{2,3},{3,2},{4,5},{5,4},{6,7},{7,6},{8,9},{9,8},{10,11... | collective-permute-start | bytes 638984 | tf_op jit(solution)/shard_map/ppermute | solution.py:243
  18.2 1.5 %collective-permute-start.2 = (bf16[208,512]{1,0:T(8,128)(2,1)S(1)}, bf16[208,512]{1,0:T(8,128)(2,1)S(1)}, u32[]{:S(2)}, u32[]{:S(2)}) collective-permute-start(bf16[208,512]{1,0:T(8,128)(2,1)S(1)} %shard_map.77.asked_ref.refs_0_), channel_id=1, source_target_pairs={{0,2},{1,3},{2,0},{3,1},{4,6},{5,7},{6,4},{7,5},{8,10},{9,11},{10,... | collective-permute-start | bytes 638984 | tf_op jit(solution)/shard_map/ppermute | solution.py:243
  19.7 0.0 collective-permute-done.3.refs_0_
  19.7 0.0 collective-permute-start.4
  19.7 0.5 %collective-permute-start.9 = (bf16[208,512]{1,0:T(8,128)(2,1)S(1)}, bf16[208,512]{1,0:T(8,128)(2,1)S(1)}, u32[]{:S(2)}, u32[]{:S(2)}) collective-permute-start(bf16[208,512]{1,0:T(8,128)(2,1)S(1)} %collective-permute-done.3.refs_0_), channel_id=1, source_target_pairs={{0,2},{1,3},{2,0},{3,1},{4,6},{5,7},{6,4},{7,5},{8,10},{9,11},{10,... | collective-permute-start | bytes 638984 | tf_op jit(solution)/shard_map/ppermute | solution.py:243
  20.2 0.0 collective-permute-done.7.refs_1_.refs_3_
  20.2 2.6 %shard_map.80 = (bf16[224,512]{1,0:T(8,128)(2,1)S(1)}, f32[8,128]{1,0:T(8,128)S(1)}) custom-call(bf16[208,512]{1,0:T(8,128)(2,1)S(1)} %shard_map.77.asked_ref.refs_0_, bf16[208,512]{1,0:T(8,128)(2,1)S(1)} %shard_map.74.own_ref.refs_0_, bf16[208,512]{1,0:T(8,128)(2,1)S(1)} %collective-permute-done.other_ref.refs_1_, ...), custom_call_target="tpu_custom_call" | custom-call | flops 2214592512 | tf_op jit(solution)/shard_map/pallas_call | solution.py:334
  22.9 4.5 %collective-permute-start.11 = (bf16[224,512]{1,0:T(8,128)(2,1)S(1)}, bf16[224,512]{1,0:T(8,128)(2,1)S(1)}, u32[]{:S(2)}, u32[]{:S(2)}) collective-permute-start(bf16[224,512]{1,0:T(8,128)(2,1)S(1)} %get-tuple-element.26), channel_id=1, source_target_pairs={{0,12},{1,13},{2,14},{3,15},{16,28},{17,29},{18,30},{19,31}} | collective-permute-start | bytes 688136 | tf_op jit(solution)/shard_map/ppermute | solution.py:246
  27.4 0.0 collective-permute-done.5.refs_1_
  27.5 0.0 collective-permute-done.4.refs_1_
  27.6 2.4 %collective-permute-done.9.block_ref = bf16[208,512]{1,0:T(8,128)(2,1)S(1)} collective-permute-done((bf16[208,512]{1,0:T(8,128)(2,1)S(1)}, bf16[208,512]{1,0:T(8,128)(2,1)S(1)}, u32[]{:S(2)}, u32[]{:S(2)}) %collective-permute-start.9) | collective-permute-done | bytes 213024 | tf_op jit(solution)/shard_map/ppermute | solution.py:243
  30.0 0.0 collective-permute-start.10
  30.0 0.0 collective-permute-done.2.block_ref
  30.0 0.5 %collective-permute-start.8 = (bf16[208,512]{1,0:T(8,128)(2,1)S(1)}, bf16[208,512]{1,0:T(8,128)(2,1)S(1)}, u32[]{:S(2)}, u32[]{:S(2)}) collective-permute-start(bf16[208,512]{1,0:T(8,128)(2,1)S(1)} %shard_map.83.refs_0_), channel_id=1, source_target_pairs={{0,1},{1,0},{2,3},{3,2},{4,5},{5,4},{6,7},{7,6},{8,9},{9,8},{10,11... | collective-permute-start | bytes 638984 | tf_op jit(solution)/shard_map/ppermute | solution.py:243
  30.5 0.9 %collective-permute-done.10.refs_3_ = bf16[208,512]{1,0:T(8,128)(2,1)S(1)} collective-permute-done((bf16[208,512]{1,0:T(8,128)(2,1)S(1)}, bf16[208,512]{1,0:T(8,128)(2,1)S(1)}, u32[]{:S(2)}, u32[]{:S(2)}) %collective-permute-start.10) | collective-permute-done | bytes 213024 | tf_op jit(solution)/shard_map/ppermute | solution.py:243
  31.5 0.3 collective-permute-done.8.refs_1_
  31.8 0.2 shard_map.85.sum_ref
  32.0 0.6 %collective-permute-done.11.more_ref = bf16[224,512]{1,0:T(8,128)(2,1)S(1)} collective-permute-done((bf16[224,512]{1,0:T(8,128)(2,1)S(1)}, bf16[224,512]{1,0:T(8,128)(2,1)S(1)}, u32[]{:S(2)}, u32[]{:S(2)}) %collective-permute-start.11) | collective-permute-done | bytes 229408 | tf_op jit(solution)/shard_map/ppermute | solution.py:246
  32.6 1.1 %shard_map.86 = bf16[192,512]{1,0:T(8,128)(2,1)} custom-call(f32[192,512]{1,0:T(8,128)S(1)} %shard_map.85.sum_ref, bf16[224,512]{1,0:T(8,128)(2,1)S(1)} %collective-permute-done.11.more_ref, bf16[192,512]{1,0:T(8,128)(2,1)S(1)} %get-tuple-element.27.gate_ref, f32[1,512]{1,0:T(1,128)S(1)} %get-tuple-element.28.gain_ref, ...), custom_call_target="tpu_custom_call" | custom-call | tf_op jit(solution)/shard_map/pallas_call | solution.py:372
  (8 shorter events, 0.2 us)
Async XLA Ops:
  0.0 12.2 %copy-start.4 = (f32[8,16]{1,0:T(8,128)S(1)}, f32[8,16]{1,0:T(8,128)}, u32[]{:S(2)}) copy-start(f32[8,16]{1,0:T(8,128)} %bias_ref.1) | copy-start | bytes 1540
  0.0 12.2 %copy-start.5 = (f32[512]{0:T(512)S(1)}, f32[512]{0:T(512)}, u32[]{:S(2)}) copy-start(f32[512]{0:T(512)} %param.12) | copy-start | bytes 6148
  1.9 10.3 %copy-start = (bf16[512,2048]{1,0:T(8,128)(2,1)S(1)}, bf16[512,2048]{1,0:T(8,128)(2,1)}, u32[]{:S(2)}) copy-start(bf16[512,2048]{1,0:T(8,128)(2,1)} %refs_4_.3) | copy-start | bytes 6291460
  1.9 10.3 %copy-start.1 = (bf16[192,512]{1,0:T(8,128)(2,1)S(1)}, bf16[192,512]{1,0:T(8,128)(2,1)}, u32[]{:S(2)}) copy-start(bf16[192,512]{1,0:T(8,128)(2,1)} %tokens_ref.1) | copy-start | bytes 589828
  1.9 10.3 %copy-start.2 = (bf16[512,512]{1,0:T(8,128)(2,1)S(1)}, bf16[512,512]{1,0:T(8,128)(2,1)}, u32[]{:S(2)}) copy-start(bf16[512,512]{1,0:T(8,128)(2,1)} %wo_ref.1) | copy-start | bytes 1572868
  1.9 7.7 %collective-permute-start = (bf16[208,512]{1,0:T(8,128)(2,1)}, bf16[208,512]{1,0:T(8,128)(2,1)S(1)}, u32[]{:S(2)}, u32[]{:S(2)}) collective-permute-start(bf16[208,512]{1,0:T(8,128)(2,1)} %shard_map.73.own_ref), channel_id=1, source_target_pairs={{0,1},{1,0},{2,3},{3,2},{4,5},{5,4},{6,7},{7,6},{8,9},{9,8},{10,11... | collective-permute-start | bytes 638984 | tf_op jit(solution)/shard_map/ppermute | solution.py:243
  2.4 15.2 %collective-permute-start.1 = (bf16[208,512]{1,0:T(8,128)(2,1)}, bf16[208,512]{1,0:T(8,128)(2,1)S(1)}, u32[]{:S(2)}, u32[]{:S(2)}) collective-permute-start(bf16[208,512]{1,0:T(8,128)(2,1)} %shard_map.73.own_ref), channel_id=1, source_target_pairs={{0,4},{1,5},{2,6},{3,7},{4,8},{5,9},{6,10},{7,11},{8,12},{9,13},{1... | collective-permute-start | bytes 638984 | tf_op jit(solution)/shard_map/ppermute | solution.py:246
  5.1 14.6 %collective-permute-start.3 = (bf16[208,512]{1,0:T(8,128)(2,1)}, bf16[208,512]{1,0:T(8,128)(2,1)S(1)}, u32[]{:S(2)}, u32[]{:S(2)}) collective-permute-start(bf16[208,512]{1,0:T(8,128)(2,1)} %shard_map.73.own_ref), channel_id=1, source_target_pairs={{0,8},{1,9},{2,10},{3,11},{4,12},{5,13},{6,14},{7,15},{16,24},{17,... | collective-permute-start | bytes 638984 | tf_op jit(solution)/shard_map/ppermute | solution.py:246
  9.6 1.0 %copy-start.3 = (bf16[208,512]{1,0:T(8,128)(2,1)S(1)}, bf16[208,512]{1,0:T(8,128)(2,1)}, u32[]{:S(2)}) copy-start(bf16[208,512]{1,0:T(8,128)(2,1)} %shard_map.73.own_ref) | copy-start | bytes 638980
  10.6 7.1 %collective-permute-start.6 = (bf16[208,512]{1,0:T(8,128)(2,1)S(1)}, bf16[208,512]{1,0:T(8,128)(2,1)S(1)}, u32[]{:S(2)}, u32[]{:S(2)}) collective-permute-start(bf16[208,512]{1,0:T(8,128)(2,1)S(1)} %shard_map.74.own_ref.refs_0_), channel_id=1, source_target_pairs={{0,2},{1,3},{2,0},{3,1},{4,6},{5,7},{6,4},{7,5},{8,10},{9,11},{10,... | collective-permute-start | bytes 638984 | tf_op jit(solution)/shard_map/ppermute | solution.py:243
  17.7 2.6 %collective-permute-start.7 = (bf16[208,512]{1,0:T(8,128)(2,1)S(1)}, bf16[208,512]{1,0:T(8,128)(2,1)S(1)}, u32[]{:S(2)}, u32[]{:S(2)}) collective-permute-start(bf16[208,512]{1,0:T(8,128)(2,1)S(1)} %shard_map.78.refs_0_.refs_2_), channel_id=1, source_target_pairs={{0,1},{1,0},{2,3},{3,2},{4,5},{5,4},{6,7},{7,6},{8,9},{9,8},{10,11... | collective-permute-start | bytes 638984 | tf_op jit(solution)/shard_map/ppermute | solution.py:243
  17.7 9.7 %collective-permute-start.5 = (bf16[208,512]{1,0:T(8,128)(2,1)S(1)}, bf16[208,512]{1,0:T(8,128)(2,1)S(1)}, u32[]{:S(2)}, u32[]{:S(2)}) collective-permute-start(bf16[208,512]{1,0:T(8,128)(2,1)S(1)} %shard_map.77.asked_ref.refs_0_), channel_id=1, source_target_pairs={{0,1},{1,0},{2,3},{3,2},{4,5},{5,4},{6,7},{7,6},{8,9},{9,8},{10,11... | collective-permute-start | bytes 638984 | tf_op jit(solution)/shard_map/ppermute | solution.py:243
  18.2 11.8 %collective-permute-start.2 = (bf16[208,512]{1,0:T(8,128)(2,1)S(1)}, bf16[208,512]{1,0:T(8,128)(2,1)S(1)}, u32[]{:S(2)}, u32[]{:S(2)}) collective-permute-start(bf16[208,512]{1,0:T(8,128)(2,1)S(1)} %shard_map.77.asked_ref.refs_0_), channel_id=1, source_target_pairs={{0,2},{1,3},{2,0},{3,1},{4,6},{5,7},{6,4},{7,5},{8,10},{9,11},{10,... | collective-permute-start | bytes 638984 | tf_op jit(solution)/shard_map/ppermute | solution.py:243
  19.7 7.8 %collective-permute-start.4 = (bf16[208,512]{1,0:T(8,128)(2,1)S(1)}, bf16[208,512]{1,0:T(8,128)(2,1)S(1)}, u32[]{:S(2)}, u32[]{:S(2)}) collective-permute-start(bf16[208,512]{1,0:T(8,128)(2,1)S(1)} %collective-permute-done.3.refs_0_), channel_id=1, source_target_pairs={{0,1},{1,0},{2,3},{3,2},{4,5},{5,4},{6,7},{7,6},{8,9},{9,8},{10,11... | collective-permute-start | bytes 638984 | tf_op jit(solution)/shard_map/ppermute | solution.py:243
  19.7 10.3 %collective-permute-start.9 = (bf16[208,512]{1,0:T(8,128)(2,1)S(1)}, bf16[208,512]{1,0:T(8,128)(2,1)S(1)}, u32[]{:S(2)}, u32[]{:S(2)}) collective-permute-start(bf16[208,512]{1,0:T(8,128)(2,1)S(1)} %collective-permute-done.3.refs_0_), channel_id=1, source_target_pairs={{0,2},{1,3},{2,0},{3,1},{4,6},{5,7},{6,4},{7,5},{8,10},{9,11},{10,... | collective-permute-start | bytes 638984 | tf_op jit(solution)/shard_map/ppermute | solution.py:243
  22.9 9.7 %collective-permute-start.11 = (bf16[224,512]{1,0:T(8,128)(2,1)S(1)}, bf16[224,512]{1,0:T(8,128)(2,1)S(1)}, u32[]{:S(2)}, u32[]{:S(2)}) collective-permute-start(bf16[224,512]{1,0:T(8,128)(2,1)S(1)} %get-tuple-element.26), channel_id=1, source_target_pairs={{0,12},{1,13},{2,14},{3,15},{16,28},{17,29},{18,30},{19,31}} | collective-permute-start | bytes 688136 | tf_op jit(solution)/shard_map/ppermute | solution.py:246
  30.0 1.5 %collective-permute-start.10 = (bf16[208,512]{1,0:T(8,128)(2,1)S(1)}, bf16[208,512]{1,0:T(8,128)(2,1)S(1)}, u32[]{:S(2)}, u32[]{:S(2)}) collective-permute-start(bf16[208,512]{1,0:T(8,128)(2,1)S(1)} %shard_map.84.refs_2_), channel_id=1, source_target_pairs={{0,1},{1,0},{2,3},{3,2},{4,5},{5,4},{6,7},{7,6},{8,9},{9,8},{10,11... | collective-permute-start | bytes 638984 | tf_op jit(solution)/shard_map/ppermute | solution.py:243
  30.0 1.8 %collective-permute-start.8 = (bf16[208,512]{1,0:T(8,128)(2,1)S(1)}, bf16[208,512]{1,0:T(8,128)(2,1)S(1)}, u32[]{:S(2)}, u32[]{:S(2)}) collective-permute-start(bf16[208,512]{1,0:T(8,128)(2,1)S(1)} %shard_map.83.refs_0_), channel_id=1, source_target_pairs={{0,1},{1,0},{2,3},{3,2},{4,5},{5,4},{6,7},{7,6},{8,9},{9,8},{10,11... | collective-permute-start | bytes 638984 | tf_op jit(solution)/shard_map/ppermute | solution.py:243

commit v6 on v5

--- a/solution.py
+++ b/solution.py
@@ -346,21 +346,18 @@
     steps = sorted(far)
     for step in steps[1:]:
         pass_on(step, far[step])
-    for step in steps:
-        last = step == steps[-1]
-        extra = (tick,) if step == 1 else ()
-        total, *told = attend(step, far[step], total, *extra, weight=COST[4], tell=last)
-    (tick,) = told
     sets = {}
     for step in steps:
-        block = pin(across[step], tick)
+        extra = (tick,) if step == 1 else ()
+        total, done = attend(step, far[step], total, *extra, weight=COST[4])
+        block = pin(across[step], done)
         sets[step] = [block, swap(block, 1)]
-    for step in steps[:-2]:
+    for step in steps[:-1]:
         (total,) = attend(step, sets[step], total, weight=COST[5], tell=False)
-    blocks = [block for step in steps[-2:] for block in sets[step]]
+    blocks = sets[steps[-1]]
     args = [queries, stamp_rows, *blocks, w_proj, table, total]
     total = pl.pallas_call(
-        functools.partial(sets_kernel, near, steps[-2:]),
+        functools.partial(sets_kernel, near, steps[-1:]),
         out_shape=jax.ShapeDtypeStruct((rows, width), F32),
         in_specs=[VMEM] * len(args),
         out_specs=VMEM,

time: 33.9 us -> 33.9 us (level)
  waiting for transfers between devices: 7.79 us -> 8.33 us
  starting transfers between devices: 16.8 us -> 16.3 us
    ppermute x3, waiting for transfers between devices: 0.62 us -> 1.11 us  [hop(): lax.ppermute(block, 'pb', [(a * near + i, b * near + i) for a, b in pairs...]
    ppermute x9, starting transfers between devices: 5.14 us -> 4.71 us  [swap(): return lax.ppermute(block, 'pb', [(i, i ^ bit) for i in range(shards)])]
    pallas_call x4 -> x5, Pallas kernels: 1.72 us -> 1.76 us  [attend(): pl.pallas_call(own_kernel if total is None else functools.partial(attend_...]
  transfers between devices with their start and end apart: 12 -> 12, of which waited for: 5 -> 4; matrix products, arithmetic and copies ran while one was open for 0% -> 0% of each run, Pallas kernels for 15% -> 14%
where the time goes in v6:
time: 33.9 us; the launch traced here: 33.7 us
  starting transfers between devices  16.3 us (48%)
  waiting for transfers between devices  8.33 us (25%)
  Pallas kernels  7.88 us (23%)
  local copies, waits for them, and re-layouts  0.98 us (3%)
    ppermute x3, starting transfers between devices, hop(): lax.ppermute(block, 'pb', [(a * near + i, b * near + i) for a, b in pairs...  11.6 us
    ppermute x9, waiting for transfers between devices, swap(): return lax.ppermute(block, 'pb', [(i, i ^ bit) for i in range(shards)])  7.23 us
    ppermute x9, starting transfers between devices, swap(): return lax.ppermute(block, 'pb', [(i, i ^ bit) for i in range(shards)])  4.71 us
    pallas_call x1, Pallas kernels, body(): pl.pallas_call(functools.partial(return_kernel, near), out_shape=(jax.Sha...  2.63 us
    pallas_call x1, Pallas kernels, body(): pl.pallas_call(norm_kernel, out_shape=jax.ShapeDtypeStruct((rows + TAIL,...  1.87 us
    pallas_call x5, Pallas kernels, attend(): pl.pallas_call(own_kernel if total is None else functools.partial(attend_...  1.76 us
    pallas_call x1, Pallas kernels, body(): pl.pallas_call(last_kernel, out_shape=jax.ShapeDtypeStruct((rows, width),...  1.12 us
    ppermute x3, waiting for transfers between devices, hop(): lax.ppermute(block, 'pb', [(a * near + i, b * near + i) for a, b in pairs...  1.11 us
  transfers between devices with their start and end apart: 12, of which 4 were waited for; matrix products, arithmetic and copies ran while one was open for 0% of the time, Pallas kernels for 14%

profile of v6, /device:TPU:0, one launch (start us, length us, event | category | flops | bytes accessed | tf_op | source)
XLA Modules:
  0.0 33.7 jit_solution(1102161720265828583)
XLA Ops:
  0.0 0.0 copy-start.4
  0.0 0.0 copy-start.5
  0.0 1.9 %shard_map.73.own_ref = bf16[208,512]{1,0:T(8,128)(2,1)} custom-call(bf16[192,512]{1,0:T(8,128)(2,1)} %tokens_ref.1, s32[1,192]{1,0:T(1,128)} %bitcast.5, f32[1,512]{1,0:T(1,128)} %bitcast.4), custom_call_target="tpu_custom_call" | custom-call | tf_op jit(solution)/shard_map/pallas_call | solution.py:250
  1.9 0.0 copy-start
  1.9 0.0 copy-start.1
  1.9 0.0 copy-start.2
  1.9 0.5 %collective-permute-start = (bf16[208,512]{1,0:T(8,128)(2,1)}, bf16[208,512]{1,0:T(8,128)(2,1)S(1)}, u32[]{:S(2)}, u32[]{:S(2)}) collective-permute-start(bf16[208,512]{1,0:T(8,128)(2,1)} %shard_map.73.own_ref), channel_id=1, source_target_pairs={{0,1},{1,0},{2,3},{3,2},{4,5},{5,4},{6,7},{7,6},{8,9},{9,8},{10,11... | collective-permute-start | bytes 638984 | tf_op jit(solution)/shard_map/ppermute | solution.py:243
  2.4 2.6 %collective-permute-start.4 = (bf16[208,512]{1,0:T(8,128)(2,1)}, bf16[208,512]{1,0:T(8,128)(2,1)S(1)}, u32[]{:S(2)}, u32[]{:S(2)}) collective-permute-start(bf16[208,512]{1,0:T(8,128)(2,1)} %shard_map.73.own_ref), channel_id=1, source_target_pairs={{0,4},{1,5},{2,6},{3,7},{4,8},{5,9},{6,10},{7,11},{8,12},{9,13},{1... | collective-permute-start | bytes 638984 | tf_op jit(solution)/shard_map/ppermute | solution.py:246
  5.1 4.5 %collective-permute-start.1 = (bf16[208,512]{1,0:T(8,128)(2,1)}, bf16[208,512]{1,0:T(8,128)(2,1)S(1)}, u32[]{:S(2)}, u32[]{:S(2)}) collective-permute-start(bf16[208,512]{1,0:T(8,128)(2,1)} %shard_map.73.own_ref), channel_id=1, source_target_pairs={{0,8},{1,9},{2,10},{3,11},{4,12},{5,13},{6,14},{7,15},{16,24},{17,... | collective-permute-start | bytes 638984 | tf_op jit(solution)/shard_map/ppermute | solution.py:246
  9.6 0.0 collective-permute-done.other_ref.refs_1_
  9.6 0.0 copy-start.3
  9.6 1.0 %copy-done.3 = bf16[208,512]{1,0:T(8,128)(2,1)S(1)} copy-done((bf16[208,512]{1,0:T(8,128)(2,1)S(1)}, bf16[208,512]{1,0:T(8,128)(2,1)}, u32[]{:S(2)}) %copy-start.3) | copy-done | bytes 213016
  10.6 1.6 %collective-permute-start.6 = (bf16[208,512]{1,0:T(8,128)(2,1)S(1)}, bf16[208,512]{1,0:T(8,128)(2,1)S(1)}, u32[]{:S(2)}, u32[]{:S(2)}) collective-permute-start(bf16[208,512]{1,0:T(8,128)(2,1)S(1)} %shard_map.74.own_ref.refs_0_), channel_id=1, source_target_pairs={{0,2},{1,3},{2,0},{3,1},{4,6},{5,7},{6,4},{7,5},{8,10},{9,11},{10,... | collective-permute-start | bytes 638984 | tf_op jit(solution)/shard_map/ppermute | solution.py:243
  12.2 0.0 copy-done.4
  12.2 0.0 copy-done.5
  12.2 0.0 copy-done
  12.2 0.0 copy-done.1
  12.2 0.0 copy-done.2
  12.2 0.4 %shard_map.75 = (bf16[192,512]{1,0:T(8,128)(2,1)S(1)}, bf16[192,512]{1,0:T(8,128)(2,1)S(1)}, s32[192,128]{1,0:T(8,128)S(1)}, s32[4,128]{1,0:T(4,128)S(1)}, bf16[...) custom-call(bf16[208,512]{1,0:T(8,128)(2,1)S(1)} %shard_map.74.own_ref.refs_0_, ...), custom_call_target="tpu_custom_call" | custom-call | flops 805306368 | tf_op jit(solution)/shard_map/pallas_call | solution.py:282
  12.6 1.6 %shard_map.76 = (f32[192,512]{1,0:T(8,128)S(1)}, f32[8,128]{1,0:T(8,128)S(1)}) custom-call(bf16[192,512]{1,0:T(8,128)(2,1)S(1)} %get-tuple-element.20.q_ref, s32[192,128]{1,0:T(8,128)S(1)} %get-tuple-element.21.stamp_ref, bf16[208,512]{1,0:T(8,128)(2,1)S(1)} %shard_map.74.own_ref.refs_0_, bf16[208,512]{1,0:T(8,128)(2,1)S(1)} %collective-permute-done.other_ref.refs_1_, ...), custom_call_target="tpu_custom_call" | custom-call | flops 2214592512 | tf_op jit(solution)/shard_map/pallas_call | solution.py:309
  14.2 3.5 %collective-permute-done.6.block_ref = bf16[208,512]{1,0:T(8,128)(2,1)S(1)} collective-permute-done((bf16[208,512]{1,0:T(8,128)(2,1)S(1)}, bf16[208,512]{1,0:T(8,128)(2,1)S(1)}, u32[]{:S(2)}, u32[]{:S(2)}) %collective-permute-start.6) | collective-permute-done | bytes 213024 | tf_op jit(solution)/shard_map/ppermute | solution.py:243
  17.7 0.0 collective-permute-start.7
  17.7 0.0 collective-permute-done.4.block_ref
  17.7 0.5 %collective-permute-start.5 = (bf16[208,512]{1,0:T(8,128)(2,1)S(1)}, bf16[208,512]{1,0:T(8,128)(2,1)S(1)}, u32[]{:S(2)}, u32[]{:S(2)}) collective-permute-start(bf16[208,512]{1,0:T(8,128)(2,1)S(1)} %shard_map.77.asked_ref.refs_0_), channel_id=1, source_target_pairs={{0,1},{1,0},{2,3},{3,2},{4,5},{5,4},{6,7},{7,6},{8,9},{9,8},{10,11... | collective-permute-start | bytes 638984 | tf_op jit(solution)/shard_map/ppermute | solution.py:243
  18.2 1.5 %collective-permute-start.9 = (bf16[208,512]{1,0:T(8,128)(2,1)S(1)}, bf16[208,512]{1,0:T(8,128)(2,1)S(1)}, u32[]{:S(2)}, u32[]{:S(2)}) collective-permute-start(bf16[208,512]{1,0:T(8,128)(2,1)S(1)} %shard_map.77.asked_ref.refs_0_), channel_id=1, source_target_pairs={{0,2},{1,3},{2,0},{3,1},{4,6},{5,7},{6,4},{7,5},{8,10},{9,11},{10,... | collective-permute-start | bytes 638984 | tf_op jit(solution)/shard_map/ppermute | solution.py:243
  19.7 0.0 collective-permute-done.1.refs_0_
  19.7 0.0 collective-permute-start.3
  19.7 0.5 %collective-permute-start.2 = (bf16[208,512]{1,0:T(8,128)(2,1)S(1)}, bf16[208,512]{1,0:T(8,128)(2,1)S(1)}, u32[]{:S(2)}, u32[]{:S(2)}) collective-permute-start(bf16[208,512]{1,0:T(8,128)(2,1)S(1)} %collective-permute-done.1.refs_0_), channel_id=1, source_target_pairs={{0,2},{1,3},{2,0},{3,1},{4,6},{5,7},{6,4},{7,5},{8,10},{9,11},{10,... | collective-permute-start | bytes 638984 | tf_op jit(solution)/shard_map/ppermute | solution.py:243
  20.2 0.0 collective-permute-done.7.refs_1_.refs_3_
  20.2 2.6 %shard_map.80 = (bf16[224,512]{1,0:T(8,128)(2,1)S(1)}, f32[8,128]{1,0:T(8,128)S(1)}) custom-call(bf16[208,512]{1,0:T(8,128)(2,1)S(1)} %shard_map.77.asked_ref.refs_0_, bf16[208,512]{1,0:T(8,128)(2,1)S(1)} %shard_map.74.own_ref.refs_0_, bf16[208,512]{1,0:T(8,128)(2,1)S(1)} %collective-permute-done.other_ref.refs_1_, ...), custom_call_target="tpu_custom_call" | custom-call | flops 2214592512 | tf_op jit(solution)/shard_map/pallas_call | solution.py:334
  22.9 4.5 %collective-permute-start.11 = (bf16[224,512]{1,0:T(8,128)(2,1)S(1)}, bf16[224,512]{1,0:T(8,128)(2,1)S(1)}, u32[]{:S(2)}, u32[]{:S(2)}) collective-permute-start(bf16[224,512]{1,0:T(8,128)(2,1)S(1)} %get-tuple-element.30), channel_id=1, source_target_pairs={{0,12},{1,13},{2,14},{3,15},{16,28},{17,29},{18,30},{19,31}} | collective-permute-start | bytes 688136 | tf_op jit(solution)/shard_map/ppermute | solution.py:246
  27.4 0.0 collective-permute-done.5.refs_1_
  27.5 0.0 collective-permute-done.9.block_ref
  27.5 0.1 collective-permute-start.10
  27.6 0.0 collective-permute-done.3.refs_1_
  27.7 2.3 %collective-permute-done.2.block_ref = bf16[208,512]{1,0:T(8,128)(2,1)S(1)} collective-permute-done((bf16[208,512]{1,0:T(8,128)(2,1)S(1)}, bf16[208,512]{1,0:T(8,128)(2,1)S(1)}, u32[]{:S(2)}, u32[]{:S(2)}) %collective-permute-start.2) | collective-permute-done | bytes 213024 | tf_op jit(solution)/shard_map/ppermute | solution.py:243
  30.0 0.0 collective-permute-start.8
  30.0 0.0 collective-permute-done.10.refs_1_
  30.1 1.4 %collective-permute-done.8.refs_1_ = bf16[208,512]{1,0:T(8,128)(2,1)S(1)} collective-permute-done((bf16[208,512]{1,0:T(8,128)(2,1)S(1)}, bf16[208,512]{1,0:T(8,128)(2,1)S(1)}, u32[]{:S(2)}, u32[]{:S(2)}) %collective-permute-start.8) | collective-permute-done | bytes 213024 | tf_op jit(solution)/shard_map/ppermute | solution.py:243
  31.5 1.1 %collective-permute-done.11.more_ref = bf16[224,512]{1,0:T(8,128)(2,1)S(1)} collective-permute-done((bf16[224,512]{1,0:T(8,128)(2,1)S(1)}, bf16[224,512]{1,0:T(8,128)(2,1)S(1)}, u32[]{:S(2)}, u32[]{:S(2)}) %collective-permute-start.11) | collective-permute-done | bytes 229408 | tf_op jit(solution)/shard_map/ppermute | solution.py:246
  32.6 1.1 %shard_map.87 = bf16[192,512]{1,0:T(8,128)(2,1)} custom-call(f32[192,512]{1,0:T(8,128)S(1)} %shard_map.86.sum_ref, bf16[224,512]{1,0:T(8,128)(2,1)S(1)} %collective-permute-done.11.more_ref, bf16[192,512]{1,0:T(8,128)(2,1)S(1)} %get-tuple-element.31.gate_ref, f32[1,512]{1,0:T(1,128)S(1)} %get-tuple-element.32.gain_ref, ...), custom_call_target="tpu_custom_call" | custom-call | tf_op jit(solution)/shard_map/pallas_call | solution.py:369
  (10 shorter events, 0.2 us)
Async XLA Ops:
  0.0 12.2 %copy-start.4 = (f32[8,16]{1,0:T(8,128)S(1)}, f32[8,16]{1,0:T(8,128)}, u32[]{:S(2)}) copy-start(f32[8,16]{1,0:T(8,128)} %bias_ref.1) | copy-start | bytes 1540
  0.0 12.2 %copy-start.5 = (f32[512]{0:T(512)S(1)}, f32[512]{0:T(512)}, u32[]{:S(2)}) copy-start(f32[512]{0:T(512)} %param.12) | copy-start | bytes 6148
  1.9 10.3 %copy-start = (bf16[512,2048]{1,0:T(8,128)(2,1)S(1)}, bf16[512,2048]{1,0:T(8,128)(2,1)}, u32[]{:S(2)}) copy-start(bf16[512,2048]{1,0:T(8,128)(2,1)} %refs_2_.9) | copy-start | bytes 6291460
  1.9 10.3 %copy-start.1 = (bf16[192,512]{1,0:T(8,128)(2,1)S(1)}, bf16[192,512]{1,0:T(8,128)(2,1)}, u32[]{:S(2)}) copy-start(bf16[192,512]{1,0:T(8,128)(2,1)} %tokens_ref.1) | copy-start | bytes 589828
  1.9 10.3 %copy-start.2 = (bf16[512,512]{1,0:T(8,128)(2,1)S(1)}, bf16[512,512]{1,0:T(8,128)(2,1)}, u32[]{:S(2)}) copy-start(bf16[512,512]{1,0:T(8,128)(2,1)} %wo_ref.1) | copy-start | bytes 1572868
  1.9 7.7 %collective-permute-start = (bf16[208,512]{1,0:T(8,128)(2,1)}, bf16[208,512]{1,0:T(8,128)(2,1)S(1)}, u32[]{:S(2)}, u32[]{:S(2)}) collective-permute-start(bf16[208,512]{1,0:T(8,128)(2,1)} %shard_map.73.own_ref), channel_id=1, source_target_pairs={{0,1},{1,0},{2,3},{3,2},{4,5},{5,4},{6,7},{7,6},{8,9},{9,8},{10,11... | collective-permute-start | bytes 638984 | tf_op jit(solution)/shard_map/ppermute | solution.py:243
  2.4 15.2 %collective-permute-start.4 = (bf16[208,512]{1,0:T(8,128)(2,1)}, bf16[208,512]{1,0:T(8,128)(2,1)S(1)}, u32[]{:S(2)}, u32[]{:S(2)}) collective-permute-start(bf16[208,512]{1,0:T(8,128)(2,1)} %shard_map.73.own_ref), channel_id=1, source_target_pairs={{0,4},{1,5},{2,6},{3,7},{4,8},{5,9},{6,10},{7,11},{8,12},{9,13},{1... | collective-permute-start | bytes 638984 | tf_op jit(solution)/shard_map/ppermute | solution.py:246
  5.1 14.6 %collective-permute-start.1 = (bf16[208,512]{1,0:T(8,128)(2,1)}, bf16[208,512]{1,0:T(8,128)(2,1)S(1)}, u32[]{:S(2)}, u32[]{:S(2)}) collective-permute-start(bf16[208,512]{1,0:T(8,128)(2,1)} %shard_map.73.own_ref), channel_id=1, source_target_pairs={{0,8},{1,9},{2,10},{3,11},{4,12},{5,13},{6,14},{7,15},{16,24},{17,... | collective-permute-start | bytes 638984 | tf_op jit(solution)/shard_map/ppermute | solution.py:246
  9.6 1.0 %copy-start.3 = (bf16[208,512]{1,0:T(8,128)(2,1)S(1)}, bf16[208,512]{1,0:T(8,128)(2,1)}, u32[]{:S(2)}) copy-start(bf16[208,512]{1,0:T(8,128)(2,1)} %shard_map.73.own_ref) | copy-start | bytes 638980
  10.6 7.1 %collective-permute-start.6 = (bf16[208,512]{1,0:T(8,128)(2,1)S(1)}, bf16[208,512]{1,0:T(8,128)(2,1)S(1)}, u32[]{:S(2)}, u32[]{:S(2)}) collective-permute-start(bf16[208,512]{1,0:T(8,128)(2,1)S(1)} %shard_map.74.own_ref.refs_0_), channel_id=1, source_target_pairs={{0,2},{1,3},{2,0},{3,1},{4,6},{5,7},{6,4},{7,5},{8,10},{9,11},{10,... | collective-permute-start | bytes 638984 | tf_op jit(solution)/shard_map/ppermute | solution.py:243
  17.7 2.6 %collective-permute-start.7 = (bf16[208,512]{1,0:T(8,128)(2,1)S(1)}, bf16[208,512]{1,0:T(8,128)(2,1)S(1)}, u32[]{:S(2)}, u32[]{:S(2)}) collective-permute-start(bf16[208,512]{1,0:T(8,128)(2,1)S(1)} %shard_map.78.refs_0_.refs_2_), channel_id=1, source_target_pairs={{0,1},{1,0},{2,3},{3,2},{4,5},{5,4},{6,7},{7,6},{8,9},{9,8},{10,11... | collective-permute-start | bytes 638984 | tf_op jit(solution)/shard_map/ppermute | solution.py:243
  17.7 9.7 %collective-permute-start.5 = (bf16[208,512]{1,0:T(8,128)(2,1)S(1)}, bf16[208,512]{1,0:T(8,128)(2,1)S(1)}, u32[]{:S(2)}, u32[]{:S(2)}) collective-permute-start(bf16[208,512]{1,0:T(8,128)(2,1)S(1)} %shard_map.77.asked_ref.refs_0_), channel_id=1, source_target_pairs={{0,1},{1,0},{2,3},{3,2},{4,5},{5,4},{6,7},{7,6},{8,9},{9,8},{10,11... | collective-permute-start | bytes 638984 | tf_op jit(solution)/shard_map/ppermute | solution.py:243
  18.2 9.3 %collective-permute-start.9 = (bf16[208,512]{1,0:T(8,128)(2,1)S(1)}, bf16[208,512]{1,0:T(8,128)(2,1)S(1)}, u32[]{:S(2)}, u32[]{:S(2)}) collective-permute-start(bf16[208,512]{1,0:T(8,128)(2,1)S(1)} %shard_map.77.asked_ref.refs_0_), channel_id=1, source_target_pairs={{0,2},{1,3},{2,0},{3,1},{4,6},{5,7},{6,4},{7,5},{8,10},{9,11},{10,... | collective-permute-start | bytes 638984 | tf_op jit(solution)/shard_map/ppermute | solution.py:243
  19.7 7.9 %collective-permute-start.3 = (bf16[208,512]{1,0:T(8,128)(2,1)S(1)}, bf16[208,512]{1,0:T(8,128)(2,1)S(1)}, u32[]{:S(2)}, u32[]{:S(2)}) collective-permute-start(bf16[208,512]{1,0:T(8,128)(2,1)S(1)} %collective-permute-done.1.refs_0_), channel_id=1, source_target_pairs={{0,1},{1,0},{2,3},{3,2},{4,5},{5,4},{6,7},{7,6},{8,9},{9,8},{10,11... | collective-permute-start | bytes 638984 | tf_op jit(solution)/shard_map/ppermute | solution.py:243
  19.7 10.3 %collective-permute-start.2 = (bf16[208,512]{1,0:T(8,128)(2,1)S(1)}, bf16[208,512]{1,0:T(8,128)(2,1)S(1)}, u32[]{:S(2)}, u32[]{:S(2)}) collective-permute-start(bf16[208,512]{1,0:T(8,128)(2,1)S(1)} %collective-permute-done.1.refs_0_), channel_id=1, source_target_pairs={{0,2},{1,3},{2,0},{3,1},{4,6},{5,7},{6,4},{7,5},{8,10},{9,11},{10,... | collective-permute-start | bytes 638984 | tf_op jit(solution)/shard_map/ppermute | solution.py:243
  22.9 9.7 %collective-permute-start.11 = (bf16[224,512]{1,0:T(8,128)(2,1)S(1)}, bf16[224,512]{1,0:T(8,128)(2,1)S(1)}, u32[]{:S(2)}, u32[]{:S(2)}) collective-permute-start(bf16[224,512]{1,0:T(8,128)(2,1)S(1)} %get-tuple-element.30), channel_id=1, source_target_pairs={{0,12},{1,13},{2,14},{3,15},{16,28},{17,29},{18,30},{19,31}} | collective-permute-start | bytes 688136 | tf_op jit(solution)/shard_map/ppermute | solution.py:246
  27.5 2.5 %collective-permute-start.10 = (bf16[208,512]{1,0:T(8,128)(2,1)S(1)}, bf16[208,512]{1,0:T(8,128)(2,1)S(1)}, u32[]{:S(2)}, u32[]{:S(2)}) collective-permute-start(bf16[208,512]{1,0:T(8,128)(2,1)S(1)} %shard_map.84.refs_0_), channel_id=1, source_target_pairs={{0,1},{1,0},{2,3},{3,2},{4,5},{5,4},{6,7},{7,6},{8,9},{9,8},{10,11... | collective-permute-start | bytes 638984 | tf_op jit(solution)/shard_map/ppermute | solution.py:243
  30.0 1.5 %collective-permute-start.8 = (bf16[208,512]{1,0:T(8,128)(2,1)S(1)}, bf16[208,512]{1,0:T(8,128)(2,1)S(1)}, u32[]{:S(2)}, u32[]{:S(2)}) collective-permute-start(bf16[208,512]{1,0:T(8,128)(2,1)S(1)} %shard_map.83.refs_0_), channel_id=1, source_target_pairs={{0,1},{1,0},{2,3},{3,2},{4,5},{5,4},{6,7},{7,6},{8,9},{9,8},{10,11... | collective-permute-start | bytes 638984 | tf_op jit(solution)/shard_map/ppermute | solution.py:243
